TPU v7x, 32 devices: a whole 2x2x4 slice. The times are simulated.
32 devices in a mesh: dp: 8 (over z, x), mp: 4 (over y, core).
Axes of the slice: x: 2, y: 2, z: 4, core: 2. Of those that a mesh axis runs over, the one named last changes fastest.
Arguments:
- inputs: bfloat16 [24, 2048, 256], P('dp', 'mp'), may hold values from -6 to 6
- segments: int32 [24, 2048], P('dp', 'mp'), may hold values from 0 to 512, as said below
- w_qkv: bfloat16 [3, 256, 256], P(None, None, 'mp'), may hold values from -0.375 to 0.375
- b_qv: bfloat16 [2, 256], P(None, 'mp'), may hold values from -3 to 3
- w_out: bfloat16 [256, 256], P('mp'), may hold values from -2 to 2
- b_out: bfloat16 [256], replicated, may hold values from -3 to 3
- gain_one: float32 [256], replicated, may hold values from 0.1 to 1.9
- shift_one: float32 [256], replicated, may hold values from -2 to 2
- w_in: bfloat16 [256, 512], P(None, 'mp'), may hold values from -0.375 to 0.375
- b_in: bfloat16 [512], P('mp'), may hold values from -3 to 3
- w_back: bfloat16 [512, 256], P('mp'), may hold values from -0.375 to 0.375
- b_back: bfloat16 [256], replicated, may hold values from -3 to 3
- gain_two: float32 [256], replicated, may hold values from 0.1 to 1.9
- shift_two: float32 [256], replicated, may hold values from -2 to 2
- cotangent: bfloat16 [24, 2048, 256], P('dp', 'mp'), may hold values from -6 to 6
Outputs:
- result: bfloat16 [24, 2048, 256], P('dp', 'mp')
- grad_inputs: float32 [24, 2048, 256], P('dp', 'mp')
- grad_qkv: float32 [3, 256, 256], P(None, None, 'mp')
- grad_bias_qv: float32 [2, 256], P(None, 'mp')
- grad_w_out: float32 [256, 256], P('mp')
- grad_b_out: float32 [256], replicated
- grad_gain_one: float32 [256], replicated
- grad_shift_one: float32 [256], replicated
- grad_w_in: float32 [256, 512], P(None, 'mp')
- grad_b_in: float32 [512], P('mp')
- grad_w_back: float32 [512, 256], P('mp')
- grad_b_back: float32 [256], replicated
- grad_gain_two: float32 [256], replicated
- grad_shift_two: float32 [256], replicated
Inputs may be any that keep to these rules, and one draw needn't show every extreme that they name: `segments`: cell numbers start at 0 in every row and never fall along it; in every row one cell covers positions 256 to 1791.
All inputs are finite; a program needn't handle non-finite values.
Results may differ from a plain program's by a relative error of at most 0.017.
Values may be sent and summed in bfloat16 or wider, within the bound.
No kernel may reach another device: no remote copies, remote signals or barrier semaphores. Data moves between devices by JAX's collectives and lax.ppermute only.
A program may use at most 128 MiB of HBM per device.

v0:
```python
import functools

import jax
import jax.numpy as jnp
from jax import lax
from jax.experimental import pallas as pl
from jax.experimental.pallas import tpu as pltpu
from jax.sharding import PartitionSpec as P

HEADS = 4
EPS = 1e-06
FAR = -(2.0**99)
GELU_C = 0.7978845608028654
GELU_A = 0.044715

BF = jnp.bfloat16
F32 = jnp.float32

NN = (((1,), (0,)), ((), ()))
NT = (((1,), (1,)), ((), ()))
TN = (((0,), (0,)), ((), ()))

MB = 2**20
LIMITS = (20, 20, 12, 12)


def mm(left, right, dims):
    return lax.dot_general(left, right, dims, preferred_element_type=F32)


def call(kernel, name, args, outs, scratch=(), flops=0, limit=20):
    whole = pl.BlockSpec(memory_space=pltpu.VMEM)
    return pl.pallas_call(
        kernel,
        out_shape=[jax.ShapeDtypeStruct(shape, kind) for shape, kind in outs],
        in_specs=[whole] * len(args),
        out_specs=[whole] * len(outs),
        scratch_shapes=[pltpu.VMEM(shape, kind) for shape, kind in scratch],
        compiler_params=pltpu.CompilerParams(vmem_limit_bytes=limit * MB),
        cost_estimate=pl.CostEstimate(flops=flops // 20, bytes_accessed=0, transcendentals=0),
        name=name,
    )(*args)


def pack_kernel(rows, *refs):
    w_qkv, b_qv, w_out, w_in, b_in, w_back, segs, x = refs[:8]
    xs, two = refs[8:-1], refs[-1]
    width, model = w_qkv.shape[1:]
    units = w_in.shape[1]
    half = model // 2
    here = x.shape[1]
    for r in range(rows):
        out = xs[r]
        out[0:here, :] = x[r]
        out[here : here + 16, :] = jnp.zeros((16, model), BF)
        seg = segs[r : r + 1, :]
        at = here
        for digit in (jnp.bitwise_and(seg, 31), jnp.right_shift(seg, 5)):
            digit = digit.astype(F32).astype(BF)
            for start in range(0, here, model):
                out[at : at + 1, :] = digit[:, start : start + model]
                at += 1
    out = xs[0]
    at = here + 16
    for c in range(3):
        out[at : at + width, :] = w_qkv[c]
        at += width
    out[at : at + 16, :] = jnp.zeros((16, model), BF)
    out[at : at + 1, 0:width] = b_qv[0:1, :]
    out[at : at + 1, width : 2 * width] = b_qv[1:2, :]
    two[0:width, :] = w_out[...]
    at = width
    two[at : at + half, 0:units] = w_in[0:half, :]
    two[at : at + half, units : 2 * units] = w_in[half:, :]
    at += half
    two[at : at + units, :] = w_back[...]
    at += units
    two[at : at + 16, :] = jnp.zeros((16, model), BF)
    two[at : at + 1, 0:units] = b_in[...]


def pack(w_qkv, b_qv, w_out, w_in, b_in, w_back, segments, inputs):
    width, units, model = w_qkv.shape[2], w_in.shape[1], w_in.shape[0]
    rows, here = segments.shape
    sizes = [here + 16] * rows
    sizes[0] += 3 * width + 16
    sizes.append(width + model // 2 + units + 16)
    args = (
        w_qkv.transpose(0, 2, 1),
        b_qv,
        w_out,
        w_in,
        b_in.reshape(1, units),
        w_back,
        segments,
        inputs,
    )
    return call(
        functools.partial(pack_kernel, rows),
        "pack",
        [pltpu.with_memory_space_constraint(a, pltpu.HBM) for a in args],
        [((size, model), BF) for size in sizes],
    )


def forward_kernel(parts, here, hd, *refs):
    xs, ws = refs[:parts], refs[parts : 2 * parts]
    e_out, kv_out, qt_out, o_out, w_kv, w_q, bias, feats, qfeat = refs[2 * parts :]
    heads = parts
    length = parts * here
    at = here + 16
    for h in range(heads):
        w_q[h * hd : (h + 1) * hd, :] = ws[h][at : at + hd, :]
        w_kv[h * 2 * hd : (h + 1) * 2 * hd, :] = ws[h][at + hd : at + 3 * hd, :]
        line = ws[h][at + 3 * hd : at + 3 * hd + 1, 0 : 2 * hd].astype(F32)
        bias[h] = jnp.broadcast_to(line, (2 * hd, 2 * hd)).T
    per = here // xs[0].shape[1]
    lane = lax.broadcasted_iota(jnp.int32, (hd, here), 0).astype(F32)
    for b in range(parts):
        low = [xs[b][here + i : here + i + 1, :].astype(F32) for i in range(per)]
        high = [xs[b][here + per + i : here + per + i + 1, :].astype(F32) for i in range(per)]
        low, high = jnp.concatenate(low, axis=1), jnp.concatenate(high, axis=1)
        same = lane == jnp.where(lane < 32, low, high + 32.0)
        feats[:, b * here : (b + 1) * here] = jnp.where(same, 0.0, FAR).astype(BF)
        if b == 0:
            qfeat[...] = same.astype(F32)
    ones = value_ones(hd, length)

    def two_heads(pair, _):
        first = 2 * pair
        proj = mm(w_q[pl.ds(pl.multiple_of(first * hd, 2 * hd), 2 * hd), :], xs[0][0:here, :], NT)
        qs = []
        for i in range(2):
            qt = proj[i * hd : (i + 1) * hd] + bias[first + i, :hd, 0:1]
            qt = qt.astype(BF).astype(F32) * (hd**-0.5)
            qt_out[first + i] = qt.astype(BF)
            qs.append(jnp.concatenate([qt, qfeat[...]], axis=0).T.astype(BF))
        w = w_kv[pl.ds(pl.multiple_of(first * 2 * hd, 4 * hd), 4 * hd), :]
        for b in range(parts):
            cols = slice(b * here, (b + 1) * here)
            proj = mm(w, xs[b][0:here, :], NT)
            for i in range(2):
                at = 2 * i * hd
                kv_out[first + i, 0:hd, cols] = proj[at : at + hd].astype(BF)
                kv_out[first + i, hd:, cols] = (
                    proj[at + hd : at + 2 * hd] + bias[first + i, hd:, 0:1]
                ).astype(BF)

        def score(i):
            keys = jnp.concatenate([kv_out[first + i, 0:hd, :], feats[...]], axis=0)
            scores = mm(qs[i], keys, NN)
            return scores, jnp.max(scores, axis=-1, keepdims=True)

        later = score(0)
        for i in range(2):
            scores, top = later
            if i == 0:
                later = score(1)
            expo = jnp.exp(scores - top).astype(BF)
            e_out[first + i] = expo
            values = jnp.concatenate([kv_out[first + i, hd:, :], ones], axis=0)
            o_out[first + i] = mm(expo, values, NT)
        return 0

    lax.fori_loop(0, heads // 2, two_heads, 0)


def value_ones(hd, length):
    return (lax.broadcasted_iota(jnp.int32, (hd, length), 0) < 2).astype(F32).astype(BF)


def attend_forward(blocks, ws, heads, here):
    parts = len(blocks)
    model = blocks[0].shape[1]
    length = parts * here
    hd = model // heads
    return call(
        functools.partial(forward_kernel, parts, here, hd),
        "attend_forward",
        (*blocks, *ws),
        [
            ((heads, here, length), BF),
            ((heads, 2 * hd, length), BF),
            ((heads, hd, here), BF),
            ((heads, here, 2 * hd), F32),
        ],
        [
            ((heads * 2 * hd, model), BF),
            ((heads * hd, model), BF),
            ((heads, 2 * hd, 2 * hd), F32),
            ((hd, length), BF),
            ((hd, here), F32),
        ],
        flops=heads * 4 * here * length * 256,
        limit=LIMITS[0],
    )


def middle_kernel(parts, heads, rows, *refs):
    os, xs = refs[:rows], refs[rows : 2 * rows]
    cot_in = refs[2 * rows]
    ws = refs[2 * rows + 1 : 2 * rows + 1 + parts]
    at = 2 * rows + 1 + parts
    b_out, g_one, e_one, b_back, g_two, e_two = refs[at : at + 6]
    result_out, keep_out, send_out, dh1_out, do_out = refs[at + 6 : at + 11]
    w_out, w_pad, w_in, w_back, o_all, x_all = refs[at + 11 : at + 17]
    dw_out, dw_in, dw_back, db_in, sums = refs[at + 17 :]
    here, model = cot_in.shape[1:]
    hd = model // heads
    per = w_out.shape[0] // parts
    units = w_back.shape[0] // parts
    half_model = model // 2
    w_pad[...] = jnp.zeros(w_pad.shape, BF)
    bias = []
    for b in range(parts):
        at = 0
        w_out[b * per : (b + 1) * per, :] = ws[b][at : at + per, :]
        w_pad[b * 2 * per : b * 2 * per + per, :] = ws[b][at : at + per, :]
        at += per
        cols = slice(b * units, (b + 1) * units)
        w_in[0:half_model, cols] = ws[b][at : at + half_model, 0:units]
        w_in[half_model:, cols] = ws[b][at : at + half_model, units : 2 * units]
        at += half_model
        w_back[b * units : (b + 1) * units, :] = ws[b][at : at + units, :]
        at += units
        bias.append(ws[b][at : at + 1, 0:units].astype(F32))
    b_in = jnp.concatenate(bias, axis=1)
    lane = lax.broadcasted_iota(jnp.int32, (here, 2 * hd), 1)
    for r in range(rows):
        o_all[r] = os[r][...]
        x_all[r] = xs[r][0:here, :]
    for total in (dw_out, dw_in, dw_back, db_in, sums):
        total[...] = jnp.zeros(total.shape, F32)

    def norm(h):
        centre = h - jnp.mean(h, axis=-1, keepdims=True)
        rstd = lax.rsqrt(jnp.mean(centre * centre, axis=-1, keepdims=True) + EPS)
        return centre * rstd, rstd

    def norm_back(dy, gain, unit, rstd):
        dn = dy * gain
        mean = jnp.mean(dn, axis=-1, keepdims=True)
        along = jnp.mean(dn * unit, axis=-1, keepdims=True)
        return rstd * (dn - mean - unit * along)

    def down(v):
        return jnp.sum(v, axis=0, keepdims=True)

    def one_row(r, _):
        o_in = [o_all[r, h] for h in range(heads)]
        inv = [1.0 / o[:, hd : hd + 1] for o in o_in]
        normal = [o * i for o, i in zip(o_in, inv)]
        tiles = [
            jnp.where(lane < hd, normal[h], pltpu.roll(normal[h + 1], hd, 1))
            for h in range(0, heads, 2)
        ]
        att = jnp.concatenate(tiles, axis=1).astype(BF)
        h1 = x_all[r].astype(F32) + mm(att, w_out[...], NN) + b_out[...].astype(F32)
        n1, rstd1 = norm(h1)
        y1 = n1 * g_one[...] + e_one[...]
        y1b = y1.astype(BF)
        pre = mm(y1b, w_in[...], NN) + b_in
        square = pre * pre
        th = jnp.tanh(GELU_C * pre * (1.0 + GELU_A * square))
        half = 0.5 * (1.0 + th)
        act = (pre * half).astype(BF)
        slope = half + 0.5 * pre * (1.0 - th * th) * (GELU_C * (1.0 + 3.0 * GELU_A * square))
        h2 = y1 + mm(act, w_back[...], NN) + b_back[...].astype(F32)
        n2, rstd2 = norm(h2)
        result_out[r] = (n2 * g_two[...] + e_two[...]).astype(BF)
        cot = cot_in[r].astype(F32)
        dh2 = norm_back(cot, g_two[...], n2, rstd2)
        dz = dh2.astype(BF)
        dact = mm(dz, w_back[...], NT)
        dpre = (dact * slope).astype(BF)
        dw_back[...] += mm(act, dz, TN)
        dw_in[...] += mm(y1b, dpre, TN)
        db_in[...] += down(dpre.astype(F32))
        dy1 = mm(dpre, w_in[...], NT) + dh2
        dh1 = norm_back(dy1, g_one[...], n1, rstd1)
        dh1_out[r] = dh1
        da = dh1.astype(BF)
        dw_out[...] += mm(att, da, TN)
        dwide = mm(da, w_pad[...], NT)
        for h in range(heads):
            grad = (dwide[:, 2 * hd * h : 2 * hd * (h + 1)] * inv[h]).astype(BF)
            wide = grad.astype(F32)
            inner = jnp.sum(wide * normal[h], axis=-1, keepdims=True)
            high = inner.astype(BF).astype(F32)
            rest = inner - high
            wide = jnp.where(lane == hd, -high, jnp.where(lane == hd + 1, -rest, wide))
            do_out[r, h] = wide.astype(BF)
        rows_of = [down(dh1), down(dy1 * n1), down(dy1), down(dh2), down(cot * n2), down(cot)]
        for i, row in enumerate(rows_of):
            sums[i : i + 1, :] += row
        return 0

    lax.fori_loop(0, rows, one_row, 0)
    for b in range(parts):
        out = send_out if b % 2 else keep_out
        kind = out.dtype
        c = b // 2
        cols = slice(b * units, (b + 1) * units)
        at = 0
        out[c, at : at + per, :] = dw_out[b * per : (b + 1) * per, :].astype(kind)
        at += per
        out[c, at : at + half_model, 0:units] = dw_in[0:half_model, cols].astype(kind)
        out[c, at : at + half_model, units : 2 * units] = dw_in[half_model:, cols].astype(kind)
        at += half_model
        out[c, at : at + units, :] = dw_back[b * units : (b + 1) * units, :].astype(kind)
        at += units
        out[c, at:, :] = jnp.zeros((16, model), kind)
        out[c, at : at + 1, 0:units] = db_in[:, cols].astype(kind)
        out[c, at + 1 : at + 7, :] = sums[0:6, :].astype(kind)


def middle(os, xs, cotangent, ws, vectors, heads):
    parts = len(ws)
    rows, here, model = cotangent.shape
    hd = model // heads
    size = ws[0].shape[0]
    width = model // parts
    units = size - 16 - width - model // 2
    return call(
        functools.partial(middle_kernel, parts, heads, rows),
        "middle",
        (*os, *xs, cotangent, *ws, *vectors),
        [
            (cotangent.shape, BF),
            ((parts // 2, size, model), F32),
            ((parts // 2, size, model), BF),
            ((rows, here, model), F32),
            ((rows, heads, here, 2 * hd), BF),
        ],
        [
            ((parts * width, model), BF),
            ((2 * parts * width, model), BF),
            ((model, parts * units), BF),
            ((parts * units, model), BF),
            ((rows, heads, here, 2 * hd), F32),
            ((rows, here, model), BF),
            ((parts * width, model), F32),
            ((model, parts * units), F32),
            ((parts * units, model), F32),
            ((1, parts * units), F32),
            ((8, model), F32),
        ],
        flops=rows * 6 * here * model * (2 * model + 2 * parts * units),
        limit=LIMITS[1],
    )


def backward_kernel(row, first, each, *refs):
    e_in, kv_in, qt_in, do_in, dkv, dq, ds = refs
    hd, here = qt_in.shape[1:]
    length = kv_in.shape[2]
    chunk = here // 2
    ones = value_ones(hd, length)

    def some_heads(step, _):
        for i in range(each):
            o = step * each + i
            h = first + o
            values = jnp.concatenate([kv_in[h, hd:, :], ones], axis=0)
            for c in range(2):
                rows = slice(c * chunk, (c + 1) * chunk)
                dp = mm(do_in[row, h, rows, :], values, NN)
                ds[i, rows, :] = (dp * e_in[h, rows, :].astype(F32)).astype(BF)
            dkv[o, hd:, :] = mm(do_in[row, h], e_in[h], TN)[:hd].astype(BF)
            dkv[o, :hd, :] = mm(qt_in[h], ds[i], NN).astype(BF)
            dq[o] = (mm(kv_in[h, :hd, :], ds[i], NT) * (hd**-0.5)).astype(BF)
        return 0

    lax.fori_loop(0, dq.shape[0] // each, some_heads, 0)


def attend_backward(row, first, count, each, e, kv, qt, do):
    _, hd, here = qt.shape
    length = kv.shape[2]
    return call(
        functools.partial(backward_kernel, row, first, each),
        "attend_backward",
        (e, kv, qt, do),
        [((count, 2 * hd, length), BF), ((count, hd, here), BF)],
        [((each, here, length), BF)],
        flops=count * 6 * here * length * 256,
        limit=LIMITS[2],
    )


def inputs_kernel(parts, here, row, pieces, *refs):
    dkvs, dqs = refs[:pieces], refs[pieces : 2 * pieces]
    at = 2 * pieces
    dh1_in = refs[at]
    ws = refs[at + 1 : at + 1 + parts]
    dx_own, dx_keep, dx_send, w_kv, w_q = refs[at + 1 + parts :]
    hd = w_q.shape[0] // parts
    at = here + 16
    for b in range(parts):
        w_q[b * hd : (b + 1) * hd, :] = ws[b][at : at + hd, :]
        w_kv[b * 2 * hd : (b + 1) * 2 * hd, :] = ws[b][at + hd : at + 3 * hd, :]
    for b in range(parts):
        dx = mm(joined(dkvs, slice(b * here, (b + 1) * here)), w_kv[...], TN)
        if b == 0:
            dx_own[...] = dx + mm(joined(dqs, slice(0, here)), w_q[...], TN) + dh1_in[row]
        elif b % 2:
            dx_send[b // 2] = dx.astype(BF)
        else:
            dx_keep[b // 2 - 1] = dx


def joined(refs, cols):
    return jnp.concatenate([ref[h, :, cols] for ref in refs for h in range(ref.shape[0])], axis=0)


def input_gradients(row, dkvs, dqs, dh1, ws):
    parts = len(ws)
    here, model = dh1.shape[1:]
    return call(
        functools.partial(inputs_kernel, parts, here, row, len(dkvs)),
        "input_gradients",
        (*dkvs, *dqs, dh1, *ws),
        [
            ((here, model), F32),
            ((parts // 2 - 1, here, model), F32),
            ((parts // 2, here, model), BF),
        ],
        [((2 * model, model), BF), ((model, model), BF)],
        flops=4 * parts * here * model * model,
        limit=LIMITS[3],
    )


def weights_kernel(parts, here, first, last, many, *refs):
    dkvs, dqs = refs[:many], refs[many : 2 * many]
    at = 2 * many
    xs = refs[at : at + parts]
    at += parts
    if not first:
        grads_in = refs[at]
        at += 1
    outs = refs[at:]
    model = xs[0].shape[1]
    hd = model // parts
    dq = joined(dqs, slice(0, here))
    gkv = None
    for b in range(parts):
        term = mm(joined(dkvs, slice(b * here, (b + 1) * here)), xs[b][0:here, :], NN)
        gkv = term if gkv is None else gkv + term
    gq = mm(dq, xs[0][0:here, :], NN)
    bq = mm(jnp.ones((8, here), BF), dq, NT)[0:1]
    length = parts * here
    bkv = mm(jnp.ones((8, length), BF), joined(dkvs, slice(0, length)), NT)[0:1]
    for b in range(parts):
        pieces = [
            (slice(0, hd), slice(0, model), gq[b * hd : (b + 1) * hd]),
            (slice(hd, 3 * hd), slice(0, model), gkv[b * 2 * hd : (b + 1) * 2 * hd]),
            (slice(3 * hd, 3 * hd + 1), slice(0, hd), bq[:, b * hd : (b + 1) * hd]),
            (
                slice(3 * hd, 3 * hd + 1),
                slice(hd, 2 * hd),
                bkv[:, b * 2 * hd + hd : (b + 1) * 2 * hd],
            ),
        ]
        out, c = (outs[b % 2], b // 2) if last else (outs[0], b)
        out[c, 3 * hd :, :] = jnp.zeros((16, model), out.dtype)
        for rows, cols, value in pieces:
            if not first:
                value = value + grads_in[b, rows, cols]
            out[c, rows, cols] = value.astype(out.dtype)


def weight_gradients(dkvs, dqs, grads, blocks, here, first, last):
    parts = len(blocks)
    model = blocks[0].shape[1]
    size = 3 * (model // parts) + 16
    if last:
        outs = [((parts // 2, size, model), F32), ((parts // 2, size, model), BF)]
    else:
        outs = [((parts, size, model), F32)]
    return call(
        functools.partial(weights_kernel, parts, here, first, last, len(dkvs)),
        "weight_gradients",
        (*dkvs, *dqs, *blocks) + (() if first else (grads,)),
        outs,
        flops=4 * parts * here * model * model,
        limit=LIMITS[3],
    )


def add_kernel(rows, *refs):
    owns, nears, fars = refs[:rows], refs[rows : 2 * rows], refs[2 * rows : 3 * rows]
    out = refs[3 * rows]
    for r in range(rows):
        out[r] = owns[r][...] + nears[r][0].astype(F32) + fars[r][...].astype(F32)


def add_inputs(owns, nears, fars):
    rows = len(owns)
    (out,) = call(
        functools.partial(add_kernel, rows),
        "add_inputs",
        (*owns, *nears, *fars),
        [((rows,) + owns[0].shape, F32)],
        limit=LIMITS[3],
    )
    return out


def finish_one_kernel(a, b, qkv, bias):
    width = qkv.shape[1]
    total = a[...].astype(F32) + b[...].astype(F32)
    for c in range(3):
        qkv[c] = total[c * width : (c + 1) * width]
    line = total[3 * width : 3 * width + 1]
    bias[0:1, :] = line[:, 0:width]
    bias[1:2, :] = line[:, width : 2 * width]


def finish_two_kernel(a, b, w_out, w_in, b_in, w_back, *sums):
    width, model = w_out.shape
    units = w_back.shape[0]
    half = model // 2
    total = a[...].astype(F32) + b[...].astype(F32)
    w_out[...] = total[:width]
    at = width
    w_in[0:half, :] = total[at : at + half, 0:units]
    w_in[half:, :] = total[at : at + half, units : 2 * units]
    at += half
    w_back[...] = total[at : at + units]
    at += units
    b_in[...] = total[at : at + 1, 0:units]
    for i, out in enumerate(sums):
        out[...] = total[at + 1 + i : at + 2 + i]


def swap(value, axis, size, bit):
    return lax.ppermute(value, axis, [(i, i ^ bit) for i in range(size)])


def after(value, *others):
    return lax.optimization_barrier((value, *others))[0]


def layer(mesh_sizes, *args):
    (inputs, segments, w_qkv, b_qv, w_out, b_out, gain_one, shift_one) = args[:8]
    (w_in, b_in, w_back, b_back, gain_two, shift_two, cotangent) = args[8:]
    dp, mp = mesh_sizes
    rows, here, model = inputs.shape
    heads = HEADS
    width = w_qkv.shape[2]
    units = w_in.shape[1]

    def near(value):
        return swap(value, "mp", mp, 1)

    def far(value):
        return swap(value, "mp", mp, 2)

    *packs, two = pack(w_qkv, b_qv, w_out, w_in, b_in, w_back, segments, inputs)
    vectors = [
        v.reshape(1, model) for v in (b_out, gain_one, shift_one, b_back, gain_two, shift_two)
    ]
    fars = [far(packs[0])]
    nears = [near(after(packs[0], *vectors))]
    for r in range(1, rows):
        fars.append(far(after(packs[r], nears[r - 1])))
        nears.append(near(packs[r]))
    two_far = far(after(two, nears[-1]))
    two_near = near(two)
    boths = [near(fars[0])]
    saved, boths_of = [], []
    for r in range(rows):
        blocks = [packs[r], nears[r], fars[r], boths[r]]
        boths_of.append(blocks)
        out = attend_forward(blocks, boths_of[0], heads, here)
        saved.append(out)
        if r + 1 < rows:
            boths.append(near(after(fars[r + 1], out[2])))
    two_both = near(after(two_far, saved[max(rows - 2, 0)][2]))
    result, keep_two, send_two, dh1s, dos = middle(
        [s[3] for s in saved],
        packs,
        cotangent,
        [two, two_near, two_far, two_both],
        vectors,
        heads,
    )

    def chain(keep, send):
        got = near(send)
        mine = keep[0] + got[0].astype(F32)
        other = (keep[1] + got[1].astype(F32)).astype(BF)
        yield other
        value = mine + far(other).astype(F32)
        bit = 1
        while bit < dp:
            sent = value.astype(BF)
            yield sent
            got = swap(sent, "dp", dp, bit)
            value = sent.astype(F32) + got.astype(F32)
            bit *= 2
        yield (sent, got)

    steps = chain(keep_two, send_two)
    total_two = None
    ready = []
    grads = None
    owns, near_got, far_got = [], [], []
    pending = None

    def advance():
        nonlocal total_two, pending
        step = next(steps, None)
        if isinstance(step, tuple):
            total_two = step
        elif step is not None:
            ready.append(step)
        if pending is not None:
            other = (pending[0] + pending[1].astype(F32)).astype(BF)
            far_got.append(far(other))
            ready.append(other)
            pending = None

    for r in range(rows):
        dkvs, dqs = [], []
        last = r == rows - 1
        splits = [(0, heads, 2)] if r != 1 else [(0, heads // 2, 1), (heads // 2, heads // 2, 1)]
        for first, count, each in splits:
            e, kv, qt, _ = saved[r]
            if ready:
                e = after(e, *ready)
                ready.clear()
            dkv, dq = attend_backward(r, first, count, each, e, kv, qt, dos)
            dkvs.append(dkv)
            dqs.append(dq)
            advance()
        grads = weight_gradients(dkvs, dqs, grads, boths_of[r], here, r == 0, last)
        if last:
            tail = chain(*grads)
            other = next(tail)
            dkvs = [after(d, grads[1]) for d in dkvs]
        else:
            grads = grads[0]
        own, keep, send = input_gradients(r, dkvs, dqs, dh1s, boths_of[0])
        got = near(after(send, other) if last else send)
        owns.append(own)
        near_got.append(got)
        pending = (keep[0], got[1])
    sent = next(tail)
    final = after((pending[0] + pending[1].astype(F32)).astype(BF), sent)
    far_got.append(far(final))
    for step in steps:
        total_two = step
    for step in tail:
        total_one = step
    grad_inputs = add_inputs(owns, near_got, far_got)
    grad_out, grad_in, grad_b_in, grad_back, *sums = call(
        finish_two_kernel,
        "finish_two",
        total_two,
        [
            ((width, model), F32),
            ((model, units), F32),
            ((1, units), F32),
            ((units, model), F32),
        ]
        + [((1, model), F32)] * 6,
    )
    grad_qkv, grad_bias = call(
        finish_one_kernel,
        "finish_one",
        total_one,
        [((3, width, model), F32), ((2, width), F32)],
    )
    sums = [s.reshape(model) for s in sums]
    return (
        result,
        grad_inputs,
        grad_qkv.transpose(0, 2, 1),
        grad_bias,
        grad_out,
        sums[0],
        sums[1],
        sums[2],
        grad_in,
        grad_b_in.reshape(units),
        grad_back,
        sums[3],
        sums[4],
        sums[5],
    )


def solution(mesh):
    in_specs = (
        P("dp", "mp", None),
        P("dp", "mp"),
        P(None, None, "mp"),
        P(None, "mp"),
        P("mp", None),
        P(),
        P(),
        P(),
        P(None, "mp"),
        P("mp"),
        P("mp", None),
        P(),
        P(),
        P(),
        P("dp", "mp", None),
    )
    out_specs = (
        P("dp", "mp", None),
        P("dp", "mp", None),
        P(None, None, "mp"),
        P(None, "mp"),
        P("mp", None),
        P(),
        P(),
        P(),
        P(None, "mp"),
        P("mp"),
        P("mp", None),
        P(),
        P(),
        P(),
    )
    sizes = (mesh.shape["dp"], mesh.shape["mp"])
    return jax.shard_map(
        functools.partial(layer, sizes),
        mesh=mesh,
        in_specs=in_specs,
        out_specs=out_specs,
        check_vma=False,
    )
```

profile of v0, /device:TPU:0, one launch (start us, length us, event | category | flops | bytes accessed | tf_op | source)
XLA Modules:
  0.0 115.2 jit_solution(3162646098090387769)
XLA Ops:
  0.6 1.5 %pack.1 = (bf16[736,256]{1,0:T(8,128)(2,1)S(1)}, bf16[528,256]{1,0:T(8,128)(2,1)S(1)}, bf16[528,256]{1,0:T(8,128)(2,1)S(1)}, bf16[336,256]{1,0:T(8,128)(2,1)S(1)}) custom-call(bf16[3,64,256]{2,1,0:T(8,128)(2,1)} %bitcast.36, bf16[2,64]{1,0:T(2,128)(2,1)} %refs_1_.1, bf16[64,256]{1,0:T(8,128)(2,1)} %refs_2_.1, bf16[256,128]{1,0:T(8,128)(2,1)} %refs_3_.1, ...), custom_call_target="tpu_custom_call" | custom-call | tf_op jit(solution)/shard_map/pack/pallas_call | solution.py:33
  2.1 3.0 %collective-permute-start.1 = (bf16[736,256]{1,0:T(8,128)(2,1)S(1)}, bf16[736,256]{1,0:T(8,128)(2,1)S(1)}, u32[]{:S(2)}, u32[]{:S(2)}) collective-permute-start(bf16[736,256]{1,0:T(8,128)(2,1)S(1)} %get-tuple-element.80.refs_0_.refs_4_.refs_3_.refs_5_.refs_2_), channel_id=1, source_target_pairs={{0,2},{1,3},{2,0},{3,1},{4,6},{5,7},{6,4},{7,5},{8,10},{9,11},{10,... | collective-permute-start | bytes 1130504 | tf_op jit(solution)/shard_map/ppermute | solution.py:538
  6.4 7.4 %collective-permute-done.1.refs_2_.refs_6_.refs_5_.refs_7_.refs_4_ = bf16[736,256]{1,0:T(8,128)(2,1)S(1)} collective-permute-done((bf16[736,256]{1,0:T(8,128)(2,1)S(1)}, bf16[736,256]{1,0:T(8,128)(2,1)S(1)}, u32[]{:S(2)}, u32[]{:S(2)}) %collective-permute-start.1) | collective-permute-done | bytes 376864 | tf_op jit(solution)/shard_map/ppermute | solution.py:538
  13.9 1.7 %collective-permute-start.4 = (bf16[528,256]{1,0:T(8,128)(2,1)S(1)}, bf16[528,256]{1,0:T(8,128)(2,1)S(1)}, u32[]{:S(2)}, u32[]{:S(2)}) collective-permute-start(bf16[528,256]{1,0:T(8,128)(2,1)S(1)} %get-tuple-element.83.refs_0_.refs_4_), channel_id=1, source_target_pairs={{0,2},{1,3},{2,0},{3,1},{4,6},{5,7},{6,4},{7,5},{8,10},{9,11},{10,... | collective-permute-start | bytes 811016 | tf_op jit(solution)/shard_map/ppermute | solution.py:538
  16.1 6.0 %attend_forward.3 = (bf16[4,512,2048]{2,1,0:T(8,128)(2,1)S(1)}, bf16[4,128,2048]{2,1,0:T(8,128)(2,1)S(1)}, bf16[4,64,512]{2,1,0:T(8,128)(2,1)S(1)}, f32[4,512,128]{2,1,0:T(8,128)S(1)}) custom-call(bf16[736,256]{1,0:T(8,128)(2,1)S(1)} %get-tuple-element.80.refs_0_.refs_4_.refs_3_.refs_5_.refs_2_, ...), custom_call_target="tpu_custom_call" | custom-call | flops 214748368 | tf_op jit(solution)/shard_map/attend_forward/pallas_call | solution.py:33
  22.8 1.7 %collective-permute-start.7 = (bf16[528,256]{1,0:T(8,128)(2,1)S(1)}, bf16[528,256]{1,0:T(8,128)(2,1)S(1)}, u32[]{:S(2)}, u32[]{:S(2)}) collective-permute-start(bf16[528,256]{1,0:T(8,128)(2,1)S(1)} %get-tuple-element.88.refs_0_.refs_5_.refs_2_), channel_id=1, source_target_pairs={{0,2},{1,3},{2,0},{3,1},{4,6},{5,7},{6,4},{7,5},{8,10},{9,11},{10,... | collective-permute-start | bytes 811016 | tf_op jit(solution)/shard_map/ppermute | solution.py:538
  24.9 6.0 %attend_forward.4 = (bf16[4,512,2048]{2,1,0:T(8,128)(2,1)S(1)}, bf16[4,128,2048]{2,1,0:T(8,128)(2,1)S(1)}, bf16[4,64,512]{2,1,0:T(8,128)(2,1)S(1)}, f32[4,512,128]{2,1,0:T(8,128)S(1)}) custom-call(bf16[528,256]{1,0:T(8,128)(2,1)S(1)} %get-tuple-element.83.refs_0_.refs_4_, bf16[528,256]{1,0:T(8,128)(2,1)S(1)} %collective-permute-done.3.refs_1_.refs_5_, ...), custom_call_target="tpu_custom_call" | custom-call | flops 214748368 | tf_op jit(solution)/shard_map/attend_forward/pallas_call | solution.py:33
  32.6 2.8 %collective-permute-done.10.refs_9_ = bf16[336,256]{1,0:T(8,128)(2,1)S(1)} collective-permute-done((bf16[336,256]{1,0:T(8,128)(2,1)S(1)}, bf16[336,256]{1,0:T(8,128)(2,1)S(1)}, u32[]{:S(2)}, u32[]{:S(2)}) %collective-permute-start.10) | collective-permute-done | bytes 172064 | tf_op jit(solution)/shard_map/ppermute | solution.py:538
  35.4 6.0 %attend_forward.5 = (bf16[4,512,2048]{2,1,0:T(8,128)(2,1)S(1)}, bf16[4,128,2048]{2,1,0:T(8,128)(2,1)S(1)}, bf16[4,64,512]{2,1,0:T(8,128)(2,1)S(1)}, f32[4,512,128]{2,1,0:T(8,128)S(1)}) custom-call(bf16[528,256]{1,0:T(8,128)(2,1)S(1)} %get-tuple-element.88.refs_0_.refs_5_.refs_2_, bf16[528,256]{1,0:T(8,128)(2,1)S(1)} %collective-permute-done.6.refs_1_.refs_3_, ...), custom_call_target="tpu_custom_call" | custom-call | flops 214748368 | tf_op jit(solution)/shard_map/attend_forward/pallas_call | solution.py:33
  41.5 9.7 %middle.1 = (bf16[3,512,256]{2,1,0:T(8,128)(2,1)}, f32[2,336,256]{2,1,0:T(8,128)S(1)}, bf16[2,336,256]{2,1,0:T(8,128)(2,1)S(1)}, f32[3,512,256]{2,1,0:T(8,128)S(1)}, bf16[3,4,512,128]{3,2,1,0:T(8,128)(2,1)S(1)}) custom-call(f32[4,512,128]{2,1,0:T(8,128)S(1)} %get-tuple-element.81.refs_0_, f32[4,512,128]{2,1,0:T(8,128)S(1)} %get-tuple-element.86.refs_1_, ...), custom_call_target="tpu_custom_call" | custom-call | flops 181193936 | tf_op jit(solution)/shard_map/middle/pallas_call | solution.py:33
  51.7 7.4 %attend_backward.4 = (bf16[4,128,2048]{2,1,0:T(8,128)(2,1)S(1)}, bf16[4,64,512]{2,1,0:T(8,128)(2,1)S(1)}) custom-call(bf16[4,512,2048]{2,1,0:T(8,128)(2,1)S(1)} %get-tuple-element.96.refs_0_, bf16[4,128,2048]{2,1,0:T(8,128)(2,1)S(1)} %get-tuple-element.97.refs_1_, bf16[4,64,512]{2,1,0:T(8,128)(2,1)S(1)} %get-tuple-element.84.refs_2_, ...), custom_call_target="tpu_custom_call" | custom-call | flops 322122560 | tf_op jit(solution)/shard_map/attend_backward/pallas_call | solution.py:33
  60.1 1.8 %collective-permute-start.13 = (bf16[336,256]{1,0:T(8,128)(2,1)S(1)}, bf16[336,256]{1,0:T(8,128)(2,1)S(1)}, u32[]{:S(2)}, u32[]{:S(2)}) collective-permute-start(bf16[336,256]{1,0:T(8,128)(2,1)S(1)} %fusion.5), channel_id=1, source_target_pairs={{0,2},{1,3},{2,0},{3,1},{4,6},{5,7},{6,4},{7,5},{8,10},{9,11},{10,... | collective-permute-start | bytes 516104 | tf_op jit(solution)/shard_map/ppermute | solution.py:538
  63.3 3.9 %attend_backward.5 = (bf16[2,128,2048]{2,1,0:T(8,128)(2,1)S(1)}, bf16[2,64,512]{2,1,0:T(8,128)(2,1)S(1)}) custom-call(bf16[4,512,2048]{2,1,0:T(8,128)(2,1)S(1)} %get-tuple-element.111.refs_0_, bf16[4,128,2048]{2,1,0:T(8,128)(2,1)S(1)} %get-tuple-element.107.refs_1_, bf16[4,64,512]{2,1,0:T(8,128)(2,1)S(1)} %get-tuple-element.89.refs_2_, ...), custom_call_target="tpu_custom_call" | custom-call | flops 161061280 | tf_op jit(solution)/shard_map/attend_backward/pallas_call | solution.py:33
  67.2 1.6 %collective-permute-start.15 = (bf16[336,256]{1,0:T(8,128)(2,1)S(1)}, bf16[336,256]{1,0:T(8,128)(2,1)S(1)}, u32[]{:S(2)}, u32[]{:S(2)}) collective-permute-start(bf16[336,256]{1,0:T(8,128)(2,1)S(1)} %fusion), channel_id=1, source_target_pairs={{0,4},{4,0},{8,12},{12,8},{16,20},{20,16},{24,28},{28,24},{1,5},{5... | collective-permute-start | bytes 516104 | tf_op jit(solution)/shard_map/ppermute | solution.py:538
  68.9 3.8 %attend_backward.6 = (bf16[2,128,2048]{2,1,0:T(8,128)(2,1)S(1)}, bf16[2,64,512]{2,1,0:T(8,128)(2,1)S(1)}) custom-call(bf16[4,512,2048]{2,1,0:T(8,128)(2,1)S(1)} %get-tuple-element.111.refs_0_, bf16[4,128,2048]{2,1,0:T(8,128)(2,1)S(1)} %get-tuple-element.107.refs_1_, bf16[4,64,512]{2,1,0:T(8,128)(2,1)S(1)} %get-tuple-element.89.refs_2_, ...), custom_call_target="tpu_custom_call" | custom-call | flops 161061280 | tf_op jit(solution)/shard_map/attend_backward/pallas_call | solution.py:33
  74.1 7.6 %attend_backward.7 = (bf16[4,128,2048]{2,1,0:T(8,128)(2,1)S(1)}, bf16[4,64,512]{2,1,0:T(8,128)(2,1)S(1)}) custom-call(bf16[4,512,2048]{2,1,0:T(8,128)(2,1)S(1)} %get-tuple-element.117.refs_0_, bf16[4,128,2048]{2,1,0:T(8,128)(2,1)S(1)} %get-tuple-element.118.refs_1_, bf16[4,64,512]{2,1,0:T(8,128)(2,1)S(1)} %get-tuple-element.119.refs_2_, ...), custom_call_target="tpu_custom_call" | custom-call | flops 322122560 | tf_op jit(solution)/shard_map/attend_backward/pallas_call | solution.py:33
  83.1 1.6 %collective-permute-start.19 = (bf16[512,256]{1,0:T(8,128)(2,1)S(1)}, bf16[512,256]{1,0:T(8,128)(2,1)S(1)}, u32[]{:S(2)}, u32[]{:S(2)}) collective-permute-start(bf16[512,256]{1,0:T(8,128)(2,1)S(1)} %fusion.1), channel_id=1, source_target_pairs={{0,2},{1,3},{2,0},{3,1},{4,6},{5,7},{6,4},{7,5},{8,10},{9,11},{10,... | collective-permute-start | bytes 786440 | tf_op jit(solution)/shard_map/ppermute | solution.py:538
  85.8 1.6 %collective-permute-start.26 = (bf16[336,256]{1,0:T(8,128)(2,1)S(1)}, bf16[336,256]{1,0:T(8,128)(2,1)S(1)}, u32[]{:S(2)}, u32[]{:S(2)}) collective-permute-start(bf16[336,256]{1,0:T(8,128)(2,1)S(1)} %add_convert_fusion.4), channel_id=1, source_target_pairs={{0,8},{4,12},{8,0},{12,4},{16,24},{20,28},{24,16},{28,20},{1,9},{5... | collective-permute-start | bytes 516104 | tf_op jit(solution)/shard_map/ppermute | solution.py:538
  88.8 3.6 %collective-permute-done.26 = bf16[336,256]{1,0:T(8,128)(2,1)S(1)} collective-permute-done((bf16[336,256]{1,0:T(8,128)(2,1)S(1)}, bf16[336,256]{1,0:T(8,128)(2,1)S(1)}, u32[]{:S(2)}, u32[]{:S(2)}) %collective-permute-start.26) | collective-permute-done | bytes 172064 | tf_op jit(solution)/shard_map/ppermute | solution.py:538
  92.4 2.6 %collective-permute-start.27 = (bf16[336,256]{1,0:T(8,128)(2,1)S(1)}, bf16[336,256]{1,0:T(8,128)(2,1)S(1)}, u32[]{:S(2)}, u32[]{:S(2)}) collective-permute-start(bf16[336,256]{1,0:T(8,128)(2,1)S(1)} %add_convert_fusion.3.a), channel_id=1, source_target_pairs={{0,16},{4,20},{8,24},{12,28},{16,0},{20,4},{24,8},{28,12},{1,17},{... | collective-permute-start | bytes 516104 | tf_op jit(solution)/shard_map/ppermute | solution.py:538
  97.1 3.5 %collective-permute-done.23 = bf16[208,256]{1,0:T(8,128)(2,1)S(1)} collective-permute-done((bf16[208,256]{1,0:T(8,128)(2,1)S(1)}, bf16[208,256]{1,0:T(8,128)(2,1)S(1)}, u32[]{:S(2)}, u32[]{:S(2)}) %collective-permute-start.23) | collective-permute-done | bytes 106528 | tf_op jit(solution)/shard_map/ppermute | solution.py:538
  100.6 1.6 %collective-permute-start.24 = (bf16[208,256]{1,0:T(8,128)(2,1)S(1)}, bf16[208,256]{1,0:T(8,128)(2,1)S(1)}, u32[]{:S(2)}, u32[]{:S(2)}) collective-permute-start(bf16[208,256]{1,0:T(8,128)(2,1)S(1)} %add_convert_fusion.7), channel_id=1, source_target_pairs={{0,8},{4,12},{8,0},{12,4},{16,24},{20,28},{24,16},{28,20},{1,9},{5... | collective-permute-start | bytes 319496 | tf_op jit(solution)/shard_map/ppermute | solution.py:538
  102.9 2.5 %collective-permute-done.24 = bf16[208,256]{1,0:T(8,128)(2,1)S(1)} collective-permute-done((bf16[208,256]{1,0:T(8,128)(2,1)S(1)}, bf16[208,256]{1,0:T(8,128)(2,1)S(1)}, u32[]{:S(2)}, u32[]{:S(2)}) %collective-permute-start.24) | collective-permute-done | bytes 106528 | tf_op jit(solution)/shard_map/ppermute | solution.py:538
  107.6 5.5 %collective-permute-done.25.b = bf16[208,256]{1,0:T(8,128)(2,1)S(1)} collective-permute-done((bf16[208,256]{1,0:T(8,128)(2,1)S(1)}, bf16[208,256]{1,0:T(8,128)(2,1)S(1)}, u32[]{:S(2)}, u32[]{:S(2)}) %collective-permute-start.25) | collective-permute-done | bytes 106528 | tf_op jit(solution)/shard_map/ppermute | solution.py:538
  (73 shorter events, 19.9 us)
Async XLA Ops:
  2.1 11.8 %collective-permute-start.1 = (bf16[736,256]{1,0:T(8,128)(2,1)S(1)}, bf16[736,256]{1,0:T(8,128)(2,1)S(1)}, u32[]{:S(2)}, u32[]{:S(2)}) collective-permute-start(bf16[736,256]{1,0:T(8,128)(2,1)S(1)} %get-tuple-element.80.refs_0_.refs_4_.refs_3_.refs_5_.refs_2_), channel_id=1, source_target_pairs={{0,2},{1,3},{2,0},{3,1},{4,6},{5,7},{6,4},{7,5},{8,10},{9,11},{10,... | collective-permute-start | bytes 1130504 | tf_op jit(solution)/shard_map/ppermute | solution.py:538
  6.4 7.5 %collective-permute-start = (bf16[736,256]{1,0:T(8,128)(2,1)S(1)}, bf16[736,256]{1,0:T(8,128)(2,1)S(1)}, u32[]{:S(2)}, u32[]{:S(2)}) collective-permute-start(bf16[736,256]{1,0:T(8,128)(2,1)S(1)} %get-tuple-element.80.refs_0_.refs_4_.refs_3_.refs_5_.refs_2_), channel_id=1, source_target_pairs={{0,1},{1,0},{2,3},{3,2},{4,5},{5,4},{6,7},{7,6},{8,9},{9,8},{10,11... | collective-permute-start | bytes 1130504 | tf_op jit(solution)/shard_map/ppermute | solution.py:538
  13.9 8.9 %collective-permute-start.4 = (bf16[528,256]{1,0:T(8,128)(2,1)S(1)}, bf16[528,256]{1,0:T(8,128)(2,1)S(1)}, u32[]{:S(2)}, u32[]{:S(2)}) collective-permute-start(bf16[528,256]{1,0:T(8,128)(2,1)S(1)} %get-tuple-element.83.refs_0_.refs_4_), channel_id=1, source_target_pairs={{0,2},{1,3},{2,0},{3,1},{4,6},{5,7},{6,4},{7,5},{8,10},{9,11},{10,... | collective-permute-start | bytes 811016 | tf_op jit(solution)/shard_map/ppermute | solution.py:538
  15.6 7.2 %collective-permute-start.3 = (bf16[528,256]{1,0:T(8,128)(2,1)S(1)}, bf16[528,256]{1,0:T(8,128)(2,1)S(1)}, u32[]{:S(2)}, u32[]{:S(2)}) collective-permute-start(bf16[528,256]{1,0:T(8,128)(2,1)S(1)} %get-tuple-element.83.refs_0_.refs_4_), channel_id=1, source_target_pairs={{0,1},{1,0},{2,3},{3,2},{4,5},{5,4},{6,7},{7,6},{8,9},{9,8},{10,11... | collective-permute-start | bytes 811016 | tf_op jit(solution)/shard_map/ppermute | solution.py:538
  15.8 8.7 %collective-permute-start.6 = (bf16[528,256]{1,0:T(8,128)(2,1)S(1)}, bf16[528,256]{1,0:T(8,128)(2,1)S(1)}, u32[]{:S(2)}, u32[]{:S(2)}) collective-permute-start(bf16[528,256]{1,0:T(8,128)(2,1)S(1)} %get-tuple-element.88.refs_0_.refs_5_.refs_2_), channel_id=1, source_target_pairs={{0,1},{1,0},{2,3},{3,2},{4,5},{5,4},{6,7},{7,6},{8,9},{9,8},{10,11... | collective-permute-start | bytes 811016 | tf_op jit(solution)/shard_map/ppermute | solution.py:538
  22.8 9.3 %collective-permute-start.7 = (bf16[528,256]{1,0:T(8,128)(2,1)S(1)}, bf16[528,256]{1,0:T(8,128)(2,1)S(1)}, u32[]{:S(2)}, u32[]{:S(2)}) collective-permute-start(bf16[528,256]{1,0:T(8,128)(2,1)S(1)} %get-tuple-element.88.refs_0_.refs_5_.refs_2_), channel_id=1, source_target_pairs={{0,2},{1,3},{2,0},{3,1},{4,6},{5,7},{6,4},{7,5},{8,10},{9,11},{10,... | collective-permute-start | bytes 811016 | tf_op jit(solution)/shard_map/ppermute | solution.py:538
  24.6 10.8 %collective-permute-start.10 = (bf16[336,256]{1,0:T(8,128)(2,1)S(1)}, bf16[336,256]{1,0:T(8,128)(2,1)S(1)}, u32[]{:S(2)}, u32[]{:S(2)}) collective-permute-start(bf16[336,256]{1,0:T(8,128)(2,1)S(1)} %get-tuple-element.93.refs_7_), channel_id=1, source_target_pairs={{0,2},{1,3},{2,0},{3,1},{4,6},{5,7},{6,4},{7,5},{8,10},{9,11},{10,... | collective-permute-start | bytes 516104 | tf_op jit(solution)/shard_map/ppermute | solution.py:538
  32.1 9.3 %collective-permute-start.9 = (bf16[336,256]{1,0:T(8,128)(2,1)S(1)}, bf16[336,256]{1,0:T(8,128)(2,1)S(1)}, u32[]{:S(2)}, u32[]{:S(2)}) collective-permute-start(bf16[336,256]{1,0:T(8,128)(2,1)S(1)} %get-tuple-element.93.refs_7_), channel_id=1, source_target_pairs={{0,1},{1,0},{2,3},{3,2},{4,5},{5,4},{6,7},{7,6},{8,9},{9,8},{10,11... | collective-permute-start | bytes 516104 | tf_op jit(solution)/shard_map/ppermute | solution.py:538
  35.4 6.1 %collective-permute-start.11 = (bf16[336,256]{1,0:T(8,128)(2,1)S(1)}, bf16[336,256]{1,0:T(8,128)(2,1)S(1)}, u32[]{:S(2)}, u32[]{:S(2)}) collective-permute-start(bf16[336,256]{1,0:T(8,128)(2,1)S(1)} %collective-permute-done.10.refs_9_), channel_id=1, source_target_pairs={{0,1},{1,0},{2,3},{3,2},{4,5},{5,4},{6,7},{7,6},{8,9},{9,8},{10,11... | collective-permute-start | bytes 516104 | tf_op jit(solution)/shard_map/ppermute | solution.py:538
  51.1 8.9 %collective-permute-start.12 = (bf16[2,336,256]{2,1,0:T(8,128)(2,1)S(1)}, bf16[2,336,256]{2,1,0:T(8,128)(2,1)S(1)}, u32[]{:S(2)}, u32[]{:S(2)}) collective-permute-start(bf16[2,336,256]{2,1,0:T(8,128)(2,1)S(1)} %get-tuple-element.105), channel_id=1, source_target_pairs={{0,1},{1,0},{2,3},{3,2},{4,5},{5,4},{6,7},{7,6},{8,9},{9,8},{10,11... | collective-permute-start | bytes 1032200 | tf_op jit(solution)/shard_map/ppermute | solution.py:538
  60.0 8.8 %collective-permute-start.14 = (bf16[2,512,256]{2,1,0:T(8,128)(2,1)S(1)}, bf16[2,512,256]{2,1,0:T(8,128)(2,1)S(1)}, u32[]{:S(2)}, u32[]{:S(2)}) collective-permute-start(bf16[2,512,256]{2,1,0:T(8,128)(2,1)S(1)} %get-tuple-element.110), channel_id=1, source_target_pairs={{0,1},{1,0},{2,3},{3,2},{4,5},{5,4},{6,7},{7,6},{8,9},{9,8},{10,11... | collective-permute-start | bytes 1572872 | tf_op jit(solution)/shard_map/ppermute | solution.py:538
  60.1 7.1 %collective-permute-start.13 = (bf16[336,256]{1,0:T(8,128)(2,1)S(1)}, bf16[336,256]{1,0:T(8,128)(2,1)S(1)}, u32[]{:S(2)}, u32[]{:S(2)}) collective-permute-start(bf16[336,256]{1,0:T(8,128)(2,1)S(1)} %fusion.5), channel_id=1, source_target_pairs={{0,2},{1,3},{2,0},{3,1},{4,6},{5,7},{6,4},{7,5},{8,10},{9,11},{10,... | collective-permute-start | bytes 516104 | tf_op jit(solution)/shard_map/ppermute | solution.py:538
  67.2 6.8 %collective-permute-start.15 = (bf16[336,256]{1,0:T(8,128)(2,1)S(1)}, bf16[336,256]{1,0:T(8,128)(2,1)S(1)}, u32[]{:S(2)}, u32[]{:S(2)}) collective-permute-start(bf16[336,256]{1,0:T(8,128)(2,1)S(1)} %fusion), channel_id=1, source_target_pairs={{0,4},{4,0},{8,12},{12,8},{16,20},{20,16},{24,28},{28,24},{1,5},{5... | collective-permute-start | bytes 516104 | tf_op jit(solution)/shard_map/ppermute | solution.py:538
  83.1 5.1 %collective-permute-start.17 = (bf16[2,208,256]{2,1,0:T(8,128)(2,1)S(1)}, bf16[2,208,256]{2,1,0:T(8,128)(2,1)S(1)}, u32[]{:S(2)}, u32[]{:S(2)}) collective-permute-start(bf16[2,208,256]{2,1,0:T(8,128)(2,1)S(1)} %get-tuple-element.122), channel_id=1, source_target_pairs={{0,1},{1,0},{2,3},{3,2},{4,5},{5,4},{6,7},{7,6},{8,9},{9,8},{10,11... | collective-permute-start | bytes 638984 | tf_op jit(solution)/shard_map/ppermute | solution.py:538
  83.1 30.7 %collective-permute-start.19 = (bf16[512,256]{1,0:T(8,128)(2,1)S(1)}, bf16[512,256]{1,0:T(8,128)(2,1)S(1)}, u32[]{:S(2)}, u32[]{:S(2)}) collective-permute-start(bf16[512,256]{1,0:T(8,128)(2,1)S(1)} %fusion.1), channel_id=1, source_target_pairs={{0,2},{1,3},{2,0},{3,1},{4,6},{5,7},{6,4},{7,5},{8,10},{9,11},{10,... | collective-permute-start | bytes 786440 | tf_op jit(solution)/shard_map/ppermute | solution.py:538
  85.5 10.4 %collective-permute-start.16 = (bf16[2,512,256]{2,1,0:T(8,128)(2,1)S(1)}, bf16[2,512,256]{2,1,0:T(8,128)(2,1)S(1)}, u32[]{:S(2)}, u32[]{:S(2)}) collective-permute-start(bf16[2,512,256]{2,1,0:T(8,128)(2,1)S(1)} %get-tuple-element.125), channel_id=1, source_target_pairs={{0,1},{1,0},{2,3},{3,2},{4,5},{5,4},{6,7},{7,6},{8,9},{9,8},{10,11... | collective-permute-start | bytes 1572872 | tf_op jit(solution)/shard_map/ppermute | solution.py:538
  85.8 6.6 %collective-permute-start.26 = (bf16[336,256]{1,0:T(8,128)(2,1)S(1)}, bf16[336,256]{1,0:T(8,128)(2,1)S(1)}, u32[]{:S(2)}, u32[]{:S(2)}) collective-permute-start(bf16[336,256]{1,0:T(8,128)(2,1)S(1)} %add_convert_fusion.4), channel_id=1, source_target_pairs={{0,8},{4,12},{8,0},{12,4},{16,24},{20,28},{24,16},{28,20},{1,9},{5... | collective-permute-start | bytes 516104 | tf_op jit(solution)/shard_map/ppermute | solution.py:538
  88.2 6.8 %collective-permute-start.21 = (bf16[208,256]{1,0:T(8,128)(2,1)S(1)}, bf16[208,256]{1,0:T(8,128)(2,1)S(1)}, u32[]{:S(2)}, u32[]{:S(2)}) collective-permute-start(bf16[208,256]{1,0:T(8,128)(2,1)S(1)} %fusion.6), channel_id=1, source_target_pairs={{0,2},{1,3},{2,0},{3,1},{4,6},{5,7},{6,4},{7,5},{8,10},{9,11},{10,... | collective-permute-start | bytes 319496 | tf_op jit(solution)/shard_map/ppermute | solution.py:538
  92.4 14.4 %collective-permute-start.27 = (bf16[336,256]{1,0:T(8,128)(2,1)S(1)}, bf16[336,256]{1,0:T(8,128)(2,1)S(1)}, u32[]{:S(2)}, u32[]{:S(2)}) collective-permute-start(bf16[336,256]{1,0:T(8,128)(2,1)S(1)} %add_convert_fusion.3.a), channel_id=1, source_target_pairs={{0,16},{4,20},{8,24},{12,28},{16,0},{20,4},{24,8},{28,12},{1,17},{... | collective-permute-start | bytes 516104 | tf_op jit(solution)/shard_map/ppermute | solution.py:538
  95.1 7.2 %collective-permute-start.18 = (bf16[2,512,256]{2,1,0:T(8,128)(2,1)S(1)}, bf16[2,512,256]{2,1,0:T(8,128)(2,1)S(1)}, u32[]{:S(2)}, u32[]{:S(2)}) collective-permute-start(bf16[2,512,256]{2,1,0:T(8,128)(2,1)S(1)} %get-tuple-element.128), channel_id=1, source_target_pairs={{0,1},{1,0},{2,3},{3,2},{4,5},{5,4},{6,7},{7,6},{8,9},{9,8},{10,11... | collective-permute-start | bytes 1572872 | tf_op jit(solution)/shard_map/ppermute | solution.py:538
  95.1 5.4 %collective-permute-start.23 = (bf16[208,256]{1,0:T(8,128)(2,1)S(1)}, bf16[208,256]{1,0:T(8,128)(2,1)S(1)}, u32[]{:S(2)}, u32[]{:S(2)}) collective-permute-start(bf16[208,256]{1,0:T(8,128)(2,1)S(1)} %fusion.4), channel_id=1, source_target_pairs={{0,4},{4,0},{8,12},{12,8},{16,20},{20,16},{24,28},{28,24},{1,5},{5... | collective-permute-start | bytes 319496 | tf_op jit(solution)/shard_map/ppermute | solution.py:538
  96.0 17.8 %collective-permute-start.20 = (bf16[512,256]{1,0:T(8,128)(2,1)S(1)}, bf16[512,256]{1,0:T(8,128)(2,1)S(1)}, u32[]{:S(2)}, u32[]{:S(2)}) collective-permute-start(bf16[512,256]{1,0:T(8,128)(2,1)S(1)} %fusion.2), channel_id=1, source_target_pairs={{0,2},{1,3},{2,0},{3,1},{4,6},{5,7},{6,4},{7,5},{8,10},{9,11},{10,... | collective-permute-start | bytes 786440 | tf_op jit(solution)/shard_map/ppermute | solution.py:538
  102.3 11.5 %collective-permute-start.22 = (bf16[512,256]{1,0:T(8,128)(2,1)S(1)}, bf16[512,256]{1,0:T(8,128)(2,1)S(1)}, u32[]{:S(2)}, u32[]{:S(2)}) collective-permute-start(bf16[512,256]{1,0:T(8,128)(2,1)S(1)} %fusion.3), channel_id=1, source_target_pairs={{0,2},{1,3},{2,0},{3,1},{4,6},{5,7},{6,4},{7,5},{8,10},{9,11},{10,... | collective-permute-start | bytes 786440 | tf_op jit(solution)/shard_map/ppermute | solution.py:538
  105.4 7.7 %collective-permute-start.25 = (bf16[208,256]{1,0:T(8,128)(2,1)S(1)}, bf16[208,256]{1,0:T(8,128)(2,1)S(1)}, u32[]{:S(2)}, u32[]{:S(2)}) collective-permute-start(bf16[208,256]{1,0:T(8,128)(2,1)S(1)} %add_convert_fusion.6.a), channel_id=1, source_target_pairs={{0,16},{4,20},{8,24},{12,28},{16,0},{20,4},{24,8},{28,12},{1,17},{... | collective-permute-start | bytes 319496 | tf_op jit(solution)/shard_map/ppermute | solution.py:538
  (9 other events, 97.0 us)
where the time goes:
time: 115 us
  Pallas kernels  61.3 us (53%)
  waiting for transfers between devices  27.1 us (24%)
  starting transfers between devices  24.1 us (21%)
  local copies, waits for them, and re-layouts  1.34 us (1%)
    pallas_call x18, Pallas kernels, call(): pl.pallas_call(kernel, out_shape=[jax.ShapeDtypeStruct(shape, kind) for s...  61.3 us
    ppermute x28, waiting for transfers between devices, swap(): return lax.ppermute(value, axis, [(i, i ^ bit) for i in range(size)])  27.1 us
    ppermute x28, starting transfers between devices, swap(): return lax.ppermute(value, axis, [(i, i ^ bit) for i in range(size)])  24.1 us
  transfers between devices with their start and end apart: 28, of which 8 were waited for; matrix products, arithmetic and copies ran while one was open for 2% of the time, Pallas kernels for 35%

commit v1 on v0

v1 whole, which is shorter than its diff:
```python
import functools

import jax
import jax.numpy as jnp
from jax import lax
from jax.experimental import pallas as pl
from jax.experimental.pallas import tpu as pltpu
from jax.sharding import PartitionSpec as P

HEADS = 4
EPS = 1e-06
FAR = -(2.0**99)
GELU_C = 0.7978845608028654
GELU_A = 0.044715
LOG2_E = 1.4426950408889634
LN_2 = 0.6931471805599453

BF = jnp.bfloat16
F32 = jnp.float32

NN = (((1,), (0,)), ((), ()))
NT = (((1,), (1,)), ((), ()))
TN = (((0,), (0,)), ((), ()))

MB = 2**20
LIMITS = (10, 16, 8, 8)


def mm(left, right, dims):
    return lax.dot_general(left, right, dims, preferred_element_type=F32)


def call(kernel, name, args, outs, scratch=(), flops=0, limit=20):
    whole = pl.BlockSpec(memory_space=pltpu.VMEM)
    return pl.pallas_call(
        kernel,
        out_shape=[jax.ShapeDtypeStruct(shape, kind) for shape, kind in outs],
        in_specs=[whole] * len(args),
        out_specs=[whole] * len(outs),
        scratch_shapes=[pltpu.VMEM(shape, kind) for shape, kind in scratch],
        compiler_params=pltpu.CompilerParams(vmem_limit_bytes=limit * MB),
        cost_estimate=pl.CostEstimate(flops=flops // 20, bytes_accessed=0, transcendentals=0),
        name=name,
    )(*args)


def pack_kernel(rows, *refs):
    w_qkv, b_qv, w_out, b_out, w_in, b_in, w_back, b_back, segs, x, first = refs[:11]
    later, two, biases = refs[11:-2], refs[-2], refs[-1]
    biases[...] = jnp.zeros(biases.shape, F32)
    biases[0:1, :] = b_out[...].astype(F32).reshape(1, -1)
    biases[1:2, :] = b_back[...].astype(F32).reshape(1, -1)
    width, model = w_qkv.shape[1:]
    units = w_in.shape[1]
    half = model // 2
    here = x.shape[1]
    for r in range(rows):
        out = later[0] if r else first
        at = (r - 1) * (here + 16) if r else 0
        out[at : at + here, :] = x[r]
        at += here
        out[at : at + 16, :] = jnp.zeros((16, model), BF)
        seg = segs[r : r + 1, :]
        for digit in (jnp.bitwise_and(seg, 31), jnp.right_shift(seg, 5)):
            digit = digit.astype(F32).astype(BF)
            for start in range(0, here, model):
                out[at : at + 1, :] = digit[:, start : start + model]
                at += 1
    at = here + 16
    for c in range(3):
        first[at : at + width, :] = w_qkv[c]
        at += width
    first[at : at + 16, :] = jnp.zeros((16, model), BF)
    first[at : at + 1, 0:width] = b_qv[0:1, :]
    first[at : at + 1, width : 2 * width] = b_qv[1:2, :]
    two[0:width, :] = w_out[...]
    at = width
    two[at : at + half, 0:units] = w_in[0:half, :]
    two[at : at + half, units : 2 * units] = w_in[half:, :]
    at += half
    two[at : at + units, :] = w_back[...]
    at += units
    two[at : at + 16, :] = jnp.zeros((16, model), BF)
    two[at : at + 1, 0:units] = b_in[...]


def pack(w_qkv, b_qv, w_out, b_out, w_in, b_in, w_back, b_back, segments, inputs):
    width, units, model = w_qkv.shape[2], w_in.shape[1], w_in.shape[0]
    rows, here = segments.shape
    sizes = [here + 16 + 3 * width + 16]
    if rows > 1:
        sizes.append((rows - 1) * (here + 16))
    sizes.append(width + model // 2 + units + 16)
    args = (
        w_qkv.transpose(0, 2, 1),
        b_qv,
        w_out,
        b_out,
        w_in,
        b_in.reshape(1, units),
        w_back,
        b_back,
        segments,
        inputs,
    )
    return call(
        functools.partial(pack_kernel, rows),
        "pack",
        [pltpu.with_memory_space_constraint(a, pltpu.HBM) for a in args],
        [((size, model), BF) for size in sizes] + [((8, model), F32)],
    )


def load_weights(ws, here, hd, w_q, w_kv, bias):
    at = here + 16
    for i, w in enumerate(ws):
        w_q[i * hd : (i + 1) * hd, :] = w[at : at + hd, :]
        w_kv[i * 2 * hd : (i + 1) * 2 * hd, :] = w[at + hd : at + 3 * hd, :]
        line = w[at + 3 * hd : at + 3 * hd + 1, 0 : 2 * hd].astype(F32)
        bias[i] = jnp.broadcast_to(line, (2 * hd, 2 * hd)).T


def same_cell(x, at, here, hd):
    per = here // x.shape[1]
    low = [x[at + i : at + i + 1, :].astype(F32) for i in range(per)]
    high = [x[at + per + i : at + per + i + 1, :].astype(F32) for i in range(per)]
    low, high = jnp.concatenate(low, axis=1), jnp.concatenate(high, axis=1)
    lane = lax.broadcasted_iota(jnp.int32, (hd, here), 0).astype(F32)
    return lane == jnp.where(lane < 32, low, high + 32.0)


def value_ones(hd, length, count):
    return (lax.broadcasted_iota(jnp.int32, (hd, length), 0) < count).astype(F32).astype(BF)


def attend(queries, kvs, feats, before, put):
    hd = kvs[0].shape[0] // 2
    length = kvs[0].shape[1]
    ones = value_ones(hd, length, hd)

    def score(i):
        scores = mm(queries[i], jnp.concatenate([kvs[i][:hd], feats], axis=0), NN)
        top = jnp.max(scores, axis=-1, keepdims=True)
        top = jnp.broadcast_to(top, (scores.shape[0], 2 * hd))
        if before is None:
            return scores, top, None
        steps = jnp.maximum(jnp.ceil((top - before[i]) * LOG2_E), 0.0)
        return scores, before[i] + steps * LN_2, jnp.exp2(-steps)

    later = score(0)
    for i in range(len(queries)):
        scores, top, weight = later
        if i + 1 < len(queries):
            later = score(i + 1)
        wide = jnp.concatenate([top] * (length // (2 * hd)), axis=1)
        expo = jnp.exp(scores - wide).astype(BF)
        out = mm(expo, jnp.concatenate([kvs[i][hd:], ones], axis=0), NT)
        put(i, expo, out, top, weight)


def project(x, w, bias, put):
    hd = bias.shape[1] // 2
    proj = mm(w, x, NT)
    for i in range(w.shape[0] // (2 * hd)):
        at = 2 * i * hd
        keys = proj[at : at + hd].astype(BF)
        values = (proj[at + hd : at + 2 * hd] + bias[i, hd:, 0:1]).astype(BF)
        put(i, keys, values)


def local_kernel(rows, here, hd, *refs):
    count = 2 if rows > 1 else 1
    mine, nears = refs[:count], refs[count : 2 * count]
    ws = refs[2 * count : 2 * count + 2]
    e_out, kv_out, qt_out, qa_out, o_out, top_out = refs[2 * count + 2 : 2 * count + 8]
    w_q, w_kv, bias, feats = refs[2 * count + 8 :]
    load_weights(ws, here, hd, w_q, w_kv, bias)
    for r in range(rows):
        at = (r - 1) * (here + 16) if r else 0
        pair = (mine[min(r, 1)], nears[min(r, 1)])
        for b, x in enumerate(pair):
            same = same_cell(x, at + here, here, hd)
            feats[r, :, b * here : (b + 1) * here] = jnp.where(same, 0.0, FAR).astype(BF)
            if b == 0:
                first = same.astype(F32)

        def put(i, keys, values, r=r):
            kv_out[r, i, :hd, :] = keys
            kv_out[r, i, hd:, :] = values

        block = jnp.concatenate([x[at : at + here, :] for x in pair], axis=0)
        project(block, w_kv[...], bias, put)
        proj = mm(w_q[...], pair[0][at : at + here, :], NT)
        for i in range(2):
            qt = proj[i * hd : (i + 1) * hd] + bias[i, :hd, 0:1]
            qt = qt.astype(BF).astype(F32) * (hd**-0.5)
            qt_out[r, i] = qt.astype(BF)
            qa_out[r, i] = jnp.concatenate([qt, first], axis=0).T.astype(BF)

    def one_row(r, _):
        def put(i, expo, out, top, _):
            e_out[r, i] = expo
            o_out[r, i] = out
            top_out[r, i] = top

        queries, kvs = [qa_out[r, i] for i in range(2)], [kv_out[r, i] for i in range(2)]
        attend(queries, kvs, feats[r], None, put)
        return 0

    lax.fori_loop(0, rows, one_row, 0)


def attend_local(mine, nears, ws, rows, here, hd):
    model = mine[0].shape[1]
    return call(
        functools.partial(local_kernel, rows, here, hd),
        "attend_local",
        (*mine, *nears, *ws),
        [
            ((rows, 2, here, 2 * here), BF),
            ((rows, 2, 2 * hd, 2 * here), BF),
            ((rows, 2, hd, here), BF),
            ((rows, 2, here, 2 * hd), BF),
            ((rows, 2, here, 2 * hd), F32),
            ((rows, 2, here, 2 * hd), F32),
        ],
        [
            ((2 * hd, model), BF),
            ((4 * hd, model), BF),
            ((2, 2 * hd, 2 * hd), F32),
            ((rows, hd, 2 * here), BF),
        ],
        flops=1,
        limit=LIMITS[0],
    )


def remote_kernel(rows, here, hd, *refs):
    qs, os, tops, xs, ws = refs[:2], refs[2:4], refs[4:6], refs[6:8], refs[8:12]
    e_out, kv_out, o_out, weight_out, w_q, w_kv, bias, feats = refs[12:]
    heads = len(ws)
    load_weights(ws, here, hd, w_q, w_kv, bias)
    for n, row in enumerate(rows):
        at = (row - 1) * (here + 16) if row else 0
        for b, x in enumerate(xs):
            same = same_cell(x, at + here, here, hd)
            feats[n, :, b * here : (b + 1) * here] = jnp.where(same, 0.0, FAR).astype(BF)

        def put(i, keys, values, n=n):
            kv_out[n, i, :hd, :] = keys
            kv_out[n, i, hd:, :] = values

        block = jnp.concatenate([x[at : at + here, :] for x in xs], axis=0)
        project(block, w_kv[...], bias, put)

    def one_row(n, _):
        r = rows[0] + n

        def put(h, expo, out, _, weight):
            e_out[n, h] = expo
            o_out[n, h] = out + os[h // 2][r, h % 2] * weight
            weight_out[n, h] = weight.astype(BF)

        queries = [qs[h // 2][r, h % 2] for h in range(heads)]
        before = [tops[h // 2][r, h % 2] for h in range(heads)]
        attend(queries, [kv_out[n, h] for h in range(heads)], feats[n], before, put)
        return 0

    lax.fori_loop(0, len(rows), one_row, 0)


def attend_remote(rows, queries, outs, tops, xs, ws, here, hd):
    model = xs[0].shape[1]
    heads = len(ws)
    count = len(rows)
    return call(
        functools.partial(remote_kernel, rows, here, hd),
        "attend_remote",
        (*queries, *outs, *tops, *xs, *ws),
        [
            ((count, heads, here, 2 * here), BF),
            ((count, heads, 2 * hd, 2 * here), BF),
            ((count, heads, here, 2 * hd), F32),
            ((count, heads, here, 2 * hd), BF),
        ],
        [
            ((heads * hd, model), BF),
            ((heads * 2 * hd, model), BF),
            ((heads, 2 * hd, 2 * hd), F32),
            ((count, hd, 2 * here), BF),
        ],
        flops=1,
        limit=LIMITS[0],
    )


def middle_kernel(parts, heads, rows, *refs):
    groups = min(rows, 2)
    os, xs = refs[:groups], refs[groups : 2 * groups]
    at = 2 * groups
    cot_in = refs[at]
    ws = refs[at + 1 : at + 1 + parts]
    at += 1 + parts
    g_one, e_one, g_two, e_two, biases = refs[at : at + 5]
    result_out, keep_out, send_out, dh1_out, do_out = refs[at + 5 : at + 10]
    w_out, w_pad, w_in, w_back, o_all, x_all = refs[at + 10 : at + 16]
    dw_out, dw_in, dw_back, db_in, sums = refs[at + 16 :]
    w_pad[...] = jnp.zeros(w_pad.shape, BF)
    here, model = cot_in.shape[1:]
    hd = model // heads
    per = w_out.shape[0] // parts
    units = w_back.shape[0] // parts
    half_model = model // 2
    bias = []
    for b in range(parts):
        at = 0
        w_out[b * per : (b + 1) * per, :] = ws[b][at : at + per, :]
        w_pad[b * 2 * per : b * 2 * per + per, :] = ws[b][at : at + per, :]
        at += per
        cols = slice(b * units, (b + 1) * units)
        w_in[0:half_model, cols] = ws[b][at : at + half_model, 0:units]
        w_in[half_model:, cols] = ws[b][at : at + half_model, units : 2 * units]
        at += half_model
        w_back[b * units : (b + 1) * units, :] = ws[b][at : at + units, :]
        at += units
        bias.append(ws[b][at : at + 1, 0:units].astype(F32))
    b_in = jnp.concatenate(bias, axis=1)
    lane = lax.broadcasted_iota(jnp.int32, (here, 2 * hd), 1)
    for r in range(rows):
        o_all[r] = os[min(r, 1)][max(r - 1, 0)]
        at = (r - 1) * (here + 16) if r else 0
        x_all[r] = xs[min(r, 1)][at : at + here, :]
    for total in (dw_out, dw_in, dw_back, db_in, sums):
        total[...] = jnp.zeros(total.shape, F32)

    def norm(h):
        centre = h - jnp.mean(h, axis=-1, keepdims=True)
        rstd = lax.rsqrt(jnp.mean(centre * centre, axis=-1, keepdims=True) + EPS)
        return centre * rstd, rstd

    def norm_back(dy, gain, unit, rstd):
        dn = dy * gain
        mean = jnp.mean(dn, axis=-1, keepdims=True)
        along = jnp.mean(dn * unit, axis=-1, keepdims=True)
        return rstd * (dn - mean - unit * along)

    def down(v):
        return jnp.sum(v, axis=0, keepdims=True)

    def one_row(r, _):
        o_in = [o_all[r, h] for h in range(heads)]
        inv = [1.0 / o[:, hd : hd + 1] for o in o_in]
        normal = [o * i for o, i in zip(o_in, inv)]
        tiles = [
            jnp.where(lane < hd, normal[h], pltpu.roll(normal[h + 1], hd, 1))
            for h in range(0, heads, 2)
        ]
        att = jnp.concatenate(tiles, axis=1).astype(BF)
        h1 = x_all[r].astype(F32) + mm(att, w_out[...], NN) + biases[0:1, :]
        n1, rstd1 = norm(h1)
        y1 = n1 * g_one[...] + e_one[...]
        y1b = y1.astype(BF)
        pre = mm(y1b, w_in[...], NN) + b_in
        square = pre * pre
        th = jnp.tanh(GELU_C * pre * (1.0 + GELU_A * square))
        half = 0.5 * (1.0 + th)
        act = (pre * half).astype(BF)
        slope = half + 0.5 * pre * (1.0 - th * th) * (GELU_C * (1.0 + 3.0 * GELU_A * square))
        h2 = y1 + mm(act, w_back[...], NN) + biases[1:2, :]
        n2, rstd2 = norm(h2)
        result_out[r] = (n2 * g_two[...] + e_two[...]).astype(BF)
        cot = cot_in[r].astype(F32)
        dh2 = norm_back(cot, g_two[...], n2, rstd2)
        dz = dh2.astype(BF)
        dact = mm(dz, w_back[...], NT)
        dpre = (dact * slope).astype(BF)
        dw_back[...] += mm(act, dz, TN)
        dw_in[...] += mm(y1b, dpre, TN)
        db_in[...] += down(dpre.astype(F32))
        dy1 = mm(dpre, w_in[...], NT) + dh2
        dh1 = norm_back(dy1, g_one[...], n1, rstd1)
        dh1_out[r] = dh1
        da = dh1.astype(BF)
        dw_out[...] += mm(att, da, TN)
        dwide = mm(da, w_pad[...], NT)
        for h in range(heads):
            grad = (dwide[:, 2 * hd * h : 2 * hd * (h + 1)] * inv[h]).astype(BF)
            wide = grad.astype(F32)
            inner = jnp.sum(wide * normal[h], axis=-1, keepdims=True)
            high = inner.astype(BF).astype(F32)
            rest = inner - high
            wide = jnp.where(lane == hd, -high, jnp.where(lane == hd + 1, -rest, wide))
            do_out[r, h] = wide.astype(BF)
        rows_of = [down(dh1), down(dy1 * n1), down(dy1), down(dh2), down(cot * n2), down(cot)]
        for i, row in enumerate(rows_of):
            sums[i : i + 1, :] += row
        return 0

    lax.fori_loop(0, rows, one_row, 0)
    for b in range(parts):
        out = send_out if b % 2 else keep_out
        kind = out.dtype
        c = b // 2
        cols = slice(b * units, (b + 1) * units)
        at = 0
        out[c, at : at + per, :] = dw_out[b * per : (b + 1) * per, :].astype(kind)
        at += per
        out[c, at : at + half_model, 0:units] = dw_in[0:half_model, cols].astype(kind)
        out[c, at : at + half_model, units : 2 * units] = dw_in[half_model:, cols].astype(kind)
        at += half_model
        out[c, at : at + units, :] = dw_back[b * units : (b + 1) * units, :].astype(kind)
        at += units
        out[c, at:, :] = jnp.zeros((16, model), kind)
        out[c, at : at + 1, 0:units] = db_in[:, cols].astype(kind)
        out[c, at + 1 : at + 7, :] = sums[0:6, :].astype(kind)


def middle(os, xs, cotangent, ws, vectors, heads):
    parts = len(ws)
    rows, here, model = cotangent.shape
    hd = model // heads
    width = model // parts
    size = ws[0].shape[0]
    units = size - 16 - width - model // 2
    return call(
        functools.partial(middle_kernel, parts, heads, rows),
        "middle",
        (*os, *xs, cotangent, *ws, *vectors),
        [
            (cotangent.shape, BF),
            ((parts // 2, size, model), F32),
            ((parts // 2, size, model), BF),
            ((rows, here, model), F32),
            ((rows, heads, here, 2 * hd), BF),
        ],
        [
            ((parts * width, model), BF),
            ((2 * parts * width, model), BF),
            ((model, parts * units), BF),
            ((parts * units, model), BF),
            ((rows, heads, here, 2 * hd), F32),
            ((rows, here, model), BF),
            ((parts * width, model), F32),
            ((model, parts * units), F32),
            ((parts * units, model), F32),
            ((1, parts * units), F32),
            ((8, model), F32),
        ],
        flops=rows * 6 * here * model * (2 * model + 2 * parts * units),
        limit=LIMITS[1],
    )


def heads_step(row, n, pair, ref):
    el_in, kvl_in, qt_in = ref["el", pair], ref["kvl", pair], ref["qt", pair]
    er_in, kvr_in, do_in, weight_in = ref["er"], ref["kvr"], ref["do"], ref["weight"]
    dkv, dq, ds = ref["dkv", pair], ref["dq", pair], ref["ds"]
    hd = qt_in.shape[2]
    half = kvl_in.shape[3]
    ones = value_ones(hd, half, 2)

    def one_head(i, _):
        h = 2 * pair + i
        kvs = (kvl_in[row, i], kvr_in[n, h])
        es, do = (el_in[row, i], er_in[n, h]), do_in[row, h]
        dos = (do * weight_in[n, h], do)
        for side in range(2):
            cols = slice(side * half, (side + 1) * half)
            values = jnp.concatenate([kvs[side][hd:], ones], axis=0)
            dp = mm(dos[side], values, NN)
            ds[:, cols] = (dp * es[side].astype(F32)).astype(BF)
            dkv[i, hd:, cols] = mm(dos[side], es[side], TN)[:hd].astype(BF)
        dkv[i, :hd, :] = mm(qt_in[row, i], ds[...], NN).astype(BF)
        keys = jnp.concatenate([kv[:hd] for kv in kvs], axis=1)
        dq[i] = (mm(keys, ds[...], NT) * (hd**-0.5)).astype(BF)
        return 0

    lax.fori_loop(0, 2, one_head, 0)


def joined(refs, cols):
    return jnp.concatenate([ref[h, :, cols] for ref in refs for h in range(ref.shape[0])], axis=0)


def inputs_step(row, parts, ref):
    dkvs, dqs = [[ref[name, pair] for pair in range(parts // 2)] for name in ("dkv", "dq")]
    w_q, w_kv = ref["w_q"], ref["w_kv"]
    hd = w_q.shape[0] // parts
    here = dqs[0].shape[2]
    at = here + 16
    for b in range(parts):
        w = ref["w", b]
        w_q[b * hd : (b + 1) * hd, :] = w[at : at + hd, :]
        w_kv[b * 2 * hd : (b + 1) * 2 * hd, :] = w[at + hd : at + 3 * hd, :]
    for b in range(parts):
        dx = mm(joined(dkvs, slice(b * here, (b + 1) * here)), w_kv[...], TN)
        if b == 0:
            own = mm(joined(dqs, slice(0, here)), w_q[...], TN)
            ref["dx_own"][...] = dx + own + ref["dh1"][row]
        elif b % 2:
            ref["dx_send"][b // 2] = dx.astype(BF)
        else:
            ref["dx_keep"][...] = dx


def weights_step(row, parts, last, ref):
    dkvs, dqs = [[ref[name, pair] for pair in range(parts // 2)] for name in ("dkv", "dq")]
    here = dqs[0].shape[2]
    model = ref["x", 0].shape[1]
    hd = model // parts
    length = parts * here
    at = (row - 1) * (here + 16) if row else 0
    dq = joined(dqs, slice(0, here))
    gkv = None
    for b in range(parts):
        left = joined(dkvs, slice(b * here, (b + 1) * here))
        term = mm(left, ref["x", b][at : at + here, :], NN)
        gkv = term if gkv is None else gkv + term
    gq = mm(dq, ref["x", 0][at : at + here, :], NN)
    bq = mm(jnp.ones((8, here), BF), dq, NT)[0:1]
    bkv = mm(jnp.ones((8, length), BF), joined(dkvs, slice(0, length)), NT)[0:1]
    for b in range(parts):
        pieces = [
            (slice(0, hd), slice(0, model), gq[b * hd : (b + 1) * hd]),
            (slice(hd, 3 * hd), slice(0, model), gkv[b * 2 * hd : (b + 1) * 2 * hd]),
            (slice(3 * hd, 3 * hd + 1), slice(0, hd), bq[:, b * hd : (b + 1) * hd]),
            (
                slice(3 * hd, 3 * hd + 1),
                slice(hd, 2 * hd),
                bkv[:, b * 2 * hd + hd : (b + 1) * 2 * hd],
            ),
        ]
        out, c = (ref["grads", b % 2], b // 2) if last else (ref["grads"], b)
        out[c, 3 * hd :, :] = jnp.zeros((16, model), out.dtype)
        for rows, cols, value in pieces:
            if ("grads_in",) in ref:
                value = value + ref["grads_in",][b, rows, cols]
            out[c, rows, cols] = value.astype(out.dtype)


def backward_kernel(names, row, n, pairs, parts, want, last, *refs):
    ref = {name if len(name) > 1 else name[0]: r for name, r in zip(names, refs)}
    ref.update({name: r for name, r in zip(names, refs) if len(name) == 1})
    for pair in pairs:
        heads_step(row, n, pair, ref)
    if "weights" in want:
        weights_step(row, parts, last, ref)
    if "inputs" in want:
        inputs_step(row, parts, ref)


def backward(row, n, pairs, want, last, ins):
    parts = 4
    el = ins["el", 0]
    here, half = el.shape[2:]
    length = 2 * half
    hd = ins["kvl", 0].shape[2] // 2
    model = ins["x", 0].shape[1]
    size = 3 * hd + 16
    use = set()
    outs, scratch = {}, {}
    for pair in pairs:
        use |= {("el", pair), ("kvl", pair), ("qt", pair), ("er",), ("kvr",), ("do",), ("weight",)}
        scratch["ds",] = ((here, length), BF)
    shapes = {"dkv": ((2, 2 * hd, length), BF), "dq": ((2, hd, here), BF)}
    for pair in range(parts // 2):
        for name, shape in shapes.items():
            if pair in pairs:
                (outs if len(want) < 2 else scratch)[name, pair] = shape
            elif want:
                use.add((name, pair))
    if "inputs" in want:
        use |= {("w", b) for b in range(parts)} | {("dh1",)}
        outs["dx_own",] = ((here, model), F32)
        outs["dx_keep",] = ((here, model), F32)
        outs["dx_send",] = ((parts // 2, here, model), BF)
        scratch["w_kv",] = ((2 * model, model), BF)
        scratch["w_q",] = ((model, model), BF)
    if "weights" in want:
        use |= {("x", b) for b in range(parts)}
        if ("grads_in",) in ins:
            use.add(("grads_in",))
        if last:
            outs["grads", 0] = ((parts // 2, size, model), F32)
            outs["grads", 1] = ((parts // 2, size, model), BF)
        else:
            outs["grads",] = ((parts, size, model), F32)
    order = sorted(use, key=str)
    names = tuple(order) + tuple(outs) + tuple(scratch)
    done = call(
        functools.partial(backward_kernel, names, row, n, pairs, parts, want, last),
        "backward",
        [ins[name] for name in order],
        list(outs.values()),
        list(scratch.values()),
        limit=LIMITS[2],
    )
    return dict(zip(outs, done))


def add_kernel(rows, *refs):
    owns, nears, fars, out = refs[:rows], refs[rows : 2 * rows], refs[2 * rows : -1], refs[-1]
    for r in range(rows):
        out[r] = owns[r][...] + nears[r][0].astype(F32) + fars[r][...].astype(F32)


def add_inputs(owns, nears, fars):
    rows = len(owns)
    (out,) = call(
        functools.partial(add_kernel, rows),
        "add_inputs",
        (*owns, *nears, *fars),
        [((rows,) + owns[0].shape, F32)],
        limit=LIMITS[3],
    )
    return out


def finish_one_kernel(a, b, qkv, bias):
    width = qkv.shape[1]
    total = a[...].astype(F32) + b[...].astype(F32)
    for c in range(3):
        qkv[c] = total[c * width : (c + 1) * width]
    line = total[3 * width : 3 * width + 1]
    bias[0:1, :] = line[:, 0:width]
    bias[1:2, :] = line[:, width : 2 * width]


def finish_two_kernel(a, b, w_out, w_in, b_in, w_back, *sums):
    width, model = w_out.shape
    units = w_back.shape[0]
    half = model // 2
    total = a[...].astype(F32) + b[...].astype(F32)
    w_out[...] = total[:width]
    at = width
    w_in[0:half, :] = total[at : at + half, 0:units]
    w_in[half:, :] = total[at : at + half, units : 2 * units]
    at += half
    w_back[...] = total[at : at + units]
    at += units
    b_in[...] = total[at : at + 1, 0:units]
    for i, out in enumerate(sums):
        out[...] = total[at + 1 + i : at + 2 + i]


def swap(value, axis, size, bit):
    return lax.ppermute(value, axis, [(i, i ^ bit) for i in range(size)])


def after(value, *others):
    return lax.optimization_barrier((value, *others))[0]


def layer(mesh_sizes, *args):
    (inputs, segments, w_qkv, b_qv, w_out, b_out, gain_one, shift_one) = args[:8]
    (w_in, b_in, w_back, b_back, gain_two, shift_two, cotangent) = args[8:]
    dp, mp = mesh_sizes
    rows, here, model = inputs.shape
    heads = HEADS
    width = w_qkv.shape[2]
    units = w_in.shape[1]

    def near(value):
        return swap(value, "mp", mp, 1)

    def far(value):
        return swap(value, "mp", mp, 2)

    first, *later, two, biases = pack(
        w_qkv, b_qv, w_out, b_out, w_in, b_in, w_back, b_back, segments, inputs
    )
    vectors = [v.reshape(1, model) for v in (gain_one, shift_one, gain_two, shift_two)]
    vectors.append(biases)
    hd = model // heads
    first_far = far(first)
    first_near = near(first)
    mine, nears, fars = [first], [first_near], [first_far]
    if rows > 1:
        nears.append(near(later[0]))
        fars.append(far(after(later[0], first_near)))
        mine.append(later[0])
    two_far = far(after(two, nears[-1]))
    two_near = near(after(two, nears[-1]))
    locals_of = [attend_local(mine, nears, (first, first_near), rows, here, hd)]
    first_both = near(after(first_far, locals_of[0][2]))
    boths = [first_both]
    ws = (first, first_near, first_far, first_both)
    locals_of.append(attend_local(mine, nears, ws[2:], rows, here, hd))
    queries, outs, tops = zip(*[out[3:6] for out in locals_of])
    remotes = []
    for c, rows_of in enumerate([[0], list(range(1, rows))][: min(rows, 2)]):
        if c == 1:
            boths.append(near(after(fars[1], remotes[0][2])))
        xs = [fars[c], boths[c]]
        remotes.append(attend_remote(rows_of, queries, outs, tops, xs, ws, here, hd))
    blocks = [[group[min(r, 1)] for group in (mine, nears, fars, boths)] for r in range(rows)]
    two_both = near(after(two_far, remotes[-1][2]))
    result, keep_two, send_two, dh1s, dos = middle(
        [out[2] for out in remotes],
        mine,
        cotangent,
        [two, two_near, two_far, two_both],
        vectors,
        heads,
    )

    def halved(keep, send):
        got = near(send)
        mine = keep[0] + got[0].astype(F32)
        return mine, (keep[1] + got[1].astype(F32)).astype(BF)

    def over_dp(value, bits, tied=()):
        for bit in bits:
            sent = value.astype(BF)
            if bit == bits[-1] and tied:
                sent = after(sent, *tied)
            got = swap(sent, "dp", dp, bit)
            yield sent, got
            value = sent.astype(F32) + got.astype(F32)

    bits = [1 << k for k in range(dp.bit_length() - 1)]


    def inputs_of(r, **more):
        er, kvr, _, weight = remotes[min(r, 1)]
        ins = {("er",): er, ("kvr",): kvr, ("weight",): weight, ("do",): dos, ("dh1",): dh1s}
        for pair in range(heads // 2):
            names = (("el", pair), ("kvl", pair), ("qt", pair))
            ins.update(zip(names, locals_of[pair][:3]))
        for b in range(mp):
            ins["w", b] = ws[b]
            ins["x", b] = blocks[r][b]
        return ins

    def hold(ins, *ready):
        name = next(n for n in (("er",), ("dh1",)) if n in ins)
        ins[name] = after(ins[name], *ready)
        return ins

    def run(r, pairs, want, ins, last=False):
        return backward(r, max(r - 1, 0), pairs, want, last, ins)

    got_two = near(send_two)
    other_two = steps_two = step_two = None
    grads = None
    owns, near_got, far_got = [], [], []
    ready = []
    both = tuple(range(heads // 2))
    for r in range(rows):
        last = r == rows - 1
        ins = inputs_of(r)
        if ready:
            hold(ins, *ready)
        if r == 0:
            ins.update(run(0, both[:1], (), ins))
            got_two = after(got_two, ins["dkv", 0])
            other_two = (keep_two[1] + got_two[1].astype(F32)).astype(BF)
            far_two = far(other_two)
            hold(ins, other_two)
            ins.update(run(0, both[1:], () if last else ("inputs",), ins))
        else:
            ins.update(run(r, both, (), ins))
            flag = ins["dkv", 0]
            if r > 1 or last:
                far_got[-1] = after(far_got[-1], flag)
        flag = ins["dkv", 1]
        if steps_two is None:
            value_two = keep_two[0] + got_two[0].astype(F32) + after(far_two, flag).astype(F32)
            steps_two = over_dp(value_two, bits[::-1])
            step_two = next(steps_two)
            tie = (step_two[0],)
        else:
            tie = (step_two[1], *far_got)
        if grads is not None:
            ins["grads_in",] = grads
        if last:
            break
        if r:
            ins["dh1",] = after(ins["dh1",], *tie)
            ins.update(run(r, (), ("inputs",), ins))
        got = near(ins["dx_send",] if r else after(ins["dx_send",], *tie))
        owns.append(ins["dx_own",])
        ins["x", 0] = after(ins["x", 0], ins["dx_send",])
        grads = run(r, (), ("weights",), ins)["grads",]
        got = after(got, grads)
        near_got.append(got)
        other = (ins["dx_keep",] + got[1].astype(F32)).astype(BF)
        far_got.append(far(other))
        ready = [other, step_two[0]]
    ins["x", 0] = after(ins["x", 0], *tie)
    row = run(r, (), ("weights",), ins, True)
    mine_one, other_one = halved(row["grads", 0], row["grads", 1])
    far_one = far(other_one)
    ins["dh1",] = after(ins["dh1",], other_one)
    row = run(r, (), ("inputs",), ins)
    got = near(row["dx_send",])
    owns.append(row["dx_own",])
    near_got.append(got)
    value_one = mine_one + far_one.astype(F32)
    total_one = None
    for k, total_one in enumerate(over_dp(value_one, bits)):
        if k == 0:
            other = (row["dx_keep",] + after(got[1], total_one[0]).astype(F32)).astype(BF)
            far_got.append(far(other))
    total_two = step_two
    for total_two in steps_two:
        pass
    grad_inputs = add_inputs(owns, near_got, far_got)
    grad_out, grad_in, grad_b_in, grad_back, *sums = call(
        finish_two_kernel,
        "finish_two",
        total_two,
        [
            ((width, model), F32),
            ((model, units), F32),
            ((1, units), F32),
            ((units, model), F32),
        ]
        + [((1, model), F32)] * 6,
    )
    grad_qkv, grad_bias = call(
        finish_one_kernel,
        "finish_one",
        (after(total_one[0], grad_inputs), total_one[1]),
        [((3, width, model), F32), ((2, width), F32)],
    )
    sums = [s.reshape(model) for s in sums]
    return (
        result,
        grad_inputs,
        grad_qkv.transpose(0, 2, 1),
        grad_bias,
        grad_out,
        sums[0],
        sums[1],
        sums[2],
        grad_in,
        grad_b_in.reshape(units),
        grad_back,
        sums[3],
        sums[4],
        sums[5],
    )


def solution(mesh):
    in_specs = (
        P("dp", "mp", None),
        P("dp", "mp"),
        P(None, None, "mp"),
        P(None, "mp"),
        P("mp", None),
        P(),
        P(),
        P(),
        P(None, "mp"),
        P("mp"),
        P("mp", None),
        P(),
        P(),
        P(),
        P("dp", "mp", None),
    )
    out_specs = (
        P("dp", "mp", None),
        P("dp", "mp", None),
        P(None, None, "mp"),
        P(None, "mp"),
        P("mp", None),
        P(),
        P(),
        P(),
        P(None, "mp"),
        P("mp"),
        P("mp", None),
        P(),
        P(),
        P(),
    )
    sizes = (mesh.shape["dp"], mesh.shape["mp"])
    return jax.shard_map(
        functools.partial(layer, sizes),
        mesh=mesh,
        in_specs=in_specs,
        out_specs=out_specs,
        check_vma=False,
    )
```

time: 115 us -> 110 us (0.957)
  waiting for transfers between devices: 27.1 us -> 14 us
  Pallas kernels: 61.3 us -> 65.3 us
  starting transfers between devices: 24.1 us -> 27.2 us
    ppermute x28 -> x25, waiting for transfers between devices: 27.1 us -> 14 us  [swap(): return lax.ppermute(value, axis, [(i, i ^ bit) for i in range(size)])]
    pallas_call x18, Pallas kernels: 61.3 us -> 65.3 us  [call(): pl.pallas_call(kernel, out_shape=[jax.ShapeDtypeStruct(shape, kind) for s...]
    ppermute x28 -> x25, starting transfers between devices: 24.1 us -> 27.2 us  [swap(): return lax.ppermute(value, axis, [(i, i ^ bit) for i in range(size)])]
    reshape x2 -> x0, local copies, waits for them, and re-layouts: 1.32 us -> none  [layer(): v.reshape(1, model)]
    unnamed x10 -> x46, local copies, waits for them, and re-layouts: 0.02 us -> 1.31 us
  transfers between devices with their start and end apart: 28 -> 25, of which waited for: 8 -> 15; matrix products, arithmetic and copies ran while one was open for 2% -> 0% of each run, Pallas kernels for 35% -> 47%
where the time goes in v1:
time: 110 us; the launch traced here: 109 us
  Pallas kernels  65.3 us (59%)
  starting transfers between devices  27.2 us (25%)
  waiting for transfers between devices  14 us (13%)
  local copies, waits for them, and re-layouts  1.33 us (1%)
    pallas_call x18, Pallas kernels, call(): pl.pallas_call(kernel, out_shape=[jax.ShapeDtypeStruct(shape, kind) for s...  65.3 us
    ppermute x25, starting transfers between devices, swap(): return lax.ppermute(value, axis, [(i, i ^ bit) for i in range(size)])  27.2 us
    ppermute x25, waiting for transfers between devices, swap(): return lax.ppermute(value, axis, [(i, i ^ bit) for i in range(size)])  14 us
  transfers between devices with their start and end apart: 25, of which 15 were waited for; matrix products, arithmetic and copies ran while one was open for 0% of the time, Pallas kernels for 47%

profile of v1, /device:TPU:0, one launch (start us, length us, event | category | flops | bytes accessed | tf_op | source)
XLA Modules:
  0.0 109.4 jit_solution(6806221355098412603)
XLA Ops:
  0.6 1.5 %pack.1 = (bf16[736,256]{1,0:T(8,128)(2,1)S(1)}, bf16[1056,256]{1,0:T(8,128)(2,1)S(1)}, bf16[336,256]{1,0:T(8,128)(2,1)S(1)}, f32[8,256]{1,0:T(8,128)S(1)}) custom-call(bf16[3,64,256]{2,1,0:T(8,128)(2,1)} %bitcast.38, bf16[2,64]{1,0:T(2,128)(2,1)} %refs_1_.1, bf16[64,256]{1,0:T(8,128)(2,1)} %refs_2_.1, bf16[256]{0:T(256)(128)(2,1)} %refs_3_.1, ...), custom_call_target="tpu_custom_call" | custom-call | tf_op jit(solution)/shard_map/pack/pallas_call | solution.py:35
  2.7 2.9 %collective-permute-start.2 = (bf16[736,256]{1,0:T(8,128)(2,1)S(1)}, bf16[736,256]{1,0:T(8,128)(2,1)S(1)}, u32[]{:S(2)}, u32[]{:S(2)}) collective-permute-start(bf16[736,256]{1,0:T(8,128)(2,1)S(1)} %get-tuple-element.141.refs_0_.refs_4_.refs_8_.refs_2_.refs_9_.refs_5_), channel_id=1, source_target_pairs={{0,2},{1,3},{2,0},{3,1},{4,6},{5,7},{6,4},{7,5},{8,10},{9,11},{10,... | collective-permute-start | bytes 1130504 | tf_op jit(solution)/shard_map/ppermute | solution.py:647
  5.6 2.0 %collective-permute-start.4 = (bf16[1056,256]{1,0:T(8,128)(2,1)S(1)}, bf16[1056,256]{1,0:T(8,128)(2,1)S(1)}, u32[]{:S(2)}, u32[]{:S(2)}) collective-permute-start(bf16[1056,256]{1,0:T(8,128)(2,1)S(1)} %get-tuple-element.163.refs_1_.refs_3_.refs_5_), channel_id=1, source_target_pairs={{0,2},{1,3},{2,0},{3,1},{4,6},{5,7},{6,4},{7,5},{8,10},{9,11},{10,... | collective-permute-start | bytes 1622024 | tf_op jit(solution)/shard_map/ppermute | solution.py:647
  7.6 5.7 %attend_local.2 = (bf16[3,2,512,1024]{3,2,1,0:T(8,128)(2,1)S(1)}, bf16[3,2,128,1024]{3,2,1,0:T(8,128)(2,1)S(1)}, bf16[3,2,64,512]{3,2,1,0:T(8,128)(2,1)S(1)}, bf...) custom-call(bf16[736,256]{1,0:T(8,128)(2,1)S(1)} %get-tuple-element.141.refs_0_.re, ...), custom_call_target="tpu_custom_call" | custom-call | tf_op jit(solution)/shard_map/attend_local/pallas_call | solution.py:35
  13.3 1.9 %collective-permute-done.2.refs_4_.refs_6_.refs_10_.refs_11_.refs_7_ = bf16[736,256]{1,0:T(8,128)(2,1)S(1)} collective-permute-done((bf16[736,256]{1,0:T(8,128)(2,1)S(1)}, bf16[736,256]{1,0:T(8,128)(2,1)S(1)}, u32[]{:S(2)}, u32[]{:S(2)}) %collective-permute-start.2) | collective-permute-done | bytes 376864 | tf_op jit(solution)/shard_map/ppermute | solution.py:647
  15.2 1.7 %collective-permute-done.3.refs_5_.refs_7_.refs_11_.refs_12_.refs_8_ = bf16[736,256]{1,0:T(8,128)(2,1)S(1)} collective-permute-done((bf16[736,256]{1,0:T(8,128)(2,1)S(1)}, bf16[736,256]{1,0:T(8,128)(2,1)S(1)}, u32[]{:S(2)}, u32[]{:S(2)}) %collective-permute-start.3) | collective-permute-done | bytes 376864 | tf_op jit(solution)/shard_map/ppermute | solution.py:647
  16.9 5.7 %attend_local.3 = (bf16[3,2,512,1024]{3,2,1,0:T(8,128)(2,1)S(1)}, bf16[3,2,128,1024]{3,2,1,0:T(8,128)(2,1)S(1)}, bf16[3,2,64,512]{3,2,1,0:T(8,128)(2,1)S(1)}, bf...) custom-call(bf16[736,256]{1,0:T(8,128)(2,1)S(1)} %get-tuple-element.141.refs_0_.re, ...), custom_call_target="tpu_custom_call" | custom-call | tf_op jit(solution)/shard_map/attend_local/pallas_call | solution.py:35
  23.4 3.3 %attend_remote.2 = (bf16[1,4,512,1024]{3,2,1,0:T(8,128)(2,1)S(1)}, bf16[1,4,128,1024]{3,2,1,0:T(8,128)(2,1)S(1)}, f32[1,4,512,128]{3,2,1,0:T(8,128)S(1)}, bf16[1,4,512,128]{3,2,1,0:T(8,128)(2,1)S(1)}) custom-call(bf16[3,2,512,128]{3,2,1,0:T(8,128)(2,1)S(1)} %get-tuple-element.101.refs_0_, bf16[3,2,512,128]{3,2,1,0:T(8,128)(2,1)S(1)} %get-tuple-element.104.refs_1_, ...), custom_call_target="tpu_custom_call" | custom-call | tf_op jit(solution)/shard_map/attend_remote/pallas_call | solution.py:35
  26.9 2.1 %collective-permute-start.7 = (bf16[336,256]{1,0:T(8,128)(2,1)S(1)}, bf16[336,256]{1,0:T(8,128)(2,1)S(1)}, u32[]{:S(2)}, u32[]{:S(2)}) collective-permute-start(bf16[336,256]{1,0:T(8,128)(2,1)S(1)} %get-tuple-element.114.refs_5_), channel_id=1, source_target_pairs={{0,2},{1,3},{2,0},{3,1},{4,6},{5,7},{6,4},{7,5},{8,10},{9,11},{10,... | collective-permute-start | bytes 516104 | tf_op jit(solution)/shard_map/ppermute | solution.py:647
  29.2 6.7 %attend_remote.3 = (bf16[2,4,512,1024]{3,2,1,0:T(8,128)(2,1)S(1)}, bf16[2,4,128,1024]{3,2,1,0:T(8,128)(2,1)S(1)}, f32[2,4,512,128]{3,2,1,0:T(8,128)S(1)}, bf16[2,4,512,128]{3,2,1,0:T(8,128)(2,1)S(1)}) custom-call(bf16[3,2,512,128]{3,2,1,0:T(8,128)(2,1)S(1)} %get-tuple-element.101.refs_0_, bf16[3,2,512,128]{3,2,1,0:T(8,128)(2,1)S(1)} %get-tuple-element.104.refs_1_, ...), custom_call_target="tpu_custom_call" | custom-call | tf_op jit(solution)/shard_map/attend_remote/pallas_call | solution.py:35
  37.5 9.6 %middle.1 = (bf16[3,512,256]{2,1,0:T(8,128)(2,1)}, f32[2,336,256]{2,1,0:T(8,128)S(1)}, bf16[2,336,256]{2,1,0:T(8,128)(2,1)S(1)}, f32[3,512,256]{2,1,0:T(8,128)S(1)}, bf16[3,4,512,128]{3,2,1,0:T(8,128)(2,1)S(1)}) custom-call(f32[1,4,512,128]{3,2,1,0:T(8,128)S(1)} %get-tuple-element.109.refs_0_, f32[2,4,512,128]{3,2,1,0:T(8,128)S(1)} %get-tuple-element.112.refs_1_, ...), custom_call_target="tpu_custom_call" | custom-call | flops 181193936 | tf_op jit(solution)/shard_map/middle/pallas_call | solution.py:35
  47.6 3.8 %backward.9 = (bf16[2,128,2048]{2,1,0:T(8,128)(2,1)S(1)}, bf16[2,64,512]{2,1,0:T(8,128)(2,1)S(1)}) custom-call(bf16[3,4,512,128]{3,2,1,0:T(8,128)(2,1)S(1)} %get-tuple-element.119.refs_0_.refs_2_, bf16[3,2,512,1024]{3,2,1,0:T(8,128)(2,1)S(1)} %get-tuple-element.120.refs_1_, bf16[1,4,512,1024]{3,2,1,0:T(8,128)(2,1)S(1)} %get-tuple-element.131.refs_2_.refs_5_, ...), custom_call_target="tpu_custom_call" | custom-call | tf_op jit(solution)/shard_map/backward/pallas_call | solution.py:35
  53.0 4.7 %backward.10 = (bf16[2,128,2048]{2,1,0:T(8,128)(2,1)S(1)}, bf16[2,64,512]{2,1,0:T(8,128)(2,1)S(1)}, f32[512,256]{1,0:T(8,128)S(1)}, f32[512,256]{1,0:T(8,128)S(1)}, bf16[2,512,256]{2,1,0:T(8,128)(2,1)S(1)}) custom-call(f32[3,512,256]{2,1,0:T(8,128)S(1)} %get-tuple-element.166.refs_0_, bf16[2,128,2048]{2,1,0:T(8,128)(2,1)S(1)} %get-tuple-element.125.refs_1_.refs_0_, ...), custom_call_target="tpu_custom_call" | custom-call | tf_op jit(solution)/shard_map/backward/pallas_call | solution.py:35
  60.1 1.6 %collective-permute-start.13 = (bf16[512,256]{1,0:T(8,128)(2,1)S(1)}, bf16[512,256]{1,0:T(8,128)(2,1)S(1)}, u32[]{:S(2)}, u32[]{:S(2)}) collective-permute-start(bf16[512,256]{1,0:T(8,128)(2,1)S(1)} %fusion.1), channel_id=1, source_target_pairs={{0,2},{1,3},{2,0},{3,1},{4,6},{5,7},{6,4},{7,5},{8,10},{9,11},{10,... | collective-permute-start | bytes 786440 | tf_op jit(solution)/shard_map/ppermute | solution.py:647
  61.8 2.6 %collective-permute-start.11 = (bf16[336,256]{1,0:T(8,128)(2,1)S(1)}, bf16[336,256]{1,0:T(8,128)(2,1)S(1)}, u32[]{:S(2)}, u32[]{:S(2)}) collective-permute-start(bf16[336,256]{1,0:T(8,128)(2,1)S(1)} %fusion.2), channel_id=1, source_target_pairs={{0,16},{4,20},{8,24},{12,28},{16,0},{20,4},{24,8},{28,12},{1,17},{... | collective-permute-start | bytes 516104 | tf_op jit(solution)/shard_map/ppermute | solution.py:647
  64.4 7.9 %backward.12 = (bf16[2,128,2048]{2,1,0:T(8,128)(2,1)S(1)}, bf16[2,64,512]{2,1,0:T(8,128)(2,1)S(1)}, bf16[2,128,2048]{2,1,0:T(8,128)(2,1)S(1)}, bf16[2,64,512]{2,1,0:T(8,128)(2,1)S(1)}) custom-call(bf16[3,4,512,128]{3,2,1,0:T(8,128)(2,1)S(1)} %get-tuple-element.119.refs_0_.refs_2_, bf16[3,2,512,1024]{3,2,1,0:T(8,128)(2,1)S(1)} %get-tuple-element.120.refs_1_, ...), custom_call_target="tpu_custom_call" | custom-call | tf_op jit(solution)/shard_map/backward/pallas_call | solution.py:35
  75.9 7.7 %backward.15 = (bf16[2,128,2048]{2,1,0:T(8,128)(2,1)S(1)}, bf16[2,64,512]{2,1,0:T(8,128)(2,1)S(1)}, bf16[2,128,2048]{2,1,0:T(8,128)(2,1)S(1)}, bf16[2,64,512]{2,1,0:T(8,128)(2,1)S(1)}) custom-call(bf16[3,4,512,128]{3,2,1,0:T(8,128)(2,1)S(1)} %get-tuple-element.119.refs_0_.refs_2_, bf16[3,2,512,1024]{3,2,1,0:T(8,128)(2,1)S(1)} %get-tuple-element.120.refs_1_, ...), custom_call_target="tpu_custom_call" | custom-call | tf_op jit(solution)/shard_map/backward/pallas_call | solution.py:35
  88.1 1.5 %collective-permute-start.23 = (bf16[336,256]{1,0:T(8,128)(2,1)S(1)}, bf16[336,256]{1,0:T(8,128)(2,1)S(1)}, u32[]{:S(2)}, u32[]{:S(2)}) collective-permute-start(bf16[336,256]{1,0:T(8,128)(2,1)S(1)} %add_convert_fusion.2), channel_id=1, source_target_pairs={{0,8},{4,12},{8,0},{12,4},{16,24},{20,28},{24,16},{28,20},{1,9},{5... | collective-permute-start | bytes 516104 | tf_op jit(solution)/shard_map/ppermute | solution.py:647
  91.7 1.6 %collective-permute-start.20 = (bf16[208,256]{1,0:T(8,128)(2,1)S(1)}, bf16[208,256]{1,0:T(8,128)(2,1)S(1)}, u32[]{:S(2)}, u32[]{:S(2)}) collective-permute-start(bf16[208,256]{1,0:T(8,128)(2,1)S(1)} %fusion.3), channel_id=1, source_target_pairs={{0,4},{4,0},{8,12},{12,8},{16,20},{20,16},{24,28},{28,24},{1,5},{5... | collective-permute-start | bytes 319496 | tf_op jit(solution)/shard_map/ppermute | solution.py:647
  94.4 1.6 %collective-permute-start.24 = (bf16[336,256]{1,0:T(8,128)(2,1)S(1)}, bf16[336,256]{1,0:T(8,128)(2,1)S(1)}, u32[]{:S(2)}, u32[]{:S(2)}) collective-permute-start(bf16[336,256]{1,0:T(8,128)(2,1)S(1)} %add_convert_fusion.1.a), channel_id=1, source_target_pairs={{0,4},{4,0},{8,12},{12,8},{16,20},{20,16},{24,28},{28,24},{1,5},{5... | collective-permute-start | bytes 516104 | tf_op jit(solution)/shard_map/ppermute | solution.py:647
  97.1 1.5 %collective-permute-start.21 = (bf16[208,256]{1,0:T(8,128)(2,1)S(1)}, bf16[208,256]{1,0:T(8,128)(2,1)S(1)}, u32[]{:S(2)}, u32[]{:S(2)}) collective-permute-start(bf16[208,256]{1,0:T(8,128)(2,1)S(1)} %add_convert_fusion.5), channel_id=1, source_target_pairs={{0,8},{4,12},{8,0},{12,4},{16,24},{20,28},{24,16},{28,20},{1,9},{5... | collective-permute-start | bytes 319496 | tf_op jit(solution)/shard_map/ppermute | solution.py:647
  98.6 2.1 %collective-permute-start.19 = (bf16[512,256]{1,0:T(8,128)(2,1)S(1)}, bf16[512,256]{1,0:T(8,128)(2,1)S(1)}, u32[]{:S(2)}, u32[]{:S(2)}) collective-permute-start(bf16[512,256]{1,0:T(8,128)(2,1)S(1)} %add_convert_fusion), channel_id=1, source_target_pairs={{0,2},{1,3},{2,0},{3,1},{4,6},{5,7},{6,4},{7,5},{8,10},{9,11},{10,... | collective-permute-start | bytes 786440 | tf_op jit(solution)/shard_map/ppermute | solution.py:647
  101.9 2.3 %collective-permute-start.22 = (bf16[208,256]{1,0:T(8,128)(2,1)S(1)}, bf16[208,256]{1,0:T(8,128)(2,1)S(1)}, u32[]{:S(2)}, u32[]{:S(2)}) collective-permute-start(bf16[208,256]{1,0:T(8,128)(2,1)S(1)} %add_convert_fusion.4.a), channel_id=1, source_target_pairs={{0,16},{4,20},{8,24},{12,28},{16,0},{20,4},{24,8},{28,12},{1,17},{... | collective-permute-start | bytes 319496 | tf_op jit(solution)/shard_map/ppermute | solution.py:647
  106.5 2.2 %collective-permute-done.22.b = bf16[208,256]{1,0:T(8,128)(2,1)S(1)} collective-permute-done((bf16[208,256]{1,0:T(8,128)(2,1)S(1)}, bf16[208,256]{1,0:T(8,128)(2,1)S(1)}, u32[]{:S(2)}, u32[]{:S(2)}) %collective-permute-start.22) | collective-permute-done | bytes 106528 | tf_op jit(solution)/shard_map/ppermute | solution.py:647
  (102 shorter events, 24.1 us)
Async XLA Ops:
  2.1 5.5 %collective-permute-start.1 = (bf16[1056,256]{1,0:T(8,128)(2,1)S(1)}, bf16[1056,256]{1,0:T(8,128)(2,1)S(1)}, u32[]{:S(2)}, u32[]{:S(2)}) collective-permute-start(bf16[1056,256]{1,0:T(8,128)(2,1)S(1)} %get-tuple-element.163.refs_1_.refs_3_.refs_5_), channel_id=1, source_target_pairs={{0,1},{1,0},{2,3},{3,2},{4,5},{5,4},{6,7},{7,6},{8,9},{9,8},{10,11... | collective-permute-start | bytes 1622024 | tf_op jit(solution)/shard_map/ppermute | solution.py:647
  2.6 3.0 %collective-permute-start = (bf16[736,256]{1,0:T(8,128)(2,1)S(1)}, bf16[736,256]{1,0:T(8,128)(2,1)S(1)}, u32[]{:S(2)}, u32[]{:S(2)}) collective-permute-start(bf16[736,256]{1,0:T(8,128)(2,1)S(1)} %get-tuple-element.141.refs_0_.refs_4_.refs_8_.refs_2_.refs_9_.refs_5_), channel_id=1, source_target_pairs={{0,1},{1,0},{2,3},{3,2},{4,5},{5,4},{6,7},{7,6},{8,9},{9,8},{10,11... | collective-permute-start | bytes 1130504 | tf_op jit(solution)/shard_map/ppermute | solution.py:647
  2.7 12.5 %collective-permute-start.2 = (bf16[736,256]{1,0:T(8,128)(2,1)S(1)}, bf16[736,256]{1,0:T(8,128)(2,1)S(1)}, u32[]{:S(2)}, u32[]{:S(2)}) collective-permute-start(bf16[736,256]{1,0:T(8,128)(2,1)S(1)} %get-tuple-element.141.refs_0_.refs_4_.refs_8_.refs_2_.refs_9_.refs_5_), channel_id=1, source_target_pairs={{0,2},{1,3},{2,0},{3,1},{4,6},{5,7},{6,4},{7,5},{8,10},{9,11},{10,... | collective-permute-start | bytes 1130504 | tf_op jit(solution)/shard_map/ppermute | solution.py:647
  5.6 21.1 %collective-permute-start.4 = (bf16[1056,256]{1,0:T(8,128)(2,1)S(1)}, bf16[1056,256]{1,0:T(8,128)(2,1)S(1)}, u32[]{:S(2)}, u32[]{:S(2)}) collective-permute-start(bf16[1056,256]{1,0:T(8,128)(2,1)S(1)} %get-tuple-element.163.refs_1_.refs_3_.refs_5_), channel_id=1, source_target_pairs={{0,2},{1,3},{2,0},{3,1},{4,6},{5,7},{6,4},{7,5},{8,10},{9,11},{10,... | collective-permute-start | bytes 1622024 | tf_op jit(solution)/shard_map/ppermute | solution.py:647
  15.2 1.7 %collective-permute-start.3 = (bf16[736,256]{1,0:T(8,128)(2,1)S(1)}, bf16[736,256]{1,0:T(8,128)(2,1)S(1)}, u32[]{:S(2)}, u32[]{:S(2)}) collective-permute-start(bf16[736,256]{1,0:T(8,128)(2,1)S(1)} %collective-permute-done.2.refs_4_.refs_6_.refs_10_.refs_11_.refs_7_), channel_id=1, source_target_pairs={{0,1},{1,0},{2,3},{3,2},{4,5},{5,4},{6,7},{7,6},{8,9},{9,8},{10,11... | collective-permute-start | bytes 1130504 | tf_op jit(solution)/shard_map/ppermute | solution.py:647
  26.7 2.4 %collective-permute-start.5 = (bf16[1056,256]{1,0:T(8,128)(2,1)S(1)}, bf16[1056,256]{1,0:T(8,128)(2,1)S(1)}, u32[]{:S(2)}, u32[]{:S(2)}) collective-permute-start(bf16[1056,256]{1,0:T(8,128)(2,1)S(1)} %collective-permute-done.4.refs_6_.refs_7_), channel_id=1, source_target_pairs={{0,1},{1,0},{2,3},{3,2},{4,5},{5,4},{6,7},{7,6},{8,9},{9,8},{10,11... | collective-permute-start | bytes 1622024 | tf_op jit(solution)/shard_map/ppermute | solution.py:647
  26.9 9.0 %collective-permute-start.7 = (bf16[336,256]{1,0:T(8,128)(2,1)S(1)}, bf16[336,256]{1,0:T(8,128)(2,1)S(1)}, u32[]{:S(2)}, u32[]{:S(2)}) collective-permute-start(bf16[336,256]{1,0:T(8,128)(2,1)S(1)} %get-tuple-element.114.refs_5_), channel_id=1, source_target_pairs={{0,2},{1,3},{2,0},{3,1},{4,6},{5,7},{6,4},{7,5},{8,10},{9,11},{10,... | collective-permute-start | bytes 516104 | tf_op jit(solution)/shard_map/ppermute | solution.py:647
  29.1 7.4 %collective-permute-start.6 = (bf16[336,256]{1,0:T(8,128)(2,1)S(1)}, bf16[336,256]{1,0:T(8,128)(2,1)S(1)}, u32[]{:S(2)}, u32[]{:S(2)}) collective-permute-start(bf16[336,256]{1,0:T(8,128)(2,1)S(1)} %get-tuple-element.114.refs_5_), channel_id=1, source_target_pairs={{0,1},{1,0},{2,3},{3,2},{4,5},{5,4},{6,7},{7,6},{8,9},{9,8},{10,11... | collective-permute-start | bytes 516104 | tf_op jit(solution)/shard_map/ppermute | solution.py:647
  36.0 1.5 %collective-permute-start.8 = (bf16[336,256]{1,0:T(8,128)(2,1)S(1)}, bf16[336,256]{1,0:T(8,128)(2,1)S(1)}, u32[]{:S(2)}, u32[]{:S(2)}) collective-permute-start(bf16[336,256]{1,0:T(8,128)(2,1)S(1)} %collective-permute-done.7.refs_7_), channel_id=1, source_target_pairs={{0,1},{1,0},{2,3},{3,2},{4,5},{5,4},{6,7},{7,6},{8,9},{9,8},{10,11... | collective-permute-start | bytes 516104 | tf_op jit(solution)/shard_map/ppermute | solution.py:647
  47.2 4.3 %collective-permute-start.9 = (bf16[2,336,256]{2,1,0:T(8,128)(2,1)S(1)}, bf16[2,336,256]{2,1,0:T(8,128)(2,1)S(1)}, u32[]{:S(2)}, u32[]{:S(2)}) collective-permute-start(bf16[2,336,256]{2,1,0:T(8,128)(2,1)S(1)} %get-tuple-element.129), channel_id=1, source_target_pairs={{0,1},{1,0},{2,3},{3,2},{4,5},{5,4},{6,7},{7,6},{8,9},{9,8},{10,11... | collective-permute-start | bytes 1032200 | tf_op jit(solution)/shard_map/ppermute | solution.py:647
  51.5 6.5 %collective-permute-start.10 = (bf16[336,256]{1,0:T(8,128)(2,1)S(1)}, bf16[336,256]{1,0:T(8,128)(2,1)S(1)}, u32[]{:S(2)}, u32[]{:S(2)}) collective-permute-start(bf16[336,256]{1,0:T(8,128)(2,1)S(1)} %fusion.4), channel_id=1, source_target_pairs={{0,2},{1,3},{2,0},{3,1},{4,6},{5,7},{6,4},{7,5},{8,10},{9,11},{10,... | collective-permute-start | bytes 516104 | tf_op jit(solution)/shard_map/ppermute | solution.py:647
  58.1 2.0 %collective-permute-start.12 = (bf16[2,512,256]{2,1,0:T(8,128)(2,1)S(1)}, bf16[2,512,256]{2,1,0:T(8,128)(2,1)S(1)}, u32[]{:S(2)}, u32[]{:S(2)}) collective-permute-start(bf16[2,512,256]{2,1,0:T(8,128)(2,1)S(1)} %get-tuple-element.139), channel_id=1, source_target_pairs={{0,1},{1,0},{2,3},{3,2},{4,5},{5,4},{6,7},{7,6},{8,9},{9,8},{10,11... | collective-permute-start | bytes 1572872 | tf_op jit(solution)/shard_map/ppermute | solution.py:647
  60.1 12.4 %collective-permute-start.13 = (bf16[512,256]{1,0:T(8,128)(2,1)S(1)}, bf16[512,256]{1,0:T(8,128)(2,1)S(1)}, u32[]{:S(2)}, u32[]{:S(2)}) collective-permute-start(bf16[512,256]{1,0:T(8,128)(2,1)S(1)} %fusion.1), channel_id=1, source_target_pairs={{0,2},{1,3},{2,0},{3,1},{4,6},{5,7},{6,4},{7,5},{8,10},{9,11},{10,... | collective-permute-start | bytes 786440 | tf_op jit(solution)/shard_map/ppermute | solution.py:647
  61.8 10.7 %collective-permute-start.11 = (bf16[336,256]{1,0:T(8,128)(2,1)S(1)}, bf16[336,256]{1,0:T(8,128)(2,1)S(1)}, u32[]{:S(2)}, u32[]{:S(2)}) collective-permute-start(bf16[336,256]{1,0:T(8,128)(2,1)S(1)} %fusion.2), channel_id=1, source_target_pairs={{0,16},{4,20},{8,24},{12,28},{16,0},{20,4},{24,8},{28,12},{1,17},{... | collective-permute-start | bytes 516104 | tf_op jit(solution)/shard_map/ppermute | solution.py:647
  73.3 2.0 %collective-permute-start.14 = (bf16[2,512,256]{2,1,0:T(8,128)(2,1)S(1)}, bf16[2,512,256]{2,1,0:T(8,128)(2,1)S(1)}, u32[]{:S(2)}, u32[]{:S(2)}) collective-permute-start(bf16[2,512,256]{2,1,0:T(8,128)(2,1)S(1)} %get-tuple-element.154), channel_id=1, source_target_pairs={{0,1},{1,0},{2,3},{3,2},{4,5},{5,4},{6,7},{7,6},{8,9},{9,8},{10,11... | collective-permute-start | bytes 1572872 | tf_op jit(solution)/shard_map/ppermute | solution.py:647
  75.4 8.4 %collective-permute-start.15 = (bf16[512,256]{1,0:T(8,128)(2,1)S(1)}, bf16[512,256]{1,0:T(8,128)(2,1)S(1)}, u32[]{:S(2)}, u32[]{:S(2)}) collective-permute-start(bf16[512,256]{1,0:T(8,128)(2,1)S(1)} %fusion), channel_id=1, source_target_pairs={{0,2},{1,3},{2,0},{3,1},{4,6},{5,7},{6,4},{7,5},{8,10},{9,11},{10,... | collective-permute-start | bytes 786440 | tf_op jit(solution)/shard_map/ppermute | solution.py:647
  86.6 5.1 %collective-permute-start.18 = (bf16[208,256]{1,0:T(8,128)(2,1)S(1)}, bf16[208,256]{1,0:T(8,128)(2,1)S(1)}, u32[]{:S(2)}, u32[]{:S(2)}) collective-permute-start(bf16[208,256]{1,0:T(8,128)(2,1)S(1)} %fusion.5), channel_id=1, source_target_pairs={{0,2},{1,3},{2,0},{3,1},{4,6},{5,7},{6,4},{7,5},{8,10},{9,11},{10,... | collective-permute-start | bytes 319496 | tf_op jit(solution)/shard_map/ppermute | solution.py:647
  88.1 6.2 %collective-permute-start.23 = (bf16[336,256]{1,0:T(8,128)(2,1)S(1)}, bf16[336,256]{1,0:T(8,128)(2,1)S(1)}, u32[]{:S(2)}, u32[]{:S(2)}) collective-permute-start(bf16[336,256]{1,0:T(8,128)(2,1)S(1)} %add_convert_fusion.2), channel_id=1, source_target_pairs={{0,8},{4,12},{8,0},{12,4},{16,24},{20,28},{24,16},{28,20},{1,9},{5... | collective-permute-start | bytes 516104 | tf_op jit(solution)/shard_map/ppermute | solution.py:647
  90.5 8.1 %collective-permute-start.17 = (bf16[2,512,256]{2,1,0:T(8,128)(2,1)S(1)}, bf16[2,512,256]{2,1,0:T(8,128)(2,1)S(1)}, u32[]{:S(2)}, u32[]{:S(2)}) collective-permute-start(bf16[2,512,256]{2,1,0:T(8,128)(2,1)S(1)} %get-tuple-element.168), channel_id=1, source_target_pairs={{0,1},{1,0},{2,3},{3,2},{4,5},{5,4},{6,7},{7,6},{8,9},{9,8},{10,11... | collective-permute-start | bytes 1572872 | tf_op jit(solution)/shard_map/ppermute | solution.py:647
  91.7 5.3 %collective-permute-start.20 = (bf16[208,256]{1,0:T(8,128)(2,1)S(1)}, bf16[208,256]{1,0:T(8,128)(2,1)S(1)}, u32[]{:S(2)}, u32[]{:S(2)}) collective-permute-start(bf16[208,256]{1,0:T(8,128)(2,1)S(1)} %fusion.3), channel_id=1, source_target_pairs={{0,4},{4,0},{8,12},{12,8},{16,20},{20,16},{24,28},{28,24},{1,5},{5... | collective-permute-start | bytes 319496 | tf_op jit(solution)/shard_map/ppermute | solution.py:647
  94.4 9.8 %collective-permute-start.24 = (bf16[336,256]{1,0:T(8,128)(2,1)S(1)}, bf16[336,256]{1,0:T(8,128)(2,1)S(1)}, u32[]{:S(2)}, u32[]{:S(2)}) collective-permute-start(bf16[336,256]{1,0:T(8,128)(2,1)S(1)} %add_convert_fusion.1.a), channel_id=1, source_target_pairs={{0,4},{4,0},{8,12},{12,8},{16,20},{20,16},{24,28},{28,24},{1,5},{5... | collective-permute-start | bytes 516104 | tf_op jit(solution)/shard_map/ppermute | solution.py:647
  97.1 4.8 %collective-permute-start.21 = (bf16[208,256]{1,0:T(8,128)(2,1)S(1)}, bf16[208,256]{1,0:T(8,128)(2,1)S(1)}, u32[]{:S(2)}, u32[]{:S(2)}) collective-permute-start(bf16[208,256]{1,0:T(8,128)(2,1)S(1)} %add_convert_fusion.5), channel_id=1, source_target_pairs={{0,8},{4,12},{8,0},{12,4},{16,24},{20,28},{24,16},{28,20},{1,9},{5... | collective-permute-start | bytes 319496 | tf_op jit(solution)/shard_map/ppermute | solution.py:647
  98.6 6.5 %collective-permute-start.19 = (bf16[512,256]{1,0:T(8,128)(2,1)S(1)}, bf16[512,256]{1,0:T(8,128)(2,1)S(1)}, u32[]{:S(2)}, u32[]{:S(2)}) collective-permute-start(bf16[512,256]{1,0:T(8,128)(2,1)S(1)} %add_convert_fusion), channel_id=1, source_target_pairs={{0,2},{1,3},{2,0},{3,1},{4,6},{5,7},{6,4},{7,5},{8,10},{9,11},{10,... | collective-permute-start | bytes 786440 | tf_op jit(solution)/shard_map/ppermute | solution.py:647
  101.9 6.8 %collective-permute-start.22 = (bf16[208,256]{1,0:T(8,128)(2,1)S(1)}, bf16[208,256]{1,0:T(8,128)(2,1)S(1)}, u32[]{:S(2)}, u32[]{:S(2)}) collective-permute-start(bf16[208,256]{1,0:T(8,128)(2,1)S(1)} %add_convert_fusion.4.a), channel_id=1, source_target_pairs={{0,16},{4,20},{8,24},{12,28},{16,0},{20,4},{24,8},{28,12},{1,17},{... | collective-permute-start | bytes 319496 | tf_op jit(solution)/shard_map/ppermute | solution.py:647
  (24 other events, 243.1 us)

commit v2 on v1

--- a/solution.py
+++ b/solution.py
@@ -23,7 +23,7 @@
 TN = (((0,), (0,)), ((), ()))
 
 MB = 2**20
-LIMITS = (10, 16, 8, 8)
+LIMITS = (10, 12, 8, 8)
 
 
 def mm(left, right, dims):
@@ -172,8 +172,8 @@
     count = 2 if rows > 1 else 1
     mine, nears = refs[:count], refs[count : 2 * count]
     ws = refs[2 * count : 2 * count + 2]
-    e_out, kv_out, qt_out, qa_out, o_out, top_out = refs[2 * count + 2 : 2 * count + 8]
-    w_q, w_kv, bias, feats = refs[2 * count + 8 :]
+    e_out, kv_out, qt_out, qa_out, o_out = refs[2 * count + 2 : 2 * count + 7]
+    w_q, w_kv, bias, feats = refs[2 * count + 7 :]
     load_weights(ws, here, hd, w_q, w_kv, bias)
     for r in range(rows):
         at = (r - 1) * (here + 16) if r else 0
@@ -197,11 +197,12 @@
             qt_out[r, i] = qt.astype(BF)
             qa_out[r, i] = jnp.concatenate([qt, first], axis=0).T.astype(BF)
 
+    lane = lax.broadcasted_iota(jnp.int32, (here, 2 * hd), 1)
+
     def one_row(r, _):
         def put(i, expo, out, top, _):
             e_out[r, i] = expo
-            o_out[r, i] = out
-            top_out[r, i] = top
+            o_out[r, i] = jnp.where(lane < 3 * hd // 2, out, top)
 
         queries, kvs = [qa_out[r, i] for i in range(2)], [kv_out[r, i] for i in range(2)]
         attend(queries, kvs, feats[r], None, put)
@@ -222,7 +223,6 @@
             ((rows, 2, hd, here), BF),
             ((rows, 2, here, 2 * hd), BF),
             ((rows, 2, here, 2 * hd), F32),
-            ((rows, 2, here, 2 * hd), F32),
         ],
         [
             ((2 * hd, model), BF),
@@ -236,8 +236,8 @@
 
 
 def remote_kernel(rows, here, hd, *refs):
-    qs, os, tops, xs, ws = refs[:2], refs[2:4], refs[4:6], refs[6:8], refs[8:12]
-    e_out, kv_out, o_out, weight_out, w_q, w_kv, bias, feats = refs[12:]
+    qs, os, xs, ws = refs[:2], refs[2:4], refs[4:6], refs[6:10]
+    e_out, kv_out, o_out, weight_out, w_q, w_kv, bias, feats = refs[10:]
     heads = len(ws)
     load_weights(ws, here, hd, w_q, w_kv, bias)
     for n, row in enumerate(rows):
@@ -262,21 +262,25 @@
             weight_out[n, h] = weight.astype(BF)
 
         queries = [qs[h // 2][r, h % 2] for h in range(heads)]
-        before = [tops[h // 2][r, h % 2] for h in range(heads)]
+        at = 3 * hd // 2
+        before = [
+            jnp.broadcast_to(os[h // 2][r, h % 2, :, at : at + 1], (here, 2 * hd))
+            for h in range(heads)
+        ]
         attend(queries, [kv_out[n, h] for h in range(heads)], feats[n], before, put)
         return 0
 
     lax.fori_loop(0, len(rows), one_row, 0)
 
 
-def attend_remote(rows, queries, outs, tops, xs, ws, here, hd):
+def attend_remote(rows, queries, outs, xs, ws, here, hd):
     model = xs[0].shape[1]
     heads = len(ws)
     count = len(rows)
     return call(
         functools.partial(remote_kernel, rows, here, hd),
         "attend_remote",
-        (*queries, *outs, *tops, *xs, *ws),
+        (*queries, *outs, *xs, *ws),
         [
             ((count, heads, here, 2 * here), BF),
             ((count, heads, 2 * hd, 2 * here), BF),
@@ -303,8 +307,8 @@
     at += 1 + parts
     g_one, e_one, g_two, e_two, biases = refs[at : at + 5]
     result_out, keep_out, send_out, dh1_out, do_out = refs[at + 5 : at + 10]
-    w_out, w_pad, w_in, w_back, o_all, x_all = refs[at + 10 : at + 16]
-    dw_out, dw_in, dw_back, db_in, sums = refs[at + 16 :]
+    w_out, w_pad, w_in, w_back = refs[at + 10 : at + 14]
+    dw_out, dw_in, dw_back, db_in, db_values, sums = refs[at + 14 :]
     w_pad[...] = jnp.zeros(w_pad.shape, BF)
     here, model = cot_in.shape[1:]
     hd = model // heads
@@ -326,11 +330,20 @@
         bias.append(ws[b][at : at + 1, 0:units].astype(F32))
     b_in = jnp.concatenate(bias, axis=1)
     lane = lax.broadcasted_iota(jnp.int32, (here, 2 * hd), 1)
-    for r in range(rows):
-        o_all[r] = os[min(r, 1)][max(r - 1, 0)]
-        at = (r - 1) * (here + 16) if r else 0
-        x_all[r] = xs[min(r, 1)][at : at + here, :]
-    for total in (dw_out, dw_in, dw_back, db_in, sums):
+
+    def o_of(r, h):
+        if groups == 1:
+            return os[0][r, h]
+        return jnp.where(r == 0, os[0][0, h], os[1][jnp.maximum(r - 1, 0), h])
+
+    def x_of(r):
+        first = xs[0][0:here, :].astype(F32)
+        if groups == 1:
+            return first
+        at = pl.multiple_of(jnp.maximum(r - 1, 0) * (here + 16), 16)
+        return jnp.where(r == 0, first, xs[1][pl.ds(at, here), :].astype(F32))
+
+    for total in (dw_out, dw_in, dw_back, db_in, db_values, sums):
         total[...] = jnp.zeros(total.shape, F32)
 
     def norm(h):
@@ -348,7 +361,7 @@
         return jnp.sum(v, axis=0, keepdims=True)
 
     def one_row(r, _):
-        o_in = [o_all[r, h] for h in range(heads)]
+        o_in = [o_of(r, h) for h in range(heads)]
         inv = [1.0 / o[:, hd : hd + 1] for o in o_in]
         normal = [o * i for o, i in zip(o_in, inv)]
         tiles = [
@@ -356,16 +369,16 @@
             for h in range(0, heads, 2)
         ]
         att = jnp.concatenate(tiles, axis=1).astype(BF)
-        h1 = x_all[r].astype(F32) + mm(att, w_out[...], NN) + biases[0:1, :]
+        h1 = x_of(r) + mm(att, w_out[...], NN) + biases[0:1, :]
         n1, rstd1 = norm(h1)
         y1 = n1 * g_one[...] + e_one[...]
         y1b = y1.astype(BF)
         pre = mm(y1b, w_in[...], NN) + b_in
         square = pre * pre
-        th = jnp.tanh(GELU_C * pre * (1.0 + GELU_A * square))
-        half = 0.5 * (1.0 + th)
-        act = (pre * half).astype(BF)
-        slope = half + 0.5 * pre * (1.0 - th * th) * (GELU_C * (1.0 + 3.0 * GELU_A * square))
+        half = 0.5 + 0.5 * jnp.tanh(pre * (GELU_C + GELU_C * GELU_A * square))
+        full = pre * half
+        act = full.astype(BF)
+        slope = half + full * (1.0 - half) * (2.0 * GELU_C + 6.0 * GELU_C * GELU_A * square)
         h2 = y1 + mm(act, w_back[...], NN) + biases[1:2, :]
         n2, rstd2 = norm(h2)
         result_out[r] = (n2 * g_two[...] + e_two[...]).astype(BF)
@@ -391,6 +404,7 @@
             rest = inner - high
             wide = jnp.where(lane == hd, -high, jnp.where(lane == hd + 1, -rest, wide))
             do_out[r, h] = wide.astype(BF)
+        db_values[...] += down(dwide)
         rows_of = [down(dh1), down(dy1 * n1), down(dy1), down(dh2), down(cot * n2), down(cot)]
         for i, row in enumerate(rows_of):
             sums[i : i + 1, :] += row
@@ -412,7 +426,9 @@
         at += units
         out[c, at:, :] = jnp.zeros((16, model), kind)
         out[c, at : at + 1, 0:units] = db_in[:, cols].astype(kind)
-        out[c, at + 1 : at + 7, :] = sums[0:6, :].astype(kind)
+        out[c, at + 1 : at + 7, :] = sums[0:6, :].astype(BF).astype(kind)
+        line = db_values[:, 2 * per * b : 2 * per * b + per]
+        out[c, at + 7 : at + 8, 0:per] = line.astype(kind)
 
 
 def middle(os, xs, cotangent, ws, vectors, heads):
@@ -438,12 +454,11 @@
             ((2 * parts * width, model), BF),
             ((model, parts * units), BF),
             ((parts * units, model), BF),
-            ((rows, heads, here, 2 * hd), F32),
-            ((rows, here, model), BF),
             ((parts * width, model), F32),
             ((model, parts * units), F32),
             ((parts * units, model), F32),
             ((1, parts * units), F32),
+            ((1, 2 * model), F32),
             ((8, model), F32),
         ],
         flops=rows * 6 * here * model * (2 * model + 2 * parts * units),
@@ -503,53 +518,46 @@
             ref["dx_keep"][...] = dx
 
 
-def weights_step(row, parts, last, ref):
-    dkvs, dqs = [[ref[name, pair] for pair in range(parts // 2)] for name in ("dkv", "dq")]
-    here = dqs[0].shape[2]
+def weights_step(row, heads, parts, ref):
+    dkvs = [ref["dkv", h // 2][h % 2] for h in heads]
+    dq = jnp.concatenate([ref["dq", h // 2][h % 2] for h in heads], axis=0)
+    here = dq.shape[1]
     model = ref["x", 0].shape[1]
     hd = model // parts
-    length = parts * here
     at = (row - 1) * (here + 16) if row else 0
-    dq = joined(dqs, slice(0, here))
     gkv = None
     for b in range(parts):
-        left = joined(dkvs, slice(b * here, (b + 1) * here))
+        left = jnp.concatenate([d[:, b * here : (b + 1) * here] for d in dkvs], axis=0)
         term = mm(left, ref["x", b][at : at + here, :], NN)
         gkv = term if gkv is None else gkv + term
     gq = mm(dq, ref["x", 0][at : at + here, :], NN)
     bq = mm(jnp.ones((8, here), BF), dq, NT)[0:1]
-    bkv = mm(jnp.ones((8, length), BF), joined(dkvs, slice(0, length)), NT)[0:1]
-    for b in range(parts):
+    out = ref["grads",]
+    for c, h in enumerate(heads):
         pieces = [
-            (slice(0, hd), slice(0, model), gq[b * hd : (b + 1) * hd]),
-            (slice(hd, 3 * hd), slice(0, model), gkv[b * 2 * hd : (b + 1) * 2 * hd]),
-            (slice(3 * hd, 3 * hd + 1), slice(0, hd), bq[:, b * hd : (b + 1) * hd]),
-            (
-                slice(3 * hd, 3 * hd + 1),
-                slice(hd, 2 * hd),
-                bkv[:, b * 2 * hd + hd : (b + 1) * 2 * hd],
-            ),
+            (slice(0, hd), slice(0, model), gq[c * hd : (c + 1) * hd]),
+            (slice(hd, 3 * hd), slice(0, model), gkv[c * 2 * hd : (c + 1) * 2 * hd]),
+            (slice(3 * hd, 3 * hd + 1), slice(0, hd), bq[:, c * hd : (c + 1) * hd]),
         ]
-        out, c = (ref["grads", b % 2], b // 2) if last else (ref["grads"], b)
         out[c, 3 * hd :, :] = jnp.zeros((16, model), out.dtype)
         for rows, cols, value in pieces:
             if ("grads_in",) in ref:
-                value = value + ref["grads_in",][b, rows, cols]
+                value = value + ref["grads_in",][h, rows, cols]
             out[c, rows, cols] = value.astype(out.dtype)
 
 
-def backward_kernel(names, row, n, pairs, parts, want, last, *refs):
+def backward_kernel(names, row, n, pairs, parts, want, some, *refs):
     ref = {name if len(name) > 1 else name[0]: r for name, r in zip(names, refs)}
     ref.update({name: r for name, r in zip(names, refs) if len(name) == 1})
     for pair in pairs:
         heads_step(row, n, pair, ref)
     if "weights" in want:
-        weights_step(row, parts, last, ref)
+        weights_step(row, some, parts, ref)
     if "inputs" in want:
         inputs_step(row, parts, ref)
 
 
-def backward(row, n, pairs, want, last, ins):
+def backward(row, n, pairs, want, ins, some=(0, 1, 2, 3), kind=F32):
     parts = 4
     el = ins["el", 0]
     here, half = el.shape[2:]
@@ -580,15 +588,11 @@
         use |= {("x", b) for b in range(parts)}
         if ("grads_in",) in ins:
             use.add(("grads_in",))
-        if last:
-            outs["grads", 0] = ((parts // 2, size, model), F32)
-            outs["grads", 1] = ((parts // 2, size, model), BF)
-        else:
-            outs["grads",] = ((parts, size, model), F32)
+        outs["grads",] = ((len(some), size, model), kind)
     order = sorted(use, key=str)
     names = tuple(order) + tuple(outs) + tuple(scratch)
     done = call(
-        functools.partial(backward_kernel, names, row, n, pairs, parts, want, last),
+        functools.partial(backward_kernel, names, row, n, pairs, parts, want, some),
         "backward",
         [ins[name] for name in order],
         list(outs.values()),
@@ -616,17 +620,16 @@
     return out
 
 
-def finish_one_kernel(a, b, qkv, bias):
+def finish_one_kernel(a, b, values, qkv, bias):
     width = qkv.shape[1]
     total = a[...].astype(F32) + b[...].astype(F32)
     for c in range(3):
         qkv[c] = total[c * width : (c + 1) * width]
-    line = total[3 * width : 3 * width + 1]
-    bias[0:1, :] = line[:, 0:width]
-    bias[1:2, :] = line[:, width : 2 * width]
-
-
-def finish_two_kernel(a, b, w_out, w_in, b_in, w_back, *sums):
+    bias[0:1, :] = total[3 * width : 3 * width + 1, 0:width]
+    bias[1:2, :] = values[:, 0:width]
+
+
+def finish_two_kernel(a, b, w_out, w_in, b_in, w_back, values, *sums):
     width, model = w_out.shape
     units = w_back.shape[0]
     half = model // 2
@@ -639,6 +642,7 @@
     w_back[...] = total[at : at + units]
     at += units
     b_in[...] = total[at : at + 1, 0:units]
+    values[...] = total[at + 7 : at + 8]
     for i, out in enumerate(sums):
         out[...] = total[at + 1 + i : at + 2 + i]
 
@@ -686,13 +690,13 @@
     boths = [first_both]
     ws = (first, first_near, first_far, first_both)
     locals_of.append(attend_local(mine, nears, ws[2:], rows, here, hd))
-    queries, outs, tops = zip(*[out[3:6] for out in locals_of])
+    queries, outs = zip(*[out[3:5] for out in locals_of])
     remotes = []
     for c, rows_of in enumerate([[0], list(range(1, rows))][: min(rows, 2)]):
         if c == 1:
             boths.append(near(after(fars[1], remotes[0][2])))
         xs = [fars[c], boths[c]]
-        remotes.append(attend_remote(rows_of, queries, outs, tops, xs, ws, here, hd))
+        remotes.append(attend_remote(rows_of, queries, outs, xs, ws, here, hd))
     blocks = [[group[min(r, 1)] for group in (mine, nears, fars, boths)] for r in range(rows)]
     two_both = near(after(two_far, remotes[-1][2]))
     result, keep_two, send_two, dh1s, dos = middle(
@@ -704,17 +708,14 @@
         heads,
     )
 
-    def halved(keep, send):
-        got = near(send)
-        mine = keep[0] + got[0].astype(F32)
-        return mine, (keep[1] + got[1].astype(F32)).astype(BF)
-
-    def over_dp(value, bits, tied=()):
-        for bit in bits:
+    def over_dp(value, even, odd):
+        for bits in zip(even, odd):
+            pairs = []
+            for d in range(dp):
+                for m in range(mp):
+                    pairs.append((d * mp + m, (d ^ bits[m % 2]) * mp + m))
             sent = value.astype(BF)
-            if bit == bits[-1] and tied:
-                sent = after(sent, *tied)
-            got = swap(sent, "dp", dp, bit)
+            got = lax.ppermute(sent, ("dp", "mp"), pairs)
             yield sent, got
             value = sent.astype(F32) + got.astype(F32)
 
@@ -737,8 +738,8 @@
         ins[name] = after(ins[name], *ready)
         return ins
 
-    def run(r, pairs, want, ins, last=False):
-        return backward(r, max(r - 1, 0), pairs, want, last, ins)
+    def run(r, pairs, want, ins, **more):
+        return backward(r, max(r - 1, 0), pairs, want, ins, **more)
 
     got_two = near(send_two)
     other_two = steps_two = step_two = None
@@ -765,8 +766,9 @@
                 far_got[-1] = after(far_got[-1], flag)
         flag = ins["dkv", 1]
         if steps_two is None:
-            value_two = keep_two[0] + got_two[0].astype(F32) + after(far_two, flag).astype(F32)
-            steps_two = over_dp(value_two, bits[::-1])
+            value_two = (keep_two[0] + got_two[0].astype(F32)).astype(BF).astype(F32)
+            value_two = value_two + after(far_two, flag).astype(F32)
+            steps_two = over_dp(value_two, bits[::-1], bits[::-1])
             step_two = next(steps_two)
             tie = (step_two[0],)
         else:
@@ -788,8 +790,12 @@
         far_got.append(far(other))
         ready = [other, step_two[0]]
     ins["x", 0] = after(ins["x", 0], *tie)
-    row = run(r, (), ("weights",), ins, True)
-    mine_one, other_one = halved(row["grads", 0], row["grads", 1])
+    send = run(r, (), ("weights",), ins, some=(1, 3), kind=BF)["grads",]
+    got = near(send)
+    ins["x", 0] = after(ins["x", 0], send)
+    keep = run(r, (), ("weights",), ins, some=(0, 2))["grads",]
+    mine_one = keep[0] + got[0].astype(F32)
+    other_one = (keep[1] + got[1].astype(F32)).astype(BF)
     far_one = far(other_one)
     ins["dh1",] = after(ins["dh1",], other_one)
     row = run(r, (), ("inputs",), ins)
@@ -798,7 +804,7 @@
     near_got.append(got)
     value_one = mine_one + far_one.astype(F32)
     total_one = None
-    for k, total_one in enumerate(over_dp(value_one, bits)):
+    for k, total_one in enumerate(over_dp(value_one, bits, bits)):
         if k == 0:
             other = (row["dx_keep",] + after(got[1], total_one[0]).astype(F32)).astype(BF)
             far_got.append(far(other))
@@ -806,7 +812,7 @@
     for total_two in steps_two:
         pass
     grad_inputs = add_inputs(owns, near_got, far_got)
-    grad_out, grad_in, grad_b_in, grad_back, *sums = call(
+    grad_out, grad_in, grad_b_in, grad_back, values, *sums = call(
         finish_two_kernel,
         "finish_two",
         total_two,
@@ -816,12 +822,12 @@
             ((1, units), F32),
             ((units, model), F32),
         ]
-        + [((1, model), F32)] * 6,
+        + [((1, model), F32)] * 7,
     )
     grad_qkv, grad_bias = call(
         finish_one_kernel,
         "finish_one",
-        (after(total_one[0], grad_inputs), total_one[1]),
+        (after(total_one[0], grad_inputs), total_one[1], values),
         [((3, width, model), F32), ((2, width), F32)],
     )
     sums = [s.reshape(model) for s in sums]

time: 110 us -> 108 us (0.982)
  waiting for transfers between devices: 14 us -> 15.4 us
  local copies, waits for them, and re-layouts: 1.33 us -> 0.06 us
    ppermute x25 -> x19, starting transfers between devices: 27.2 us -> 15.9 us  [swap(): return lax.ppermute(value, axis, [(i, i ^ bit) for i in range(size)])]
    ppermute x0 -> x6, starting transfers between devices: none -> 10.9 us  [over_dp(): got = lax.ppermute(sent, ('dp', 'mp'), pairs)]
    ppermute x0 -> x6, waiting for transfers between devices: none -> 5.68 us  [over_dp(): got = lax.ppermute(sent, ('dp', 'mp'), pairs)]
    ppermute x25 -> x19, waiting for transfers between devices: 14 us -> 9.75 us  [swap(): return lax.ppermute(value, axis, [(i, i ^ bit) for i in range(size)])]
    unnamed x46 -> x18, local copies, waits for them, and re-layouts: 1.31 us -> 0.04 us
    pallas_call x18 -> x19, Pallas kernels: 65.3 us -> 64.6 us  [call(): pl.pallas_call(kernel, out_shape=[jax.ShapeDtypeStruct(shape, kind) for s...]
  transfers between devices with their start and end apart: 25 -> 25, of which waited for: 15 -> 16; matrix products, arithmetic and copies ran while one was open for 0% -> 0% of each run, Pallas kernels for 47% -> 47%
where the time goes in v2:
time: 108 us
  Pallas kernels  64.6 us (60%)
  starting transfers between devices  26.8 us (25%)
  waiting for transfers between devices  15.4 us (14%)
    pallas_call x19, Pallas kernels, call(): pl.pallas_call(kernel, out_shape=[jax.ShapeDtypeStruct(shape, kind) for s...  64.6 us
    ppermute x19, starting transfers between devices, swap(): return lax.ppermute(value, axis, [(i, i ^ bit) for i in range(size)])  15.9 us
    ppermute x6, starting transfers between devices, over_dp(): got = lax.ppermute(sent, ('dp', 'mp'), pairs)  10.9 us
    ppermute x19, waiting for transfers between devices, swap(): return lax.ppermute(value, axis, [(i, i ^ bit) for i in range(size)])  9.75 us
    ppermute x6, waiting for transfers between devices, over_dp(): got = lax.ppermute(sent, ('dp', 'mp'), pairs)  5.68 us
  transfers between devices with their start and end apart: 25, of which 16 were waited for; matrix products, arithmetic and copies ran while one was open for 0% of the time, Pallas kernels for 47%

profile of v2, /device:TPU:0, one launch (start us, length us, event | category | flops | bytes accessed | tf_op | source)
XLA Modules:
  0.0 108.3 jit_solution(13211002680060343407)
XLA Ops:
  0.6 1.5 %pack.1 = (bf16[736,256]{1,0:T(8,128)(2,1)S(1)}, bf16[1056,256]{1,0:T(8,128)(2,1)S(1)}, bf16[336,256]{1,0:T(8,128)(2,1)S(1)}, f32[8,256]{1,0:T(8,128)S(1)}) custom-call(bf16[3,64,256]{2,1,0:T(8,128)(2,1)} %bitcast.41, bf16[2,64]{1,0:T(2,128)(2,1)} %refs_1_.1, bf16[64,256]{1,0:T(8,128)(2,1)} %refs_2_.1, bf16[256]{0:T(256)(128)(2,1)} %refs_3_.1, ...), custom_call_target="tpu_custom_call" | custom-call | tf_op jit(solution)/shard_map/pack/pallas_call | solution.py:35
  2.7 2.9 %collective-permute-start.2 = (bf16[736,256]{1,0:T(8,128)(2,1)S(1)}, bf16[736,256]{1,0:T(8,128)(2,1)S(1)}, u32[]{:S(2)}, u32[]{:S(2)}) collective-permute-start(bf16[736,256]{1,0:T(8,128)(2,1)S(1)} %get-tuple-element.137.refs_0_.refs_4_.refs_6_.refs_2_.refs_9_.refs_5_), channel_id=1, source_target_pairs={{0,2},{1,3},{2,0},{3,1},{4,6},{5,7},{6,4},{7,5},{8,10},{9,11},{10,... | collective-permute-start | bytes 1130504 | tf_op jit(solution)/shard_map/ppermute | solution.py:651
  5.6 2.0 %collective-permute-start.4 = (bf16[1056,256]{1,0:T(8,128)(2,1)S(1)}, bf16[1056,256]{1,0:T(8,128)(2,1)S(1)}, u32[]{:S(2)}, u32[]{:S(2)}) collective-permute-start(bf16[1056,256]{1,0:T(8,128)(2,1)S(1)} %get-tuple-element.160.refs_1_.refs_3_.refs_5_), channel_id=1, source_target_pairs={{0,2},{1,3},{2,0},{3,1},{4,6},{5,7},{6,4},{7,5},{8,10},{9,11},{10,... | collective-permute-start | bytes 1622024 | tf_op jit(solution)/shard_map/ppermute | solution.py:651
  7.6 5.6 %attend_local.2 = (bf16[3,2,512,1024]{3,2,1,0:T(8,128)(2,1)S(1)}, bf16[3,2,128,1024]{3,2,1,0:T(8,128)(2,1)S(1)}, bf16[3,2,64,512]{3,2,1,0:T(8,128)(2,1)S(1)}, bf...) custom-call(bf16[736,256]{1,0:T(8,128)(2,1)S(1)} %get-tuple-element.137.refs_0_.refs_4_.refs_6_.refs_2_.refs_9_.refs_5_, ...), custom_call_target="tpu_custom_call" | custom-call | tf_op jit(solution)/shard_map/attend_local/pallas_call | solution.py:35
  13.2 2.0 %collective-permute-done.2.refs_4_.refs_8_.refs_11_.refs_6_.refs_7_ = bf16[736,256]{1,0:T(8,128)(2,1)S(1)} collective-permute-done((bf16[736,256]{1,0:T(8,128)(2,1)S(1)}, bf16[736,256]{1,0:T(8,128)(2,1)S(1)}, u32[]{:S(2)}, u32[]{:S(2)}) %collective-permute-start.2) | collective-permute-done | bytes 376864 | tf_op jit(solution)/shard_map/ppermute | solution.py:651
  15.2 1.7 %collective-permute-done.3.refs_5_.refs_9_.refs_12_.refs_7_.refs_8_ = bf16[736,256]{1,0:T(8,128)(2,1)S(1)} collective-permute-done((bf16[736,256]{1,0:T(8,128)(2,1)S(1)}, bf16[736,256]{1,0:T(8,128)(2,1)S(1)}, u32[]{:S(2)}, u32[]{:S(2)}) %collective-permute-start.3) | collective-permute-done | bytes 376864 | tf_op jit(solution)/shard_map/ppermute | solution.py:651
  16.9 5.6 %attend_local.3 = (bf16[3,2,512,1024]{3,2,1,0:T(8,128)(2,1)S(1)}, bf16[3,2,128,1024]{3,2,1,0:T(8,128)(2,1)S(1)}, bf16[3,2,64,512]{3,2,1,0:T(8,128)(2,1)S(1)}, bf...) custom-call(bf16[736,256]{1,0:T(8,128)(2,1)S(1)} %get-tuple-element.137.refs_0_.refs_4_.refs_6_.refs_2_.refs_9_.refs_5_, ...), custom_call_target="tpu_custom_call" | custom-call | tf_op jit(solution)/shard_map/attend_local/pallas_call | solution.py:35
  22.5 3.4 %attend_remote.2 = (bf16[1,4,512,1024]{3,2,1,0:T(8,128)(2,1)S(1)}, bf16[1,4,128,1024]{3,2,1,0:T(8,128)(2,1)S(1)}, f32[1,4,512,128]{3,2,1,0:T(8,128)S(1)}, bf16[1,4,512,128]{3,2,1,0:T(8,128)(2,1)S(1)}) custom-call(bf16[3,2,512,128]{3,2,1,0:T(8,128)(2,1)S(1)} %get-tuple-element.99.refs_0_, bf16[3,2,512,128]{3,2,1,0:T(8,128)(2,1)S(1)} %get-tuple-element.102.refs_1_, ...), custom_call_target="tpu_custom_call" | custom-call | tf_op jit(solution)/shard_map/attend_remote/pallas_call | solution.py:35
  26.3 2.0 %collective-permute-start.7 = (bf16[336,256]{1,0:T(8,128)(2,1)S(1)}, bf16[336,256]{1,0:T(8,128)(2,1)S(1)}, u32[]{:S(2)}, u32[]{:S(2)}) collective-permute-start(bf16[336,256]{1,0:T(8,128)(2,1)S(1)} %get-tuple-element.110.refs_5_), channel_id=1, source_target_pairs={{0,2},{1,3},{2,0},{3,1},{4,6},{5,7},{6,4},{7,5},{8,10},{9,11},{10,... | collective-permute-start | bytes 516104 | tf_op jit(solution)/shard_map/ppermute | solution.py:651
  28.4 7.2 %attend_remote.3 = (bf16[2,4,512,1024]{3,2,1,0:T(8,128)(2,1)S(1)}, bf16[2,4,128,1024]{3,2,1,0:T(8,128)(2,1)S(1)}, f32[2,4,512,128]{3,2,1,0:T(8,128)S(1)}, bf16[2,4,512,128]{3,2,1,0:T(8,128)(2,1)S(1)}) custom-call(bf16[3,2,512,128]{3,2,1,0:T(8,128)(2,1)S(1)} %get-tuple-element.99.refs_0_, bf16[3,2,512,128]{3,2,1,0:T(8,128)(2,1)S(1)} %get-tuple-element.102.refs_1_, ...), custom_call_target="tpu_custom_call" | custom-call | tf_op jit(solution)/shard_map/attend_remote/pallas_call | solution.py:35
  37.1 9.7 %middle.1 = (bf16[3,512,256]{2,1,0:T(8,128)(2,1)}, f32[2,336,256]{2,1,0:T(8,128)S(1)}, bf16[2,336,256]{2,1,0:T(8,128)(2,1)S(1)}, f32[3,512,256]{2,1,0:T(8,128)S(1)}, bf16[3,4,512,128]{3,2,1,0:T(8,128)(2,1)S(1)}) custom-call(f32[1,4,512,128]{3,2,1,0:T(8,128)S(1)} %get-tuple-element.105.refs_0_, f32[2,4,512,128]{3,2,1,0:T(8,128)S(1)} %get-tuple-element.108.refs_1_, ...), custom_call_target="tpu_custom_call" | custom-call | flops 181193936 | tf_op jit(solution)/shard_map/middle/pallas_call | solution.py:35
  47.3 3.9 %backward.10 = (bf16[2,128,2048]{2,1,0:T(8,128)(2,1)S(1)}, bf16[2,64,512]{2,1,0:T(8,128)(2,1)S(1)}) custom-call(bf16[3,4,512,128]{3,2,1,0:T(8,128)(2,1)S(1)} %get-tuple-element.115.refs_0_.refs_2_, bf16[3,2,512,1024]{3,2,1,0:T(8,128)(2,1)S(1)} %get-tuple-element.116.refs_1_, bf16[1,4,512,1024]{3,2,1,0:T(8,128)(2,1)S(1)} %get-tuple-element.127.refs_2_.refs_5_, ...), custom_call_target="tpu_custom_call" | custom-call | tf_op jit(solution)/shard_map/backward/pallas_call | solution.py:35
  52.6 4.7 %backward.11 = (bf16[2,128,2048]{2,1,0:T(8,128)(2,1)S(1)}, bf16[2,64,512]{2,1,0:T(8,128)(2,1)S(1)}, f32[512,256]{1,0:T(8,128)S(1)}, f32[512,256]{1,0:T(8,128)S(1)}, bf16[2,512,256]{2,1,0:T(8,128)(2,1)S(1)}) custom-call(f32[3,512,256]{2,1,0:T(8,128)S(1)} %get-tuple-element.161.refs_0_, bf16[2,128,2048]{2,1,0:T(8,128)(2,1)S(1)} %get-tuple-element.121.refs_1_.refs_0_, ...), custom_call_target="tpu_custom_call" | custom-call | tf_op jit(solution)/shard_map/backward/pallas_call | solution.py:35
  59.8 1.6 %collective-permute-start.13 = (bf16[512,256]{1,0:T(8,128)(2,1)S(1)}, bf16[512,256]{1,0:T(8,128)(2,1)S(1)}, u32[]{:S(2)}, u32[]{:S(2)}) collective-permute-start(bf16[512,256]{1,0:T(8,128)(2,1)S(1)} %fusion.1), channel_id=1, source_target_pairs={{0,2},{1,3},{2,0},{3,1},{4,6},{5,7},{6,4},{7,5},{8,10},{9,11},{10,... | collective-permute-start | bytes 786440 | tf_op jit(solution)/shard_map/ppermute | solution.py:651
  61.4 2.6 %collective-permute-start.11 = (bf16[336,256]{1,0:T(8,128)(2,1)S(1)}, bf16[336,256]{1,0:T(8,128)(2,1)S(1)}, u32[]{:S(2)}, u32[]{:S(2)}) collective-permute-start(bf16[336,256]{1,0:T(8,128)(2,1)S(1)} %fusion.2), channel_id=1, source_target_pairs={{0,16},{1,17},{2,18},{3,19},{4,20},{5,21},{6,22},{7,23},{8,24},{9,... | collective-permute-start | bytes 516104 | tf_op jit(solution)/shard_map/ppermute | solution.py:718
  64.0 7.9 %backward.13 = (bf16[2,128,2048]{2,1,0:T(8,128)(2,1)S(1)}, bf16[2,64,512]{2,1,0:T(8,128)(2,1)S(1)}, bf16[2,128,2048]{2,1,0:T(8,128)(2,1)S(1)}, bf16[2,64,512]{2,1,0:T(8,128)(2,1)S(1)}) custom-call(bf16[3,4,512,128]{3,2,1,0:T(8,128)(2,1)S(1)} %get-tuple-element.115.refs_0_.refs_2_, bf16[3,2,512,1024]{3,2,1,0:T(8,128)(2,1)S(1)} %get-tuple-element.116.refs_1_, ...), custom_call_target="tpu_custom_call" | custom-call | tf_op jit(solution)/shard_map/backward/pallas_call | solution.py:35
  75.6 7.7 %backward.16 = (bf16[2,128,2048]{2,1,0:T(8,128)(2,1)S(1)}, bf16[2,64,512]{2,1,0:T(8,128)(2,1)S(1)}, bf16[2,128,2048]{2,1,0:T(8,128)(2,1)S(1)}, bf16[2,64,512]{2,1,0:T(8,128)(2,1)S(1)}) custom-call(bf16[3,4,512,128]{3,2,1,0:T(8,128)(2,1)S(1)} %get-tuple-element.115.refs_0_.refs_2_, bf16[3,2,512,1024]{3,2,1,0:T(8,128)(2,1)S(1)} %get-tuple-element.116.refs_1_, ...), custom_call_target="tpu_custom_call" | custom-call | tf_op jit(solution)/shard_map/backward/pallas_call | solution.py:35
  85.6 1.5 %collective-permute-start.18 = (bf16[208,256]{1,0:T(8,128)(2,1)S(1)}, bf16[208,256]{1,0:T(8,128)(2,1)S(1)}, u32[]{:S(2)}, u32[]{:S(2)}) collective-permute-start(bf16[208,256]{1,0:T(8,128)(2,1)S(1)} %fusion.9), channel_id=1, source_target_pairs={{0,2},{1,3},{2,0},{3,1},{4,6},{5,7},{6,4},{7,5},{8,10},{9,11},{10,... | collective-permute-start | bytes 319496 | tf_op jit(solution)/shard_map/ppermute | solution.py:651
  87.1 1.5 %collective-permute-start.23 = (bf16[336,256]{1,0:T(8,128)(2,1)S(1)}, bf16[336,256]{1,0:T(8,128)(2,1)S(1)}, u32[]{:S(2)}, u32[]{:S(2)}) collective-permute-start(bf16[336,256]{1,0:T(8,128)(2,1)S(1)} %add_convert_fusion.2), channel_id=1, source_target_pairs={{0,8},{1,9},{2,10},{3,11},{4,12},{5,13},{6,14},{7,15},{8,0},{9,1},... | collective-permute-start | bytes 516104 | tf_op jit(solution)/shard_map/ppermute | solution.py:718
  90.7 1.5 %collective-permute-start.20 = (bf16[208,256]{1,0:T(8,128)(2,1)S(1)}, bf16[208,256]{1,0:T(8,128)(2,1)S(1)}, u32[]{:S(2)}, u32[]{:S(2)}) collective-permute-start(bf16[208,256]{1,0:T(8,128)(2,1)S(1)} %fusion.5), channel_id=1, source_target_pairs={{0,4},{1,5},{2,6},{3,7},{4,0},{5,1},{6,2},{7,3},{8,12},{9,13},{10,... | collective-permute-start | bytes 319496 | tf_op jit(solution)/shard_map/ppermute | solution.py:718
  93.3 1.5 %collective-permute-start.24 = (bf16[336,256]{1,0:T(8,128)(2,1)S(1)}, bf16[336,256]{1,0:T(8,128)(2,1)S(1)}, u32[]{:S(2)}, u32[]{:S(2)}) collective-permute-start(bf16[336,256]{1,0:T(8,128)(2,1)S(1)} %add_convert_fusion.1.a), channel_id=1, source_target_pairs={{0,4},{1,5},{2,6},{3,7},{4,0},{5,1},{6,2},{7,3},{8,12},{9,13},{10,... | collective-permute-start | bytes 516104 | tf_op jit(solution)/shard_map/ppermute | solution.py:718
  97.6 2.1 %collective-permute-start.19 = (bf16[512,256]{1,0:T(8,128)(2,1)S(1)}, bf16[512,256]{1,0:T(8,128)(2,1)S(1)}, u32[]{:S(2)}, u32[]{:S(2)}) collective-permute-start(bf16[512,256]{1,0:T(8,128)(2,1)S(1)} %add_convert_fusion), channel_id=1, source_target_pairs={{0,2},{1,3},{2,0},{3,1},{4,6},{5,7},{6,4},{7,5},{8,10},{9,11},{10,... | collective-permute-start | bytes 786440 | tf_op jit(solution)/shard_map/ppermute | solution.py:651
  100.8 2.3 %collective-permute-start.22 = (bf16[208,256]{1,0:T(8,128)(2,1)S(1)}, bf16[208,256]{1,0:T(8,128)(2,1)S(1)}, u32[]{:S(2)}, u32[]{:S(2)}) collective-permute-start(bf16[208,256]{1,0:T(8,128)(2,1)S(1)} %add_convert_fusion.5.a), channel_id=1, source_target_pairs={{0,16},{1,17},{2,18},{3,19},{4,20},{5,21},{6,22},{7,23},{8,24},{9,... | collective-permute-start | bytes 319496 | tf_op jit(solution)/shard_map/ppermute | solution.py:718
  105.4 2.2 %collective-permute-done.22.b = bf16[208,256]{1,0:T(8,128)(2,1)S(1)} collective-permute-done((bf16[208,256]{1,0:T(8,128)(2,1)S(1)}, bf16[208,256]{1,0:T(8,128)(2,1)S(1)}, u32[]{:S(2)}, u32[]{:S(2)}) %collective-permute-start.22) | collective-permute-done | bytes 106528 | tf_op jit(solution)/shard_map/ppermute | solution.py:718
  (75 shorter events, 22.7 us)
Async XLA Ops:
  2.1 5.5 %collective-permute-start.1 = (bf16[1056,256]{1,0:T(8,128)(2,1)S(1)}, bf16[1056,256]{1,0:T(8,128)(2,1)S(1)}, u32[]{:S(2)}, u32[]{:S(2)}) collective-permute-start(bf16[1056,256]{1,0:T(8,128)(2,1)S(1)} %get-tuple-element.160.refs_1_.refs_3_.refs_5_), channel_id=1, source_target_pairs={{0,1},{1,0},{2,3},{3,2},{4,5},{5,4},{6,7},{7,6},{8,9},{9,8},{10,11... | collective-permute-start | bytes 1622024 | tf_op jit(solution)/shard_map/ppermute | solution.py:651
  2.6 3.0 %collective-permute-start = (bf16[736,256]{1,0:T(8,128)(2,1)S(1)}, bf16[736,256]{1,0:T(8,128)(2,1)S(1)}, u32[]{:S(2)}, u32[]{:S(2)}) collective-permute-start(bf16[736,256]{1,0:T(8,128)(2,1)S(1)} %get-tuple-element.137.refs_0_.refs_4_.refs_6_.refs_2_.refs_9_.refs_5_), channel_id=1, source_target_pairs={{0,1},{1,0},{2,3},{3,2},{4,5},{5,4},{6,7},{7,6},{8,9},{9,8},{10,11... | collective-permute-start | bytes 1130504 | tf_op jit(solution)/shard_map/ppermute | solution.py:651
  2.7 12.5 %collective-permute-start.2 = (bf16[736,256]{1,0:T(8,128)(2,1)S(1)}, bf16[736,256]{1,0:T(8,128)(2,1)S(1)}, u32[]{:S(2)}, u32[]{:S(2)}) collective-permute-start(bf16[736,256]{1,0:T(8,128)(2,1)S(1)} %get-tuple-element.137.refs_0_.refs_4_.refs_6_.refs_2_.refs_9_.refs_5_), channel_id=1, source_target_pairs={{0,2},{1,3},{2,0},{3,1},{4,6},{5,7},{6,4},{7,5},{8,10},{9,11},{10,... | collective-permute-start | bytes 1130504 | tf_op jit(solution)/shard_map/ppermute | solution.py:651
  5.6 20.6 %collective-permute-start.4 = (bf16[1056,256]{1,0:T(8,128)(2,1)S(1)}, bf16[1056,256]{1,0:T(8,128)(2,1)S(1)}, u32[]{:S(2)}, u32[]{:S(2)}) collective-permute-start(bf16[1056,256]{1,0:T(8,128)(2,1)S(1)} %get-tuple-element.160.refs_1_.refs_3_.refs_5_), channel_id=1, source_target_pairs={{0,2},{1,3},{2,0},{3,1},{4,6},{5,7},{6,4},{7,5},{8,10},{9,11},{10,... | collective-permute-start | bytes 1622024 | tf_op jit(solution)/shard_map/ppermute | solution.py:651
  15.2 1.7 %collective-permute-start.3 = (bf16[736,256]{1,0:T(8,128)(2,1)S(1)}, bf16[736,256]{1,0:T(8,128)(2,1)S(1)}, u32[]{:S(2)}, u32[]{:S(2)}) collective-permute-start(bf16[736,256]{1,0:T(8,128)(2,1)S(1)} %collective-permute-done.2.refs_4_.refs_8_.refs_11_.refs_6_.refs_7_), channel_id=1, source_target_pairs={{0,1},{1,0},{2,3},{3,2},{4,5},{5,4},{6,7},{7,6},{8,9},{9,8},{10,11... | collective-permute-start | bytes 1130504 | tf_op jit(solution)/shard_map/ppermute | solution.py:651
  26.2 2.2 %collective-permute-start.5 = (bf16[1056,256]{1,0:T(8,128)(2,1)S(1)}, bf16[1056,256]{1,0:T(8,128)(2,1)S(1)}, u32[]{:S(2)}, u32[]{:S(2)}) collective-permute-start(bf16[1056,256]{1,0:T(8,128)(2,1)S(1)} %collective-permute-done.4.refs_4_.refs_7_), channel_id=1, source_target_pairs={{0,1},{1,0},{2,3},{3,2},{4,5},{5,4},{6,7},{7,6},{8,9},{9,8},{10,11... | collective-permute-start | bytes 1622024 | tf_op jit(solution)/shard_map/ppermute | solution.py:651
  26.3 9.3 %collective-permute-start.7 = (bf16[336,256]{1,0:T(8,128)(2,1)S(1)}, bf16[336,256]{1,0:T(8,128)(2,1)S(1)}, u32[]{:S(2)}, u32[]{:S(2)}) collective-permute-start(bf16[336,256]{1,0:T(8,128)(2,1)S(1)} %get-tuple-element.110.refs_5_), channel_id=1, source_target_pairs={{0,2},{1,3},{2,0},{3,1},{4,6},{5,7},{6,4},{7,5},{8,10},{9,11},{10,... | collective-permute-start | bytes 516104 | tf_op jit(solution)/shard_map/ppermute | solution.py:651
  28.3 7.8 %collective-permute-start.6 = (bf16[336,256]{1,0:T(8,128)(2,1)S(1)}, bf16[336,256]{1,0:T(8,128)(2,1)S(1)}, u32[]{:S(2)}, u32[]{:S(2)}) collective-permute-start(bf16[336,256]{1,0:T(8,128)(2,1)S(1)} %get-tuple-element.110.refs_5_), channel_id=1, source_target_pairs={{0,1},{1,0},{2,3},{3,2},{4,5},{5,4},{6,7},{7,6},{8,9},{9,8},{10,11... | collective-permute-start | bytes 516104 | tf_op jit(solution)/shard_map/ppermute | solution.py:651
  35.6 1.5 %collective-permute-start.8 = (bf16[336,256]{1,0:T(8,128)(2,1)S(1)}, bf16[336,256]{1,0:T(8,128)(2,1)S(1)}, u32[]{:S(2)}, u32[]{:S(2)}) collective-permute-start(bf16[336,256]{1,0:T(8,128)(2,1)S(1)} %collective-permute-done.7.refs_7_), channel_id=1, source_target_pairs={{0,1},{1,0},{2,3},{3,2},{4,5},{5,4},{6,7},{7,6},{8,9},{9,8},{10,11... | collective-permute-start | bytes 516104 | tf_op jit(solution)/shard_map/ppermute | solution.py:651
  46.9 4.3 %collective-permute-start.9 = (bf16[2,336,256]{2,1,0:T(8,128)(2,1)S(1)}, bf16[2,336,256]{2,1,0:T(8,128)(2,1)S(1)}, u32[]{:S(2)}, u32[]{:S(2)}) collective-permute-start(bf16[2,336,256]{2,1,0:T(8,128)(2,1)S(1)} %get-tuple-element.125), channel_id=1, source_target_pairs={{0,1},{1,0},{2,3},{3,2},{4,5},{5,4},{6,7},{7,6},{8,9},{9,8},{10,11... | collective-permute-start | bytes 1032200 | tf_op jit(solution)/shard_map/ppermute | solution.py:651
  51.2 6.5 %collective-permute-start.10 = (bf16[336,256]{1,0:T(8,128)(2,1)S(1)}, bf16[336,256]{1,0:T(8,128)(2,1)S(1)}, u32[]{:S(2)}, u32[]{:S(2)}) collective-permute-start(bf16[336,256]{1,0:T(8,128)(2,1)S(1)} %fusion.7), channel_id=1, source_target_pairs={{0,2},{1,3},{2,0},{3,1},{4,6},{5,7},{6,4},{7,5},{8,10},{9,11},{10,... | collective-permute-start | bytes 516104 | tf_op jit(solution)/shard_map/ppermute | solution.py:651
  57.8 2.0 %collective-permute-start.12 = (bf16[2,512,256]{2,1,0:T(8,128)(2,1)S(1)}, bf16[2,512,256]{2,1,0:T(8,128)(2,1)S(1)}, u32[]{:S(2)}, u32[]{:S(2)}) collective-permute-start(bf16[2,512,256]{2,1,0:T(8,128)(2,1)S(1)} %get-tuple-element.135), channel_id=1, source_target_pairs={{0,1},{1,0},{2,3},{3,2},{4,5},{5,4},{6,7},{7,6},{8,9},{9,8},{10,11... | collective-permute-start | bytes 1572872 | tf_op jit(solution)/shard_map/ppermute | solution.py:651
  59.8 12.3 %collective-permute-start.13 = (bf16[512,256]{1,0:T(8,128)(2,1)S(1)}, bf16[512,256]{1,0:T(8,128)(2,1)S(1)}, u32[]{:S(2)}, u32[]{:S(2)}) collective-permute-start(bf16[512,256]{1,0:T(8,128)(2,1)S(1)} %fusion.1), channel_id=1, source_target_pairs={{0,2},{1,3},{2,0},{3,1},{4,6},{5,7},{6,4},{7,5},{8,10},{9,11},{10,... | collective-permute-start | bytes 786440 | tf_op jit(solution)/shard_map/ppermute | solution.py:651
  61.4 10.7 %collective-permute-start.11 = (bf16[336,256]{1,0:T(8,128)(2,1)S(1)}, bf16[336,256]{1,0:T(8,128)(2,1)S(1)}, u32[]{:S(2)}, u32[]{:S(2)}) collective-permute-start(bf16[336,256]{1,0:T(8,128)(2,1)S(1)} %fusion.2), channel_id=1, source_target_pairs={{0,16},{1,17},{2,18},{3,19},{4,20},{5,21},{6,22},{7,23},{8,24},{9,... | collective-permute-start | bytes 516104 | tf_op jit(solution)/shard_map/ppermute | solution.py:718
  73.0 2.0 %collective-permute-start.14 = (bf16[2,512,256]{2,1,0:T(8,128)(2,1)S(1)}, bf16[2,512,256]{2,1,0:T(8,128)(2,1)S(1)}, u32[]{:S(2)}, u32[]{:S(2)}) collective-permute-start(bf16[2,512,256]{2,1,0:T(8,128)(2,1)S(1)} %get-tuple-element.150), channel_id=1, source_target_pairs={{0,1},{1,0},{2,3},{3,2},{4,5},{5,4},{6,7},{7,6},{8,9},{9,8},{10,11... | collective-permute-start | bytes 1572872 | tf_op jit(solution)/shard_map/ppermute | solution.py:651
  75.1 8.4 %collective-permute-start.15 = (bf16[512,256]{1,0:T(8,128)(2,1)S(1)}, bf16[512,256]{1,0:T(8,128)(2,1)S(1)}, u32[]{:S(2)}, u32[]{:S(2)}) collective-permute-start(bf16[512,256]{1,0:T(8,128)(2,1)S(1)} %fusion), channel_id=1, source_target_pairs={{0,2},{1,3},{2,0},{3,1},{4,6},{5,7},{6,4},{7,5},{8,10},{9,11},{10,... | collective-permute-start | bytes 786440 | tf_op jit(solution)/shard_map/ppermute | solution.py:651
  85.6 5.1 %collective-permute-start.18 = (bf16[208,256]{1,0:T(8,128)(2,1)S(1)}, bf16[208,256]{1,0:T(8,128)(2,1)S(1)}, u32[]{:S(2)}, u32[]{:S(2)}) collective-permute-start(bf16[208,256]{1,0:T(8,128)(2,1)S(1)} %fusion.9), channel_id=1, source_target_pairs={{0,2},{1,3},{2,0},{3,1},{4,6},{5,7},{6,4},{7,5},{8,10},{9,11},{10,... | collective-permute-start | bytes 319496 | tf_op jit(solution)/shard_map/ppermute | solution.py:651
  87.1 6.2 %collective-permute-start.23 = (bf16[336,256]{1,0:T(8,128)(2,1)S(1)}, bf16[336,256]{1,0:T(8,128)(2,1)S(1)}, u32[]{:S(2)}, u32[]{:S(2)}) collective-permute-start(bf16[336,256]{1,0:T(8,128)(2,1)S(1)} %add_convert_fusion.2), channel_id=1, source_target_pairs={{0,8},{1,9},{2,10},{3,11},{4,12},{5,13},{6,14},{7,15},{8,0},{9,1},... | collective-permute-start | bytes 516104 | tf_op jit(solution)/shard_map/ppermute | solution.py:718
  89.4 8.1 %collective-permute-start.17 = (bf16[2,512,256]{2,1,0:T(8,128)(2,1)S(1)}, bf16[2,512,256]{2,1,0:T(8,128)(2,1)S(1)}, u32[]{:S(2)}, u32[]{:S(2)}) collective-permute-start(bf16[2,512,256]{2,1,0:T(8,128)(2,1)S(1)} %get-tuple-element.163), channel_id=1, source_target_pairs={{0,1},{1,0},{2,3},{3,2},{4,5},{5,4},{6,7},{7,6},{8,9},{9,8},{10,11... | collective-permute-start | bytes 1572872 | tf_op jit(solution)/shard_map/ppermute | solution.py:651
  90.7 5.3 %collective-permute-start.20 = (bf16[208,256]{1,0:T(8,128)(2,1)S(1)}, bf16[208,256]{1,0:T(8,128)(2,1)S(1)}, u32[]{:S(2)}, u32[]{:S(2)}) collective-permute-start(bf16[208,256]{1,0:T(8,128)(2,1)S(1)} %fusion.5), channel_id=1, source_target_pairs={{0,4},{1,5},{2,6},{3,7},{4,0},{5,1},{6,2},{7,3},{8,12},{9,13},{10,... | collective-permute-start | bytes 319496 | tf_op jit(solution)/shard_map/ppermute | solution.py:718
  93.3 9.8 %collective-permute-start.24 = (bf16[336,256]{1,0:T(8,128)(2,1)S(1)}, bf16[336,256]{1,0:T(8,128)(2,1)S(1)}, u32[]{:S(2)}, u32[]{:S(2)}) collective-permute-start(bf16[336,256]{1,0:T(8,128)(2,1)S(1)} %add_convert_fusion.1.a), channel_id=1, source_target_pairs={{0,4},{1,5},{2,6},{3,7},{4,0},{5,1},{6,2},{7,3},{8,12},{9,13},{10,... | collective-permute-start | bytes 516104 | tf_op jit(solution)/shard_map/ppermute | solution.py:718
  96.0 4.8 %collective-permute-start.21 = (bf16[208,256]{1,0:T(8,128)(2,1)S(1)}, bf16[208,256]{1,0:T(8,128)(2,1)S(1)}, u32[]{:S(2)}, u32[]{:S(2)}) collective-permute-start(bf16[208,256]{1,0:T(8,128)(2,1)S(1)} %add_convert_fusion.6), channel_id=1, source_target_pairs={{0,8},{1,9},{2,10},{3,11},{4,12},{5,13},{6,14},{7,15},{8,0},{9,1},... | collective-permute-start | bytes 319496 | tf_op jit(solution)/shard_map/ppermute | solution.py:718
  97.6 6.5 %collective-permute-start.19 = (bf16[512,256]{1,0:T(8,128)(2,1)S(1)}, bf16[512,256]{1,0:T(8,128)(2,1)S(1)}, u32[]{:S(2)}, u32[]{:S(2)}) collective-permute-start(bf16[512,256]{1,0:T(8,128)(2,1)S(1)} %add_convert_fusion), channel_id=1, source_target_pairs={{0,2},{1,3},{2,0},{3,1},{4,6},{5,7},{6,4},{7,5},{8,10},{9,11},{10,... | collective-permute-start | bytes 786440 | tf_op jit(solution)/shard_map/ppermute | solution.py:651
  100.8 6.8 %collective-permute-start.22 = (bf16[208,256]{1,0:T(8,128)(2,1)S(1)}, bf16[208,256]{1,0:T(8,128)(2,1)S(1)}, u32[]{:S(2)}, u32[]{:S(2)}) collective-permute-start(bf16[208,256]{1,0:T(8,128)(2,1)S(1)} %add_convert_fusion.5.a), channel_id=1, source_target_pairs={{0,16},{1,17},{2,18},{3,19},{4,20},{5,21},{6,22},{7,23},{8,24},{9,... | collective-permute-start | bytes 319496 | tf_op jit(solution)/shard_map/ppermute | solution.py:718
  (10 other events, 126.6 us)

commit v3 on v2

--- a/solution.py
+++ b/solution.py
@@ -139,7 +139,7 @@
     ones = value_ones(hd, length, hd)
 
     def score(i):
-        scores = mm(queries[i], jnp.concatenate([kvs[i][:hd], feats], axis=0), NN)
+        scores = mm(queries[i], jnp.concatenate([kvs[i][:hd], feats[i]], axis=0), NN)
         top = jnp.max(scores, axis=-1, keepdims=True)
         top = jnp.broadcast_to(top, (scores.shape[0], 2 * hd))
         if before is None:
@@ -199,16 +199,13 @@
 
     lane = lax.broadcasted_iota(jnp.int32, (here, 2 * hd), 1)
 
-    def one_row(r, _):
-        def put(i, expo, out, top, _):
-            e_out[r, i] = expo
-            o_out[r, i] = jnp.where(lane < 3 * hd // 2, out, top)
-
-        queries, kvs = [qa_out[r, i] for i in range(2)], [kv_out[r, i] for i in range(2)]
-        attend(queries, kvs, feats[r], None, put)
-        return 0
-
-    lax.fori_loop(0, rows, one_row, 0)
+    def put(k, expo, out, top, _):
+        e_out[k // 2, k % 2] = expo
+        o_out[k // 2, k % 2] = jnp.where(lane < 3 * hd // 2, out, top)
+
+    queries = [qa_out[r, i] for r in range(rows) for i in range(2)]
+    kvs = [kv_out[r, i] for r in range(rows) for i in range(2)]
+    attend(queries, kvs, [feats[r] for r in range(rows) for i in range(2)], None, put)
 
 
 def attend_local(mine, nears, ws, rows, here, hd):
@@ -267,7 +264,7 @@
             jnp.broadcast_to(os[h // 2][r, h % 2, :, at : at + 1], (here, 2 * hd))
             for h in range(heads)
         ]
-        attend(queries, [kv_out[n, h] for h in range(heads)], feats[n], before, put)
+        attend(queries, [kv_out[n, h] for h in range(heads)], [feats[n]] * heads, before, put)
         return 0
 
     lax.fori_loop(0, len(rows), one_row, 0)
@@ -466,31 +463,34 @@
     )
 
 
-def heads_step(row, n, pair, ref):
-    el_in, kvl_in, qt_in = ref["el", pair], ref["kvl", pair], ref["qt", pair]
-    er_in, kvr_in, do_in, weight_in = ref["er"], ref["kvr"], ref["do"], ref["weight"]
-    dkv, dq, ds = ref["dkv", pair], ref["dq", pair], ref["ds"]
-    hd = qt_in.shape[2]
-    half = kvl_in.shape[3]
+def heads_step(row, n, pairs, ref):
+    er_in, kvr_in, do_in, weight_in, ds = (ref[k] for k in ("er", "kvr", "do", "weight", "ds"))
+    hd = kvr_in.shape[2] // 2
+    half = kvr_in.shape[3]
     ones = value_ones(hd, half, 2)
 
-    def one_head(i, _):
-        h = 2 * pair + i
-        kvs = (kvl_in[row, i], kvr_in[n, h])
-        es, do = (el_in[row, i], er_in[n, h]), do_in[row, h]
+    def one_head(step, _):
+        h = 2 * pairs[0] + step
+        i = step % 2
+
+        def pick(name):
+            found = [ref[name, pair][row, i] for pair in pairs]
+            return found[0] if len(pairs) == 1 else jnp.where(step < 2, *found)
+
+        kvs, es, do = (pick("kvl"), kvr_in[n, h]), (pick("el"), er_in[n, h]), do_in[row, h]
         dos = (do * weight_in[n, h], do)
         for side in range(2):
             cols = slice(side * half, (side + 1) * half)
             values = jnp.concatenate([kvs[side][hd:], ones], axis=0)
             dp = mm(dos[side], values, NN)
             ds[:, cols] = (dp * es[side].astype(F32)).astype(BF)
-            dkv[i, hd:, cols] = mm(dos[side], es[side], TN)[:hd].astype(BF)
-        dkv[i, :hd, :] = mm(qt_in[row, i], ds[...], NN).astype(BF)
+            ref["dkv", pairs[0]][step, hd:, cols] = mm(dos[side], es[side], TN)[:hd].astype(BF)
+        ref["dkv", pairs[0]][step, :hd, :] = mm(pick("qt"), ds[...], NN).astype(BF)
         keys = jnp.concatenate([kv[:hd] for kv in kvs], axis=1)
-        dq[i] = (mm(keys, ds[...], NT) * (hd**-0.5)).astype(BF)
+        ref["dq", pairs[0]][step] = (mm(keys, ds[...], NT) * (hd**-0.5)).astype(BF)
         return 0
 
-    lax.fori_loop(0, 2, one_head, 0)
+    lax.fori_loop(0, 2 * len(pairs), one_head, 0)
 
 
 def joined(refs, cols):
@@ -498,7 +498,7 @@
 
 
 def inputs_step(row, parts, ref):
-    dkvs, dqs = [[ref[name, pair] for pair in range(parts // 2)] for name in ("dkv", "dq")]
+    dkvs, dqs = [[ref[k] for k in ref if k[0] == name] for name in ("dkv", "dq")]
     w_q, w_kv = ref["w_q"], ref["w_kv"]
     hd = w_q.shape[0] // parts
     here = dqs[0].shape[2]
@@ -513,14 +513,21 @@
             own = mm(joined(dqs, slice(0, here)), w_q[...], TN)
             ref["dx_own"][...] = dx + own + ref["dh1"][row]
         elif b % 2:
-            ref["dx_send"][b // 2] = dx.astype(BF)
+            if ("dx_send",) in ref:
+                ref["dx_send"][b // 2] = dx.astype(BF)
+            else:
+                ref["dx_same" if b == 1 else "dx_cross"][...] = dx.astype(BF)
         else:
             ref["dx_keep"][...] = dx
 
 
 def weights_step(row, heads, parts, ref):
-    dkvs = [ref["dkv", h // 2][h % 2] for h in heads]
-    dq = jnp.concatenate([ref["dq", h // 2][h % 2] for h in heads], axis=0)
+    all_dkv, all_dq = [
+        [ref[k].at[h] for k in sorted(k for k in ref if k[0] == name) for h in range(ref[k].shape[0])]
+        for name in ("dkv", "dq")
+    ]
+    dkvs = [all_dkv[h] for h in heads]
+    dq = jnp.concatenate([all_dq[h][...] for h in heads], axis=0)
     here = dq.shape[1]
     model = ref["x", 0].shape[1]
     hd = model // parts
@@ -549,15 +556,15 @@
 def backward_kernel(names, row, n, pairs, parts, want, some, *refs):
     ref = {name if len(name) > 1 else name[0]: r for name, r in zip(names, refs)}
     ref.update({name: r for name, r in zip(names, refs) if len(name) == 1})
-    for pair in pairs:
-        heads_step(row, n, pair, ref)
+    if pairs:
+        heads_step(row, n, pairs, ref)
     if "weights" in want:
         weights_step(row, some, parts, ref)
     if "inputs" in want:
         inputs_step(row, parts, ref)
 
 
-def backward(row, n, pairs, want, ins, some=(0, 1, 2, 3), kind=F32):
+def backward(row, n, pairs, want, ins, some=(0, 1, 2, 3), kind=F32, joint=False):
     parts = 4
     el = ins["el", 0]
     here, half = el.shape[2:]
@@ -570,18 +577,20 @@
     for pair in pairs:
         use |= {("el", pair), ("kvl", pair), ("qt", pair), ("er",), ("kvr",), ("do",), ("weight",)}
         scratch["ds",] = ((here, length), BF)
-    shapes = {"dkv": ((2, 2 * hd, length), BF), "dq": ((2, hd, here), BF)}
-    for pair in range(parts // 2):
-        for name, shape in shapes.items():
-            if pair in pairs:
-                (outs if len(want) < 2 else scratch)[name, pair] = shape
-            elif want:
-                use.add((name, pair))
+    if pairs:
+        outs["dkv", pairs[0]] = ((2 * len(pairs), 2 * hd, length), BF)
+        outs["dq", pairs[0]] = ((2 * len(pairs), hd, here), BF)
+    if want:
+        use |= {k for k in ins if k[0] in ("dkv", "dq")}
     if "inputs" in want:
         use |= {("w", b) for b in range(parts)} | {("dh1",)}
         outs["dx_own",] = ((here, model), F32)
         outs["dx_keep",] = ((here, model), F32)
-        outs["dx_send",] = ((parts // 2, here, model), BF)
+        if joint:
+            outs["dx_send",] = ((parts // 2, here, model), BF)
+        else:
+            outs["dx_same",] = ((here, model), BF)
+            outs["dx_cross",] = ((here, model), BF)
         scratch["w_kv",] = ((2 * model, model), BF)
         scratch["w_q",] = ((model, model), BF)
     if "weights" in want:
@@ -605,7 +614,7 @@
 def add_kernel(rows, *refs):
     owns, nears, fars, out = refs[:rows], refs[rows : 2 * rows], refs[2 * rows : -1], refs[-1]
     for r in range(rows):
-        out[r] = owns[r][...] + nears[r][0].astype(F32) + fars[r][...].astype(F32)
+        out[r] = owns[r][...] + nears[r][...].astype(F32) + fars[r][...].astype(F32)
 
 
 def add_inputs(owns, nears, fars):
@@ -764,7 +773,7 @@
             flag = ins["dkv", 0]
             if r > 1 or last:
                 far_got[-1] = after(far_got[-1], flag)
-        flag = ins["dkv", 1]
+        flag = ins["dkv", 1] if r == 0 else ins["dkv", 0]
         if steps_two is None:
             value_two = (keep_two[0] + got_two[0].astype(F32)).astype(BF).astype(F32)
             value_two = value_two + after(far_two, flag).astype(F32)
@@ -780,13 +789,13 @@
         if r:
             ins["dh1",] = after(ins["dh1",], *tie)
             ins.update(run(r, (), ("inputs",), ins))
-        got = near(ins["dx_send",] if r else after(ins["dx_send",], *tie))
+        got = near(ins["dx_cross",] if r else after(ins["dx_cross",], *tie))
         owns.append(ins["dx_own",])
-        ins["x", 0] = after(ins["x", 0], ins["dx_send",])
+        ins["x", 0] = after(ins["x", 0], ins["dx_cross",])
         grads = run(r, (), ("weights",), ins)["grads",]
         got = after(got, grads)
-        near_got.append(got)
-        other = (ins["dx_keep",] + got[1].astype(F32)).astype(BF)
+        near_got.append(near(after(ins["dx_same",], got)))
+        other = (ins["dx_keep",] + got.astype(F32)).astype(BF)
         far_got.append(far(other))
         ready = [other, step_two[0]]
     ins["x", 0] = after(ins["x", 0], *tie)
@@ -798,10 +807,10 @@
     other_one = (keep[1] + got[1].astype(F32)).astype(BF)
     far_one = far(other_one)
     ins["dh1",] = after(ins["dh1",], other_one)
-    row = run(r, (), ("inputs",), ins)
-    got = near(row["dx_send",])
+    row = run(r, (), ("inputs",), ins, joint=True)
+    got = near(after(row["dx_send",], other_one))
     owns.append(row["dx_own",])
-    near_got.append(got)
+    near_got.append(got[0])
     value_one = mine_one + far_one.astype(F32)
     total_one = None
     for k, total_one in enumerate(over_dp(value_one, bits, bits)):

time: 108 us -> 108 us (level); the launches traced: 108 us -> 107 us
  Pallas kernels: 64.6 us -> 62.9 us
    ppermute x6, waiting for transfers between devices: 5.68 us -> 3.98 us  [over_dp(): got = lax.ppermute(sent, ('dp', 'mp'), pairs)]
    pallas_call x19, Pallas kernels: 64.6 us -> 62.9 us  [call(): pl.pallas_call(kernel, out_shape=[jax.ShapeDtypeStruct(shape, kind) for s...]
    ppermute x19 -> x21, waiting for transfers between devices: 9.75 us -> 11.1 us  [swap(): return lax.ppermute(value, axis, [(i, i ^ bit) for i in range(size)])]
    ppermute x19 -> x21, starting transfers between devices: 15.9 us -> 16.7 us  [swap(): return lax.ppermute(value, axis, [(i, i ^ bit) for i in range(size)])]
  transfers between devices with their start and end apart: 25 -> 27, of which waited for: 16 -> 15; matrix products, arithmetic and copies ran while one was open for 0% -> 0% of each run, Pallas kernels for 47% -> 46%
where the time goes in v3:
time: 108 us; the launch traced here: 107 us
  Pallas kernels  62.9 us (58%)
  starting transfers between devices  27.6 us (26%)
  waiting for transfers between devices  15.1 us (14%)
    pallas_call x19, Pallas kernels, call(): pl.pallas_call(kernel, out_shape=[jax.ShapeDtypeStruct(shape, kind) for s...  62.9 us
    ppermute x21, starting transfers between devices, swap(): return lax.ppermute(value, axis, [(i, i ^ bit) for i in range(size)])  16.7 us
    ppermute x21, waiting for transfers between devices, swap(): return lax.ppermute(value, axis, [(i, i ^ bit) for i in range(size)])  11.1 us
    ppermute x6, starting transfers between devices, over_dp(): got = lax.ppermute(sent, ('dp', 'mp'), pairs)  10.9 us
    ppermute x6, waiting for transfers between devices, over_dp(): got = lax.ppermute(sent, ('dp', 'mp'), pairs)  3.98 us
  transfers between devices with their start and end apart: 27, of which 15 were waited for; matrix products, arithmetic and copies ran while one was open for 0% of the time, Pallas kernels for 46%

profile of v3, /device:TPU:0, one launch (start us, length us, event | category | flops | bytes accessed | tf_op | source)
XLA Modules:
  0.0 107.2 jit_solution(14963069920110932179)
XLA Ops:
  0.6 1.5 %pack.1 = (bf16[736,256]{1,0:T(8,128)(2,1)S(1)}, bf16[1056,256]{1,0:T(8,128)(2,1)S(1)}, bf16[336,256]{1,0:T(8,128)(2,1)S(1)}, f32[8,256]{1,0:T(8,128)S(1)}) custom-call(bf16[3,64,256]{2,1,0:T(8,128)(2,1)} %bitcast.37, bf16[2,64]{1,0:T(2,128)(2,1)} %refs_1_.1, bf16[64,256]{1,0:T(8,128)(2,1)} %refs_2_.1, bf16[256]{0:T(256)(128)(2,1)} %refs_3_.1, ...), custom_call_target="tpu_custom_call" | custom-call | tf_op jit(solution)/shard_map/pack/pallas_call | solution.py:35
  2.7 2.9 %collective-permute-start.2 = (bf16[736,256]{1,0:T(8,128)(2,1)S(1)}, bf16[736,256]{1,0:T(8,128)(2,1)S(1)}, u32[]{:S(2)}, u32[]{:S(2)}) collective-permute-start(bf16[736,256]{1,0:T(8,128)(2,1)S(1)} %get-tuple-element.138.refs_0_.refs_4_.refs_6_.refs_2_.refs_9_.refs_3_), channel_id=1, source_target_pairs={{0,2},{1,3},{2,0},{3,1},{4,6},{5,7},{6,4},{7,5},{8,10},{9,11},{10,... | collective-permute-start | bytes 1130504 | tf_op jit(solution)/shard_map/ppermute | solution.py:660
  5.6 2.0 %collective-permute-start.4 = (bf16[1056,256]{1,0:T(8,128)(2,1)S(1)}, bf16[1056,256]{1,0:T(8,128)(2,1)S(1)}, u32[]{:S(2)}, u32[]{:S(2)}) collective-permute-start(bf16[1056,256]{1,0:T(8,128)(2,1)S(1)} %get-tuple-element.157.refs_1_.refs_3_), channel_id=1, source_target_pairs={{0,2},{1,3},{2,0},{3,1},{4,6},{5,7},{6,4},{7,5},{8,10},{9,11},{10,... | collective-permute-start | bytes 1622024 | tf_op jit(solution)/shard_map/ppermute | solution.py:660
  7.6 4.8 %attend_local.2 = (bf16[3,2,512,1024]{3,2,1,0:T(8,128)(2,1)S(1)}, bf16[3,2,128,1024]{3,2,1,0:T(8,128)(2,1)S(1)}, bf16[3,2,64,512]{3,2,1,0:T(8,128)(2,1)S(1)}, bf...) custom-call(bf16[736,256]{1,0:T(8,128)(2,1)S(1)} %get-tuple-element.138.refs_0_.refs_4_.refs_6_.refs_2_.refs_9_.refs_3_, ...), custom_call_target="tpu_custom_call" | custom-call | tf_op jit(solution)/shard_map/attend_local/pallas_call | solution.py:35
  12.4 2.8 %collective-permute-done.2.refs_4_.refs_8_.refs_11_.refs_6_.refs_5_ = bf16[736,256]{1,0:T(8,128)(2,1)S(1)} collective-permute-done((bf16[736,256]{1,0:T(8,128)(2,1)S(1)}, bf16[736,256]{1,0:T(8,128)(2,1)S(1)}, u32[]{:S(2)}, u32[]{:S(2)}) %collective-permute-start.2) | collective-permute-done | bytes 376864 | tf_op jit(solution)/shard_map/ppermute | solution.py:660
  15.2 1.7 %collective-permute-done.3.refs_5_.refs_9_.refs_12_.refs_7_.refs_6_ = bf16[736,256]{1,0:T(8,128)(2,1)S(1)} collective-permute-done((bf16[736,256]{1,0:T(8,128)(2,1)S(1)}, bf16[736,256]{1,0:T(8,128)(2,1)S(1)}, u32[]{:S(2)}, u32[]{:S(2)}) %collective-permute-start.3) | collective-permute-done | bytes 376864 | tf_op jit(solution)/shard_map/ppermute | solution.py:660
  16.9 4.8 %attend_local.3 = (bf16[3,2,512,1024]{3,2,1,0:T(8,128)(2,1)S(1)}, bf16[3,2,128,1024]{3,2,1,0:T(8,128)(2,1)S(1)}, bf16[3,2,64,512]{3,2,1,0:T(8,128)(2,1)S(1)}, bf...) custom-call(bf16[736,256]{1,0:T(8,128)(2,1)S(1)} %get-tuple-element.138.refs_0_.refs_4_.refs_6_.refs_2_.refs_9_.refs_3_, ...), custom_call_target="tpu_custom_call" | custom-call | tf_op jit(solution)/shard_map/attend_local/pallas_call | solution.py:35
  21.7 3.6 %attend_remote.2 = (bf16[1,4,512,1024]{3,2,1,0:T(8,128)(2,1)S(1)}, bf16[1,4,128,1024]{3,2,1,0:T(8,128)(2,1)S(1)}, f32[1,4,512,128]{3,2,1,0:T(8,128)S(1)}, bf16[1,4,512,128]{3,2,1,0:T(8,128)(2,1)S(1)}) custom-call(bf16[3,2,512,128]{3,2,1,0:T(8,128)(2,1)S(1)} %get-tuple-element.100.refs_0_, bf16[3,2,512,128]{3,2,1,0:T(8,128)(2,1)S(1)} %get-tuple-element.103.refs_1_, ...), custom_call_target="tpu_custom_call" | custom-call | tf_op jit(solution)/shard_map/attend_remote/pallas_call | solution.py:35
  26.3 1.8 %collective-permute-start.7 = (bf16[336,256]{1,0:T(8,128)(2,1)S(1)}, bf16[336,256]{1,0:T(8,128)(2,1)S(1)}, u32[]{:S(2)}, u32[]{:S(2)}) collective-permute-start(bf16[336,256]{1,0:T(8,128)(2,1)S(1)} %get-tuple-element.111.refs_5_), channel_id=1, source_target_pairs={{0,2},{1,3},{2,0},{3,1},{4,6},{5,7},{6,4},{7,5},{8,10},{9,11},{10,... | collective-permute-start | bytes 516104 | tf_op jit(solution)/shard_map/ppermute | solution.py:660
  28.3 7.2 %attend_remote.3 = (bf16[2,4,512,1024]{3,2,1,0:T(8,128)(2,1)S(1)}, bf16[2,4,128,1024]{3,2,1,0:T(8,128)(2,1)S(1)}, f32[2,4,512,128]{3,2,1,0:T(8,128)S(1)}, bf16[2,4,512,128]{3,2,1,0:T(8,128)(2,1)S(1)}) custom-call(bf16[3,2,512,128]{3,2,1,0:T(8,128)(2,1)S(1)} %get-tuple-element.100.refs_0_, bf16[3,2,512,128]{3,2,1,0:T(8,128)(2,1)S(1)} %get-tuple-element.103.refs_1_, ...), custom_call_target="tpu_custom_call" | custom-call | tf_op jit(solution)/shard_map/attend_remote/pallas_call | solution.py:35
  37.0 9.5 %middle.1 = (bf16[3,512,256]{2,1,0:T(8,128)(2,1)}, f32[2,336,256]{2,1,0:T(8,128)S(1)}, bf16[2,336,256]{2,1,0:T(8,128)(2,1)S(1)}, f32[3,512,256]{2,1,0:T(8,128)S(1)}, bf16[3,4,512,128]{3,2,1,0:T(8,128)(2,1)S(1)}) custom-call(f32[1,4,512,128]{3,2,1,0:T(8,128)S(1)} %get-tuple-element.106.refs_0_, f32[2,4,512,128]{3,2,1,0:T(8,128)S(1)} %get-tuple-element.109.refs_1_, ...), custom_call_target="tpu_custom_call" | custom-call | flops 181193936 | tf_op jit(solution)/shard_map/middle/pallas_call | solution.py:35
  46.9 3.9 %backward.10 = (bf16[2,128,2048]{2,1,0:T(8,128)(2,1)S(1)}, bf16[2,64,512]{2,1,0:T(8,128)(2,1)S(1)}) custom-call(bf16[3,4,512,128]{3,2,1,0:T(8,128)(2,1)S(1)} %get-tuple-element.116.refs_0_.refs_2_, bf16[3,2,512,1024]{3,2,1,0:T(8,128)(2,1)S(1)} %get-tuple-element.117.refs_1_, bf16[1,4,512,1024]{3,2,1,0:T(8,128)(2,1)S(1)} %get-tuple-element.128.refs_2_.refs_5_, ...), custom_call_target="tpu_custom_call" | custom-call | tf_op jit(solution)/shard_map/backward/pallas_call | solution.py:35
  50.8 1.5 %collective-permute-start.10 = (bf16[336,256]{1,0:T(8,128)(2,1)S(1)}, bf16[336,256]{1,0:T(8,128)(2,1)S(1)}, u32[]{:S(2)}, u32[]{:S(2)}) collective-permute-start(bf16[336,256]{1,0:T(8,128)(2,1)S(1)} %fusion.5), channel_id=1, source_target_pairs={{0,2},{1,3},{2,0},{3,1},{4,6},{5,7},{6,4},{7,5},{8,10},{9,11},{10,... | collective-permute-start | bytes 516104 | tf_op jit(solution)/shard_map/ppermute | solution.py:660
  52.4 4.7 %backward.11 = (bf16[2,128,2048]{2,1,0:T(8,128)(2,1)S(1)}, bf16[2,64,512]{2,1,0:T(8,128)(2,1)S(1)}, f32[512,256]{1,0:T(8,128)S(1)}, f32[512,256]{1,0:T(8,128)S(1...) custom-call(f32[3,512,256]{2,1,0:T(8,128)S(1)} %get-tuple-element.158.refs_0_, ...), custom_call_target="tpu_custom_call" | custom-call | tf_op jit(solution)/shard_map/backward/pallas_call | solution.py:35
  59.1 1.7 %collective-permute-start.13 = (bf16[512,256]{1,0:T(8,128)(2,1)S(1)}, bf16[512,256]{1,0:T(8,128)(2,1)S(1)}, u32[]{:S(2)}, u32[]{:S(2)}) collective-permute-start(bf16[512,256]{1,0:T(8,128)(2,1)S(1)} %add_convert_fusion.2), channel_id=1, source_target_pairs={{0,2},{1,3},{2,0},{3,1},{4,6},{5,7},{6,4},{7,5},{8,10},{9,11},{10,... | collective-permute-start | bytes 786440 | tf_op jit(solution)/shard_map/ppermute | solution.py:660
  60.8 2.6 %collective-permute-start.11 = (bf16[336,256]{1,0:T(8,128)(2,1)S(1)}, bf16[336,256]{1,0:T(8,128)(2,1)S(1)}, u32[]{:S(2)}, u32[]{:S(2)}) collective-permute-start(bf16[336,256]{1,0:T(8,128)(2,1)S(1)} %fusion), channel_id=1, source_target_pairs={{0,16},{1,17},{2,18},{3,19},{4,20},{5,21},{6,22},{7,23},{8,24},{9,... | collective-permute-start | bytes 516104 | tf_op jit(solution)/shard_map/ppermute | solution.py:727
  63.4 7.9 %backward.13 = (bf16[4,128,2048]{2,1,0:T(8,128)(2,1)S(1)}, bf16[4,64,512]{2,1,0:T(8,128)(2,1)S(1)}) custom-call(bf16[3,4,512,128]{3,2,1,0:T(8,128)(2,1)S(1)} %get-tuple-element.116.refs_0_.refs_2_, bf16[3,2,512,1024]{3,2,1,0:T(8,128)(2,1)S(1)} %get-tuple-element.117.refs_1_, bf16[3,2,512,1024]{3,2,1,0:T(8,128)(2,1)S(1)} %get-tuple-element.124.refs_4_.refs_2_, ...), custom_call_target="tpu_custom_call" | custom-call | tf_op jit(solution)/shard_map/backward/pallas_call | solution.py:35
  74.6 7.9 %backward.16 = (bf16[4,128,2048]{2,1,0:T(8,128)(2,1)S(1)}, bf16[4,64,512]{2,1,0:T(8,128)(2,1)S(1)}) custom-call(bf16[3,4,512,128]{3,2,1,0:T(8,128)(2,1)S(1)} %get-tuple-element.116.refs_0_.refs_2_, bf16[3,2,512,1024]{3,2,1,0:T(8,128)(2,1)S(1)} %get-tuple-element.117.refs_1_, bf16[3,2,512,1024]{3,2,1,0:T(8,128)(2,1)S(1)} %get-tuple-element.124.refs_4_.refs_2_, ...), custom_call_target="tpu_custom_call" | custom-call | tf_op jit(solution)/shard_map/backward/pallas_call | solution.py:35
  84.6 1.6 %collective-permute-start.20 = (bf16[208,256]{1,0:T(8,128)(2,1)S(1)}, bf16[208,256]{1,0:T(8,128)(2,1)S(1)}, u32[]{:S(2)}, u32[]{:S(2)}) collective-permute-start(bf16[208,256]{1,0:T(8,128)(2,1)S(1)} %fusion.7), channel_id=1, source_target_pairs={{0,2},{1,3},{2,0},{3,1},{4,6},{5,7},{6,4},{7,5},{8,10},{9,11},{10,... | collective-permute-start | bytes 319496 | tf_op jit(solution)/shard_map/ppermute | solution.py:660
  89.7 1.6 %collective-permute-start.22 = (bf16[208,256]{1,0:T(8,128)(2,1)S(1)}, bf16[208,256]{1,0:T(8,128)(2,1)S(1)}, u32[]{:S(2)}, u32[]{:S(2)}) collective-permute-start(bf16[208,256]{1,0:T(8,128)(2,1)S(1)} %fusion.3), channel_id=1, source_target_pairs={{0,4},{1,5},{2,6},{3,7},{4,0},{5,1},{6,2},{7,3},{8,12},{9,13},{10,... | collective-permute-start | bytes 319496 | tf_op jit(solution)/shard_map/ppermute | solution.py:727
  92.5 1.6 %collective-permute-start.26 = (bf16[336,256]{1,0:T(8,128)(2,1)S(1)}, bf16[336,256]{1,0:T(8,128)(2,1)S(1)}, u32[]{:S(2)}, u32[]{:S(2)}) collective-permute-start(bf16[336,256]{1,0:T(8,128)(2,1)S(1)} %add_convert_fusion.3.a), channel_id=1, source_target_pairs={{0,4},{1,5},{2,6},{3,7},{4,0},{5,1},{6,2},{7,3},{8,12},{9,13},{10,... | collective-permute-start | bytes 516104 | tf_op jit(solution)/shard_map/ppermute | solution.py:727
  94.8 1.5 %collective-permute-start.23 = (bf16[208,256]{1,0:T(8,128)(2,1)S(1)}, bf16[208,256]{1,0:T(8,128)(2,1)S(1)}, u32[]{:S(2)}, u32[]{:S(2)}) collective-permute-start(bf16[208,256]{1,0:T(8,128)(2,1)S(1)} %add_convert_fusion.8), channel_id=1, source_target_pairs={{0,8},{1,9},{2,10},{3,11},{4,12},{5,13},{6,14},{7,15},{8,0},{9,1},... | collective-permute-start | bytes 319496 | tf_op jit(solution)/shard_map/ppermute | solution.py:727
  96.4 2.3 %collective-permute-start.21 = (bf16[512,256]{1,0:T(8,128)(2,1)S(1)}, bf16[512,256]{1,0:T(8,128)(2,1)S(1)}, u32[]{:S(2)}, u32[]{:S(2)}) collective-permute-start(bf16[512,256]{1,0:T(8,128)(2,1)S(1)} %add_convert_fusion), channel_id=1, source_target_pairs={{0,2},{1,3},{2,0},{3,1},{4,6},{5,7},{6,4},{7,5},{8,10},{9,11},{10,... | collective-permute-start | bytes 786440 | tf_op jit(solution)/shard_map/ppermute | solution.py:660
  99.6 2.3 %collective-permute-start.24 = (bf16[208,256]{1,0:T(8,128)(2,1)S(1)}, bf16[208,256]{1,0:T(8,128)(2,1)S(1)}, u32[]{:S(2)}, u32[]{:S(2)}) collective-permute-start(bf16[208,256]{1,0:T(8,128)(2,1)S(1)} %add_convert_fusion.7.a), channel_id=1, source_target_pairs={{0,16},{1,17},{2,18},{3,19},{4,20},{5,21},{6,22},{7,23},{8,24},{9,... | collective-permute-start | bytes 319496 | tf_op jit(solution)/shard_map/ppermute | solution.py:727
  (83 shorter events, 22.7 us)
Async XLA Ops:
  2.1 5.5 %collective-permute-start.1 = (bf16[1056,256]{1,0:T(8,128)(2,1)S(1)}, bf16[1056,256]{1,0:T(8,128)(2,1)S(1)}, u32[]{:S(2)}, u32[]{:S(2)}) collective-permute-start(bf16[1056,256]{1,0:T(8,128)(2,1)S(1)} %get-tuple-element.157.refs_1_.refs_3_), channel_id=1, source_target_pairs={{0,1},{1,0},{2,3},{3,2},{4,5},{5,4},{6,7},{7,6},{8,9},{9,8},{10,11... | collective-permute-start | bytes 1622024 | tf_op jit(solution)/shard_map/ppermute | solution.py:660
  2.6 3.0 %collective-permute-start = (bf16[736,256]{1,0:T(8,128)(2,1)S(1)}, bf16[736,256]{1,0:T(8,128)(2,1)S(1)}, u32[]{:S(2)}, u32[]{:S(2)}) collective-permute-start(bf16[736,256]{1,0:T(8,128)(2,1)S(1)} %get-tuple-element.138.refs_0_.refs_4_.refs_6_.refs_2_.refs_9_.refs_3_), channel_id=1, source_target_pairs={{0,1},{1,0},{2,3},{3,2},{4,5},{5,4},{6,7},{7,6},{8,9},{9,8},{10,11... | collective-permute-start | bytes 1130504 | tf_op jit(solution)/shard_map/ppermute | solution.py:660
  2.7 12.5 %collective-permute-start.2 = (bf16[736,256]{1,0:T(8,128)(2,1)S(1)}, bf16[736,256]{1,0:T(8,128)(2,1)S(1)}, u32[]{:S(2)}, u32[]{:S(2)}) collective-permute-start(bf16[736,256]{1,0:T(8,128)(2,1)S(1)} %get-tuple-element.138.refs_0_.refs_4_.refs_6_.refs_2_.refs_9_.refs_3_), channel_id=1, source_target_pairs={{0,2},{1,3},{2,0},{3,1},{4,6},{5,7},{6,4},{7,5},{8,10},{9,11},{10,... | collective-permute-start | bytes 1130504 | tf_op jit(solution)/shard_map/ppermute | solution.py:660
  5.6 20.6 %collective-permute-start.4 = (bf16[1056,256]{1,0:T(8,128)(2,1)S(1)}, bf16[1056,256]{1,0:T(8,128)(2,1)S(1)}, u32[]{:S(2)}, u32[]{:S(2)}) collective-permute-start(bf16[1056,256]{1,0:T(8,128)(2,1)S(1)} %get-tuple-element.157.refs_1_.refs_3_), channel_id=1, source_target_pairs={{0,2},{1,3},{2,0},{3,1},{4,6},{5,7},{6,4},{7,5},{8,10},{9,11},{10,... | collective-permute-start | bytes 1622024 | tf_op jit(solution)/shard_map/ppermute | solution.py:660
  15.2 1.7 %collective-permute-start.3 = (bf16[736,256]{1,0:T(8,128)(2,1)S(1)}, bf16[736,256]{1,0:T(8,128)(2,1)S(1)}, u32[]{:S(2)}, u32[]{:S(2)}) collective-permute-start(bf16[736,256]{1,0:T(8,128)(2,1)S(1)} %collective-permute-done.2.refs_4_.refs_8_.refs_11_.refs_6_.refs_5_), channel_id=1, source_target_pairs={{0,1},{1,0},{2,3},{3,2},{4,5},{5,4},{6,7},{7,6},{8,9},{9,8},{10,11... | collective-permute-start | bytes 1130504 | tf_op jit(solution)/shard_map/ppermute | solution.py:660
  26.2 2.1 %collective-permute-start.5 = (bf16[1056,256]{1,0:T(8,128)(2,1)S(1)}, bf16[1056,256]{1,0:T(8,128)(2,1)S(1)}, u32[]{:S(2)}, u32[]{:S(2)}) collective-permute-start(bf16[1056,256]{1,0:T(8,128)(2,1)S(1)} %collective-permute-done.4.refs_4_.refs_5_), channel_id=1, source_target_pairs={{0,1},{1,0},{2,3},{3,2},{4,5},{5,4},{6,7},{7,6},{8,9},{9,8},{10,11... | collective-permute-start | bytes 1622024 | tf_op jit(solution)/shard_map/ppermute | solution.py:660
  26.3 9.2 %collective-permute-start.7 = (bf16[336,256]{1,0:T(8,128)(2,1)S(1)}, bf16[336,256]{1,0:T(8,128)(2,1)S(1)}, u32[]{:S(2)}, u32[]{:S(2)}) collective-permute-start(bf16[336,256]{1,0:T(8,128)(2,1)S(1)} %get-tuple-element.111.refs_5_), channel_id=1, source_target_pairs={{0,2},{1,3},{2,0},{3,1},{4,6},{5,7},{6,4},{7,5},{8,10},{9,11},{10,... | collective-permute-start | bytes 516104 | tf_op jit(solution)/shard_map/ppermute | solution.py:660
  28.1 7.8 %collective-permute-start.6 = (bf16[336,256]{1,0:T(8,128)(2,1)S(1)}, bf16[336,256]{1,0:T(8,128)(2,1)S(1)}, u32[]{:S(2)}, u32[]{:S(2)}) collective-permute-start(bf16[336,256]{1,0:T(8,128)(2,1)S(1)} %get-tuple-element.111.refs_5_), channel_id=1, source_target_pairs={{0,1},{1,0},{2,3},{3,2},{4,5},{5,4},{6,7},{7,6},{8,9},{9,8},{10,11... | collective-permute-start | bytes 516104 | tf_op jit(solution)/shard_map/ppermute | solution.py:660
  46.5 4.2 %collective-permute-start.9 = (bf16[2,336,256]{2,1,0:T(8,128)(2,1)S(1)}, bf16[2,336,256]{2,1,0:T(8,128)(2,1)S(1)}, u32[]{:S(2)}, u32[]{:S(2)}) collective-permute-start(bf16[2,336,256]{2,1,0:T(8,128)(2,1)S(1)} %get-tuple-element.126), channel_id=1, source_target_pairs={{0,1},{1,0},{2,3},{3,2},{4,5},{5,4},{6,7},{7,6},{8,9},{9,8},{10,11... | collective-permute-start | bytes 1032200 | tf_op jit(solution)/shard_map/ppermute | solution.py:660
  50.8 6.6 %collective-permute-start.10 = (bf16[336,256]{1,0:T(8,128)(2,1)S(1)}, bf16[336,256]{1,0:T(8,128)(2,1)S(1)}, u32[]{:S(2)}, u32[]{:S(2)}) collective-permute-start(bf16[336,256]{1,0:T(8,128)(2,1)S(1)} %fusion.5), channel_id=1, source_target_pairs={{0,2},{1,3},{2,0},{3,1},{4,6},{5,7},{6,4},{7,5},{8,10},{9,11},{10,... | collective-permute-start | bytes 516104 | tf_op jit(solution)/shard_map/ppermute | solution.py:660
  57.5 1.6 %collective-permute-start.12 = (bf16[512,256]{1,0:T(8,128)(2,1)S(1)}, bf16[512,256]{1,0:T(8,128)(2,1)S(1)}, u32[]{:S(2)}, u32[]{:S(2)}) collective-permute-start(bf16[512,256]{1,0:T(8,128)(2,1)S(1)} %get-tuple-element.136), channel_id=1, source_target_pairs={{0,1},{1,0},{2,3},{3,2},{4,5},{5,4},{6,7},{7,6},{8,9},{9,8},{10,11... | collective-permute-start | bytes 786440 | tf_op jit(solution)/shard_map/ppermute | solution.py:660
  59.1 12.4 %collective-permute-start.13 = (bf16[512,256]{1,0:T(8,128)(2,1)S(1)}, bf16[512,256]{1,0:T(8,128)(2,1)S(1)}, u32[]{:S(2)}, u32[]{:S(2)}) collective-permute-start(bf16[512,256]{1,0:T(8,128)(2,1)S(1)} %add_convert_fusion.2), channel_id=1, source_target_pairs={{0,2},{1,3},{2,0},{3,1},{4,6},{5,7},{6,4},{7,5},{8,10},{9,11},{10,... | collective-permute-start | bytes 786440 | tf_op jit(solution)/shard_map/ppermute | solution.py:660
  60.8 10.7 %collective-permute-start.11 = (bf16[336,256]{1,0:T(8,128)(2,1)S(1)}, bf16[336,256]{1,0:T(8,128)(2,1)S(1)}, u32[]{:S(2)}, u32[]{:S(2)}) collective-permute-start(bf16[336,256]{1,0:T(8,128)(2,1)S(1)} %fusion), channel_id=1, source_target_pairs={{0,16},{1,17},{2,18},{3,19},{4,20},{5,21},{6,22},{7,23},{8,24},{9,... | collective-permute-start | bytes 516104 | tf_op jit(solution)/shard_map/ppermute | solution.py:727
  74.1 8.4 %collective-permute-start.15 = (bf16[512,256]{1,0:T(8,128)(2,1)S(1)}, bf16[512,256]{1,0:T(8,128)(2,1)S(1)}, u32[]{:S(2)}, u32[]{:S(2)}) collective-permute-start(bf16[512,256]{1,0:T(8,128)(2,1)S(1)} %add_convert_fusion.1), channel_id=1, source_target_pairs={{0,2},{1,3},{2,0},{3,1},{4,6},{5,7},{6,4},{7,5},{8,10},{9,11},{10,... | collective-permute-start | bytes 786440 | tf_op jit(solution)/shard_map/ppermute | solution.py:660
  84.6 5.1 %collective-permute-start.20 = (bf16[208,256]{1,0:T(8,128)(2,1)S(1)}, bf16[208,256]{1,0:T(8,128)(2,1)S(1)}, u32[]{:S(2)}, u32[]{:S(2)}) collective-permute-start(bf16[208,256]{1,0:T(8,128)(2,1)S(1)} %fusion.7), channel_id=1, source_target_pairs={{0,2},{1,3},{2,0},{3,1},{4,6},{5,7},{6,4},{7,5},{8,10},{9,11},{10,... | collective-permute-start | bytes 319496 | tf_op jit(solution)/shard_map/ppermute | solution.py:660
  86.2 6.2 %collective-permute-start.25 = (bf16[336,256]{1,0:T(8,128)(2,1)S(1)}, bf16[336,256]{1,0:T(8,128)(2,1)S(1)}, u32[]{:S(2)}, u32[]{:S(2)}) collective-permute-start(bf16[336,256]{1,0:T(8,128)(2,1)S(1)} %add_convert_fusion.4), channel_id=1, source_target_pairs={{0,8},{1,9},{2,10},{3,11},{4,12},{5,13},{6,14},{7,15},{8,0},{9,1},... | collective-permute-start | bytes 516104 | tf_op jit(solution)/shard_map/ppermute | solution.py:727
  87.6 15.1 %collective-permute-start.17 = (bf16[512,256]{1,0:T(8,128)(2,1)S(1)}, bf16[512,256]{1,0:T(8,128)(2,1)S(1)}, u32[]{:S(2)}, u32[]{:S(2)}) collective-permute-start(bf16[512,256]{1,0:T(8,128)(2,1)S(1)} %get-tuple-element.161), channel_id=1, source_target_pairs={{0,1},{1,0},{2,3},{3,2},{4,5},{5,4},{6,7},{7,6},{8,9},{9,8},{10,11... | collective-permute-start | bytes 786440 | tf_op jit(solution)/shard_map/ppermute | solution.py:660
  88.5 7.8 %collective-permute-start.19 = (bf16[2,512,256]{2,1,0:T(8,128)(2,1)S(1)}, bf16[2,512,256]{2,1,0:T(8,128)(2,1)S(1)}, u32[]{:S(2)}, u32[]{:S(2)}) collective-permute-start(bf16[2,512,256]{2,1,0:T(8,128)(2,1)S(1)} %get-tuple-element.165), channel_id=1, source_target_pairs={{0,1},{1,0},{2,3},{3,2},{4,5},{5,4},{6,7},{7,6},{8,9},{9,8},{10,11... | collective-permute-start | bytes 1572872 | tf_op jit(solution)/shard_map/ppermute | solution.py:660
  89.7 5.1 %collective-permute-start.22 = (bf16[208,256]{1,0:T(8,128)(2,1)S(1)}, bf16[208,256]{1,0:T(8,128)(2,1)S(1)}, u32[]{:S(2)}, u32[]{:S(2)}) collective-permute-start(bf16[208,256]{1,0:T(8,128)(2,1)S(1)} %fusion.3), channel_id=1, source_target_pairs={{0,4},{1,5},{2,6},{3,7},{4,0},{5,1},{6,2},{7,3},{8,12},{9,13},{10,... | collective-permute-start | bytes 319496 | tf_op jit(solution)/shard_map/ppermute | solution.py:727
  92.5 9.5 %collective-permute-start.26 = (bf16[336,256]{1,0:T(8,128)(2,1)S(1)}, bf16[336,256]{1,0:T(8,128)(2,1)S(1)}, u32[]{:S(2)}, u32[]{:S(2)}) collective-permute-start(bf16[336,256]{1,0:T(8,128)(2,1)S(1)} %add_convert_fusion.3.a), channel_id=1, source_target_pairs={{0,4},{1,5},{2,6},{3,7},{4,0},{5,1},{6,2},{7,3},{8,12},{9,13},{10,... | collective-permute-start | bytes 516104 | tf_op jit(solution)/shard_map/ppermute | solution.py:727
  94.1 8.7 %collective-permute-start.18 = (bf16[512,256]{1,0:T(8,128)(2,1)S(1)}, bf16[512,256]{1,0:T(8,128)(2,1)S(1)}, u32[]{:S(2)}, u32[]{:S(2)}) collective-permute-start(bf16[512,256]{1,0:T(8,128)(2,1)S(1)} %get-tuple-element.163), channel_id=1, source_target_pairs={{0,1},{1,0},{2,3},{3,2},{4,5},{5,4},{6,7},{7,6},{8,9},{9,8},{10,11... | collective-permute-start | bytes 786440 | tf_op jit(solution)/shard_map/ppermute | solution.py:660
  94.8 4.8 %collective-permute-start.23 = (bf16[208,256]{1,0:T(8,128)(2,1)S(1)}, bf16[208,256]{1,0:T(8,128)(2,1)S(1)}, u32[]{:S(2)}, u32[]{:S(2)}) collective-permute-start(bf16[208,256]{1,0:T(8,128)(2,1)S(1)} %add_convert_fusion.8), channel_id=1, source_target_pairs={{0,8},{1,9},{2,10},{3,11},{4,12},{5,13},{6,14},{7,15},{8,0},{9,1},... | collective-permute-start | bytes 319496 | tf_op jit(solution)/shard_map/ppermute | solution.py:727
  96.4 7.7 %collective-permute-start.21 = (bf16[512,256]{1,0:T(8,128)(2,1)S(1)}, bf16[512,256]{1,0:T(8,128)(2,1)S(1)}, u32[]{:S(2)}, u32[]{:S(2)}) collective-permute-start(bf16[512,256]{1,0:T(8,128)(2,1)S(1)} %add_convert_fusion), channel_id=1, source_target_pairs={{0,2},{1,3},{2,0},{3,1},{4,6},{5,7},{6,4},{7,5},{8,10},{9,11},{10,... | collective-permute-start | bytes 786440 | tf_op jit(solution)/shard_map/ppermute | solution.py:660
  99.6 6.8 %collective-permute-start.24 = (bf16[208,256]{1,0:T(8,128)(2,1)S(1)}, bf16[208,256]{1,0:T(8,128)(2,1)S(1)}, u32[]{:S(2)}, u32[]{:S(2)}) collective-permute-start(bf16[208,256]{1,0:T(8,128)(2,1)S(1)} %add_convert_fusion.7.a), channel_id=1, source_target_pairs={{0,16},{1,17},{2,18},{3,19},{4,20},{5,21},{6,22},{7,23},{8,24},{9,... | collective-permute-start | bytes 319496 | tf_op jit(solution)/shard_map/ppermute | solution.py:727
  (14 other events, 182.5 us)

commit v4 on v3

--- a/solution.py
+++ b/solution.py
@@ -42,6 +42,18 @@
         cost_estimate=pl.CostEstimate(flops=flops // 20, bytes_accessed=0, transcendentals=0),
         name=name,
     )(*args)
+
+
+def stacked(lines, width):
+    place = lax.broadcasted_iota(jnp.int32, (16, width), 0)
+    out = jnp.zeros((16, width), F32)
+    for k, line in enumerate(lines):
+        line = line.astype(F32)
+        if line.shape[1] < width:
+            fill = jnp.zeros((1, width - line.shape[1]), F32)
+            line = jnp.concatenate([line, fill], axis=1)
+        out = jnp.where(place == k, jnp.broadcast_to(line, (16, width)), out)
+    return out
 
 
 def pack_kernel(rows, *refs):
@@ -59,20 +71,17 @@
         at = (r - 1) * (here + 16) if r else 0
         out[at : at + here, :] = x[r]
         at += here
-        out[at : at + 16, :] = jnp.zeros((16, model), BF)
         seg = segs[r : r + 1, :]
-        for digit in (jnp.bitwise_and(seg, 31), jnp.right_shift(seg, 5)):
-            digit = digit.astype(F32).astype(BF)
-            for start in range(0, here, model):
-                out[at : at + 1, :] = digit[:, start : start + model]
-                at += 1
+        digits = [jnp.bitwise_and(seg, 31), jnp.right_shift(seg, 5)]
+        lines = [d[:, k : k + model] for d in digits for k in range(0, here, model)]
+        out[at : at + 16, :] = stacked(lines, model).astype(BF)
     at = here + 16
     for c in range(3):
         first[at : at + width, :] = w_qkv[c]
         at += width
-    first[at : at + 16, :] = jnp.zeros((16, model), BF)
-    first[at : at + 1, 0:width] = b_qv[0:1, :]
-    first[at : at + 1, width : 2 * width] = b_qv[1:2, :]
+    both = b_qv[...].astype(F32)
+    line = jnp.concatenate([both[0:1], both[1:2]], axis=1)
+    first[at : at + 16, :] = stacked([line], model).astype(BF)
     two[0:width, :] = w_out[...]
     at = width
     two[at : at + half, 0:units] = w_in[0:half, :]
@@ -80,8 +89,7 @@
     at += half
     two[at : at + units, :] = w_back[...]
     at += units
-    two[at : at + 16, :] = jnp.zeros((16, model), BF)
-    two[at : at + 1, 0:units] = b_in[...]
+    two[at : at + 16, :] = stacked([b_in[...]], model).astype(BF)
 
 
 def pack(w_qkv, b_qv, w_out, b_out, w_in, b_in, w_back, b_back, segments, inputs):
@@ -116,14 +124,15 @@
     for i, w in enumerate(ws):
         w_q[i * hd : (i + 1) * hd, :] = w[at : at + hd, :]
         w_kv[i * 2 * hd : (i + 1) * 2 * hd, :] = w[at + hd : at + 3 * hd, :]
-        line = w[at + 3 * hd : at + 3 * hd + 1, 0 : 2 * hd].astype(F32)
+        line = w[at + 3 * hd : at + 3 * hd + 16, 0 : 2 * hd].astype(F32)[0:1]
         bias[i] = jnp.broadcast_to(line, (2 * hd, 2 * hd)).T
 
 
 def same_cell(x, at, here, hd):
     per = here // x.shape[1]
-    low = [x[at + i : at + i + 1, :].astype(F32) for i in range(per)]
-    high = [x[at + per + i : at + per + i + 1, :].astype(F32) for i in range(per)]
+    block = x[at : at + 16, :].astype(F32)
+    low = [block[i : i + 1] for i in range(per)]
+    high = [block[per + i : per + i + 1] for i in range(per)]
     low, high = jnp.concatenate(low, axis=1), jnp.concatenate(high, axis=1)
     lane = lax.broadcasted_iota(jnp.int32, (hd, here), 0).astype(F32)
     return lane == jnp.where(lane < 32, low, high + 32.0)
@@ -324,7 +333,7 @@
         at += half_model
         w_back[b * units : (b + 1) * units, :] = ws[b][at : at + units, :]
         at += units
-        bias.append(ws[b][at : at + 1, 0:units].astype(F32))
+        bias.append(ws[b][at : at + 16, 0:units].astype(F32)[0:1])
     b_in = jnp.concatenate(bias, axis=1)
     lane = lax.broadcasted_iota(jnp.int32, (here, 2 * hd), 1)
 
@@ -421,11 +430,9 @@
         at += half_model
         out[c, at : at + units, :] = dw_back[b * units : (b + 1) * units, :].astype(kind)
         at += units
-        out[c, at:, :] = jnp.zeros((16, model), kind)
-        out[c, at : at + 1, 0:units] = db_in[:, cols].astype(kind)
-        out[c, at + 1 : at + 7, :] = sums[0:6, :].astype(BF).astype(kind)
-        line = db_values[:, 2 * per * b : 2 * per * b + per]
-        out[c, at + 7 : at + 8, 0:per] = line.astype(kind)
+        lines = [db_in[:, cols]] + [sums[k : k + 1, :].astype(BF) for k in range(6)]
+        lines.append(db_values[:, 2 * per * b : 2 * per * b + per])
+        out[c, at : at + 16, :] = stacked(lines, model).astype(kind)
 
 
 def middle(os, xs, cotangent, ws, vectors, heads):
@@ -542,15 +549,14 @@
     out = ref["grads",]
     for c, h in enumerate(heads):
         pieces = [
-            (slice(0, hd), slice(0, model), gq[c * hd : (c + 1) * hd]),
-            (slice(hd, 3 * hd), slice(0, model), gkv[c * 2 * hd : (c + 1) * 2 * hd]),
-            (slice(3 * hd, 3 * hd + 1), slice(0, hd), bq[:, c * hd : (c + 1) * hd]),
+            (slice(0, hd), gq[c * hd : (c + 1) * hd]),
+            (slice(hd, 3 * hd), gkv[c * 2 * hd : (c + 1) * 2 * hd]),
+            (slice(3 * hd, 3 * hd + 16), stacked([bq[:, c * hd : (c + 1) * hd]], model)),
         ]
-        out[c, 3 * hd :, :] = jnp.zeros((16, model), out.dtype)
-        for rows, cols, value in pieces:
+        for rows, value in pieces:
             if ("grads_in",) in ref:
-                value = value + ref["grads_in",][h, rows, cols]
-            out[c, rows, cols] = value.astype(out.dtype)
+                value = value + ref["grads_in",][h, rows, :]
+            out[c, rows, :] = value.astype(out.dtype)
 
 
 def backward_kernel(names, row, n, pairs, parts, want, some, *refs):

time: 108 us -> 108 us (level)
  no operation moved by 1% of the time
where the time goes in v4:
time: 108 us; the launch traced here: 107 us
  Pallas kernels  63.1 us (58%)
  starting transfers between devices  27.6 us (26%)
  waiting for transfers between devices  15 us (14%)
    pallas_call x19, Pallas kernels, call(): pl.pallas_call(kernel, out_shape=[jax.ShapeDtypeStruct(shape, kind) for s...  63.1 us
    ppermute x21, starting transfers between devices, swap(): return lax.ppermute(value, axis, [(i, i ^ bit) for i in range(size)])  16.6 us
    ppermute x21, waiting for transfers between devices, swap(): return lax.ppermute(value, axis, [(i, i ^ bit) for i in range(size)])  11.1 us
    ppermute x6, starting transfers between devices, over_dp(): got = lax.ppermute(sent, ('dp', 'mp'), pairs)  11 us
    ppermute x6, waiting for transfers between devices, over_dp(): got = lax.ppermute(sent, ('dp', 'mp'), pairs)  3.9 us
  transfers between devices with their start and end apart: 27, of which 15 were waited for; matrix products, arithmetic and copies ran while one was open for 0% of the time, Pallas kernels for 46%

profile of v4, /device:TPU:0, one launch (start us, length us, event | category | flops | bytes accessed | tf_op | source)
XLA Modules:
  0.0 107.2 jit_solution(15527725638520986210)
XLA Ops:
  0.6 1.5 %pack.1 = (bf16[736,256]{1,0:T(8,128)(2,1)S(1)}, bf16[1056,256]{1,0:T(8,128)(2,1)S(1)}, bf16[336,256]{1,0:T(8,128)(2,1)S(1)}, f32[8,256]{1,0:T(8,128)S(1)}) custom-call(bf16[3,64,256]{2,1,0:T(8,128)(2,1)} %bitcast.37, bf16[2,64]{1,0:T(2,128)(2,1)} %refs_1_.1, bf16[64,256]{1,0:T(8,128)(2,1)} %refs_2_.1, bf16[256]{0:T(256)(128)(2,1)} %refs_3_.1, ...), custom_call_target="tpu_custom_call" | custom-call | tf_op jit(solution)/shard_map/pack/pallas_call | solution.py:35
  2.7 2.9 %collective-permute-start.2 = (bf16[736,256]{1,0:T(8,128)(2,1)S(1)}, bf16[736,256]{1,0:T(8,128)(2,1)S(1)}, u32[]{:S(2)}, u32[]{:S(2)}) collective-permute-start(bf16[736,256]{1,0:T(8,128)(2,1)S(1)} %get-tuple-element.138.refs_0_.refs_4_.refs_6_.refs_2_.refs_9_.refs_3_), channel_id=1, source_target_pairs={{0,2},{1,3},{2,0},{3,1},{4,6},{5,7},{6,4},{7,5},{8,10},{9,11},{10,... | collective-permute-start | bytes 1130504 | tf_op jit(solution)/shard_map/ppermute | solution.py:666
  5.6 2.0 %collective-permute-start.4 = (bf16[1056,256]{1,0:T(8,128)(2,1)S(1)}, bf16[1056,256]{1,0:T(8,128)(2,1)S(1)}, u32[]{:S(2)}, u32[]{:S(2)}) collective-permute-start(bf16[1056,256]{1,0:T(8,128)(2,1)S(1)} %get-tuple-element.157.refs_1_.refs_3_), channel_id=1, source_target_pairs={{0,2},{1,3},{2,0},{3,1},{4,6},{5,7},{6,4},{7,5},{8,10},{9,11},{10,... | collective-permute-start | bytes 1622024 | tf_op jit(solution)/shard_map/ppermute | solution.py:666
  7.6 4.8 %attend_local.2 = (bf16[3,2,512,1024]{3,2,1,0:T(8,128)(2,1)S(1)}, bf16[3,2,128,1024]{3,2,1,0:T(8,128)(2,1)S(1)}, bf16[3,2,64,512]{3,2,1,0:T(8,128)(2,1)S(1)}, bf...) custom-call(bf16[736,256]{1,0:T(8,128)(2,1)S(1)} %get-tuple-element.138.refs_0_.refs_4_.refs_6_.refs_2_.refs_9_.refs_3_, ...), custom_call_target="tpu_custom_call" | custom-call | tf_op jit(solution)/shard_map/attend_local/pallas_call | solution.py:35
  12.4 2.8 %collective-permute-done.2.refs_4_.refs_8_.refs_11_.refs_6_.refs_5_ = bf16[736,256]{1,0:T(8,128)(2,1)S(1)} collective-permute-done((bf16[736,256]{1,0:T(8,128)(2,1)S(1)}, bf16[736,256]{1,0:T(8,128)(2,1)S(1)}, u32[]{:S(2)}, u32[]{:S(2)}) %collective-permute-start.2) | collective-permute-done | bytes 376864 | tf_op jit(solution)/shard_map/ppermute | solution.py:666
  15.2 1.7 %collective-permute-done.3.refs_5_.refs_9_.refs_12_.refs_7_.refs_6_ = bf16[736,256]{1,0:T(8,128)(2,1)S(1)} collective-permute-done((bf16[736,256]{1,0:T(8,128)(2,1)S(1)}, bf16[736,256]{1,0:T(8,128)(2,1)S(1)}, u32[]{:S(2)}, u32[]{:S(2)}) %collective-permute-start.3) | collective-permute-done | bytes 376864 | tf_op jit(solution)/shard_map/ppermute | solution.py:666
  16.9 4.8 %attend_local.3 = (bf16[3,2,512,1024]{3,2,1,0:T(8,128)(2,1)S(1)}, bf16[3,2,128,1024]{3,2,1,0:T(8,128)(2,1)S(1)}, bf16[3,2,64,512]{3,2,1,0:T(8,128)(2,1)S(1)}, bf...) custom-call(bf16[736,256]{1,0:T(8,128)(2,1)S(1)} %get-tuple-element.138.refs_0_.refs_4_.refs_6_.refs_2_.refs_9_.refs_3_, ...), custom_call_target="tpu_custom_call" | custom-call | tf_op jit(solution)/shard_map/attend_local/pallas_call | solution.py:35
  21.6 3.6 %attend_remote.2 = (bf16[1,4,512,1024]{3,2,1,0:T(8,128)(2,1)S(1)}, bf16[1,4,128,1024]{3,2,1,0:T(8,128)(2,1)S(1)}, f32[1,4,512,128]{3,2,1,0:T(8,128)S(1)}, bf16[1,4,512,128]{3,2,1,0:T(8,128)(2,1)S(1)}) custom-call(bf16[3,2,512,128]{3,2,1,0:T(8,128)(2,1)S(1)} %get-tuple-element.100.refs_0_, bf16[3,2,512,128]{3,2,1,0:T(8,128)(2,1)S(1)} %get-tuple-element.103.refs_1_, ...), custom_call_target="tpu_custom_call" | custom-call | tf_op jit(solution)/shard_map/attend_remote/pallas_call | solution.py:35
  26.3 1.8 %collective-permute-start.7 = (bf16[336,256]{1,0:T(8,128)(2,1)S(1)}, bf16[336,256]{1,0:T(8,128)(2,1)S(1)}, u32[]{:S(2)}, u32[]{:S(2)}) collective-permute-start(bf16[336,256]{1,0:T(8,128)(2,1)S(1)} %get-tuple-element.111.refs_5_), channel_id=1, source_target_pairs={{0,2},{1,3},{2,0},{3,1},{4,6},{5,7},{6,4},{7,5},{8,10},{9,11},{10,... | collective-permute-start | bytes 516104 | tf_op jit(solution)/shard_map/ppermute | solution.py:666
  28.3 7.2 %attend_remote.3 = (bf16[2,4,512,1024]{3,2,1,0:T(8,128)(2,1)S(1)}, bf16[2,4,128,1024]{3,2,1,0:T(8,128)(2,1)S(1)}, f32[2,4,512,128]{3,2,1,0:T(8,128)S(1)}, bf16[2,4,512,128]{3,2,1,0:T(8,128)(2,1)S(1)}) custom-call(bf16[3,2,512,128]{3,2,1,0:T(8,128)(2,1)S(1)} %get-tuple-element.100.refs_0_, bf16[3,2,512,128]{3,2,1,0:T(8,128)(2,1)S(1)} %get-tuple-element.103.refs_1_, ...), custom_call_target="tpu_custom_call" | custom-call | tf_op jit(solution)/shard_map/attend_remote/pallas_call | solution.py:35
  37.0 9.7 %middle.1 = (bf16[3,512,256]{2,1,0:T(8,128)(2,1)}, f32[2,336,256]{2,1,0:T(8,128)S(1)}, bf16[2,336,256]{2,1,0:T(8,128)(2,1)S(1)}, f32[3,512,256]{2,1,0:T(8,128)S(1)}, bf16[3,4,512,128]{3,2,1,0:T(8,128)(2,1)S(1)}) custom-call(f32[1,4,512,128]{3,2,1,0:T(8,128)S(1)} %get-tuple-element.106.refs_0_, f32[2,4,512,128]{3,2,1,0:T(8,128)S(1)} %get-tuple-element.109.refs_1_, ...), custom_call_target="tpu_custom_call" | custom-call | flops 181193936 | tf_op jit(solution)/shard_map/middle/pallas_call | solution.py:35
  47.0 3.9 %backward.10 = (bf16[2,128,2048]{2,1,0:T(8,128)(2,1)S(1)}, bf16[2,64,512]{2,1,0:T(8,128)(2,1)S(1)}) custom-call(bf16[3,4,512,128]{3,2,1,0:T(8,128)(2,1)S(1)} %get-tuple-element.116.refs_0_.refs_2_, bf16[3,2,512,1024]{3,2,1,0:T(8,128)(2,1)S(1)} %get-tuple-element.117.refs_1_, bf16[1,4,512,1024]{3,2,1,0:T(8,128)(2,1)S(1)} %get-tuple-element.128.refs_2_.refs_5_, ...), custom_call_target="tpu_custom_call" | custom-call | tf_op jit(solution)/shard_map/backward/pallas_call | solution.py:35
  50.9 1.5 %collective-permute-start.10 = (bf16[336,256]{1,0:T(8,128)(2,1)S(1)}, bf16[336,256]{1,0:T(8,128)(2,1)S(1)}, u32[]{:S(2)}, u32[]{:S(2)}) collective-permute-start(bf16[336,256]{1,0:T(8,128)(2,1)S(1)} %fusion.5), channel_id=1, source_target_pairs={{0,2},{1,3},{2,0},{3,1},{4,6},{5,7},{6,4},{7,5},{8,10},{9,11},{10,... | collective-permute-start | bytes 516104 | tf_op jit(solution)/shard_map/ppermute | solution.py:666
  52.4 4.7 %backward.11 = (bf16[2,128,2048]{2,1,0:T(8,128)(2,1)S(1)}, bf16[2,64,512]{2,1,0:T(8,128)(2,1)S(1)}, f32[512,256]{1,0:T(8,128)S(1)}, f32[512,256]{1,0:T(8,128)S(1...) custom-call(f32[3,512,256]{2,1,0:T(8,128)S(1)} %get-tuple-element.158.refs_0_, ...), custom_call_target="tpu_custom_call" | custom-call | tf_op jit(solution)/shard_map/backward/pallas_call | solution.py:35
  59.2 1.7 %collective-permute-start.13 = (bf16[512,256]{1,0:T(8,128)(2,1)S(1)}, bf16[512,256]{1,0:T(8,128)(2,1)S(1)}, u32[]{:S(2)}, u32[]{:S(2)}) collective-permute-start(bf16[512,256]{1,0:T(8,128)(2,1)S(1)} %add_convert_fusion.2), channel_id=1, source_target_pairs={{0,2},{1,3},{2,0},{3,1},{4,6},{5,7},{6,4},{7,5},{8,10},{9,11},{10,... | collective-permute-start | bytes 786440 | tf_op jit(solution)/shard_map/ppermute | solution.py:666
  60.9 2.6 %collective-permute-start.11 = (bf16[336,256]{1,0:T(8,128)(2,1)S(1)}, bf16[336,256]{1,0:T(8,128)(2,1)S(1)}, u32[]{:S(2)}, u32[]{:S(2)}) collective-permute-start(bf16[336,256]{1,0:T(8,128)(2,1)S(1)} %fusion), channel_id=1, source_target_pairs={{0,16},{1,17},{2,18},{3,19},{4,20},{5,21},{6,22},{7,23},{8,24},{9,... | collective-permute-start | bytes 516104 | tf_op jit(solution)/shard_map/ppermute | solution.py:733
  63.5 7.9 %backward.13 = (bf16[4,128,2048]{2,1,0:T(8,128)(2,1)S(1)}, bf16[4,64,512]{2,1,0:T(8,128)(2,1)S(1)}) custom-call(bf16[3,4,512,128]{3,2,1,0:T(8,128)(2,1)S(1)} %get-tuple-element.116.refs_0_.refs_2_, bf16[3,2,512,1024]{3,2,1,0:T(8,128)(2,1)S(1)} %get-tuple-element.117.refs_1_, bf16[3,2,512,1024]{3,2,1,0:T(8,128)(2,1)S(1)} %get-tuple-element.124.refs_4_.refs_2_, ...), custom_call_target="tpu_custom_call" | custom-call | tf_op jit(solution)/shard_map/backward/pallas_call | solution.py:35
  74.7 7.9 %backward.16 = (bf16[4,128,2048]{2,1,0:T(8,128)(2,1)S(1)}, bf16[4,64,512]{2,1,0:T(8,128)(2,1)S(1)}) custom-call(bf16[3,4,512,128]{3,2,1,0:T(8,128)(2,1)S(1)} %get-tuple-element.116.refs_0_.refs_2_, bf16[3,2,512,1024]{3,2,1,0:T(8,128)(2,1)S(1)} %get-tuple-element.117.refs_1_, bf16[3,2,512,1024]{3,2,1,0:T(8,128)(2,1)S(1)} %get-tuple-element.124.refs_4_.refs_2_, ...), custom_call_target="tpu_custom_call" | custom-call | tf_op jit(solution)/shard_map/backward/pallas_call | solution.py:35
  84.6 1.6 %collective-permute-start.20 = (bf16[208,256]{1,0:T(8,128)(2,1)S(1)}, bf16[208,256]{1,0:T(8,128)(2,1)S(1)}, u32[]{:S(2)}, u32[]{:S(2)}) collective-permute-start(bf16[208,256]{1,0:T(8,128)(2,1)S(1)} %fusion.7), channel_id=1, source_target_pairs={{0,2},{1,3},{2,0},{3,1},{4,6},{5,7},{6,4},{7,5},{8,10},{9,11},{10,... | collective-permute-start | bytes 319496 | tf_op jit(solution)/shard_map/ppermute | solution.py:666
  89.8 1.6 %collective-permute-start.22 = (bf16[208,256]{1,0:T(8,128)(2,1)S(1)}, bf16[208,256]{1,0:T(8,128)(2,1)S(1)}, u32[]{:S(2)}, u32[]{:S(2)}) collective-permute-start(bf16[208,256]{1,0:T(8,128)(2,1)S(1)} %fusion.3), channel_id=1, source_target_pairs={{0,4},{1,5},{2,6},{3,7},{4,0},{5,1},{6,2},{7,3},{8,12},{9,13},{10,... | collective-permute-start | bytes 319496 | tf_op jit(solution)/shard_map/ppermute | solution.py:733
  92.6 1.6 %collective-permute-start.26 = (bf16[336,256]{1,0:T(8,128)(2,1)S(1)}, bf16[336,256]{1,0:T(8,128)(2,1)S(1)}, u32[]{:S(2)}, u32[]{:S(2)}) collective-permute-start(bf16[336,256]{1,0:T(8,128)(2,1)S(1)} %add_convert_fusion.3.a), channel_id=1, source_target_pairs={{0,4},{1,5},{2,6},{3,7},{4,0},{5,1},{6,2},{7,3},{8,12},{9,13},{10,... | collective-permute-start | bytes 516104 | tf_op jit(solution)/shard_map/ppermute | solution.py:733
  94.9 1.5 %collective-permute-start.23 = (bf16[208,256]{1,0:T(8,128)(2,1)S(1)}, bf16[208,256]{1,0:T(8,128)(2,1)S(1)}, u32[]{:S(2)}, u32[]{:S(2)}) collective-permute-start(bf16[208,256]{1,0:T(8,128)(2,1)S(1)} %add_convert_fusion.8), channel_id=1, source_target_pairs={{0,8},{1,9},{2,10},{3,11},{4,12},{5,13},{6,14},{7,15},{8,0},{9,1},... | collective-permute-start | bytes 319496 | tf_op jit(solution)/shard_map/ppermute | solution.py:733
  96.5 2.3 %collective-permute-start.21 = (bf16[512,256]{1,0:T(8,128)(2,1)S(1)}, bf16[512,256]{1,0:T(8,128)(2,1)S(1)}, u32[]{:S(2)}, u32[]{:S(2)}) collective-permute-start(bf16[512,256]{1,0:T(8,128)(2,1)S(1)} %add_convert_fusion), channel_id=1, source_target_pairs={{0,2},{1,3},{2,0},{3,1},{4,6},{5,7},{6,4},{7,5},{8,10},{9,11},{10,... | collective-permute-start | bytes 786440 | tf_op jit(solution)/shard_map/ppermute | solution.py:666
  99.7 2.3 %collective-permute-start.24 = (bf16[208,256]{1,0:T(8,128)(2,1)S(1)}, bf16[208,256]{1,0:T(8,128)(2,1)S(1)}, u32[]{:S(2)}, u32[]{:S(2)}) collective-permute-start(bf16[208,256]{1,0:T(8,128)(2,1)S(1)} %add_convert_fusion.7.a), channel_id=1, source_target_pairs={{0,16},{1,17},{2,18},{3,19},{4,20},{5,21},{6,22},{7,23},{8,24},{9,... | collective-permute-start | bytes 319496 | tf_op jit(solution)/shard_map/ppermute | solution.py:733
  (83 shorter events, 22.6 us)
Async XLA Ops:
  2.1 5.5 %collective-permute-start.1 = (bf16[1056,256]{1,0:T(8,128)(2,1)S(1)}, bf16[1056,256]{1,0:T(8,128)(2,1)S(1)}, u32[]{:S(2)}, u32[]{:S(2)}) collective-permute-start(bf16[1056,256]{1,0:T(8,128)(2,1)S(1)} %get-tuple-element.157.refs_1_.refs_3_), channel_id=1, source_target_pairs={{0,1},{1,0},{2,3},{3,2},{4,5},{5,4},{6,7},{7,6},{8,9},{9,8},{10,11... | collective-permute-start | bytes 1622024 | tf_op jit(solution)/shard_map/ppermute | solution.py:666
  2.6 3.0 %collective-permute-start = (bf16[736,256]{1,0:T(8,128)(2,1)S(1)}, bf16[736,256]{1,0:T(8,128)(2,1)S(1)}, u32[]{:S(2)}, u32[]{:S(2)}) collective-permute-start(bf16[736,256]{1,0:T(8,128)(2,1)S(1)} %get-tuple-element.138.refs_0_.refs_4_.refs_6_.refs_2_.refs_9_.refs_3_), channel_id=1, source_target_pairs={{0,1},{1,0},{2,3},{3,2},{4,5},{5,4},{6,7},{7,6},{8,9},{9,8},{10,11... | collective-permute-start | bytes 1130504 | tf_op jit(solution)/shard_map/ppermute | solution.py:666
  2.7 12.5 %collective-permute-start.2 = (bf16[736,256]{1,0:T(8,128)(2,1)S(1)}, bf16[736,256]{1,0:T(8,128)(2,1)S(1)}, u32[]{:S(2)}, u32[]{:S(2)}) collective-permute-start(bf16[736,256]{1,0:T(8,128)(2,1)S(1)} %get-tuple-element.138.refs_0_.refs_4_.refs_6_.refs_2_.refs_9_.refs_3_), channel_id=1, source_target_pairs={{0,2},{1,3},{2,0},{3,1},{4,6},{5,7},{6,4},{7,5},{8,10},{9,11},{10,... | collective-permute-start | bytes 1130504 | tf_op jit(solution)/shard_map/ppermute | solution.py:666
  5.6 20.6 %collective-permute-start.4 = (bf16[1056,256]{1,0:T(8,128)(2,1)S(1)}, bf16[1056,256]{1,0:T(8,128)(2,1)S(1)}, u32[]{:S(2)}, u32[]{:S(2)}) collective-permute-start(bf16[1056,256]{1,0:T(8,128)(2,1)S(1)} %get-tuple-element.157.refs_1_.refs_3_), channel_id=1, source_target_pairs={{0,2},{1,3},{2,0},{3,1},{4,6},{5,7},{6,4},{7,5},{8,10},{9,11},{10,... | collective-permute-start | bytes 1622024 | tf_op jit(solution)/shard_map/ppermute | solution.py:666
  15.2 1.7 %collective-permute-start.3 = (bf16[736,256]{1,0:T(8,128)(2,1)S(1)}, bf16[736,256]{1,0:T(8,128)(2,1)S(1)}, u32[]{:S(2)}, u32[]{:S(2)}) collective-permute-start(bf16[736,256]{1,0:T(8,128)(2,1)S(1)} %collective-permute-done.2.refs_4_.refs_8_.refs_11_.refs_6_.refs_5_), channel_id=1, source_target_pairs={{0,1},{1,0},{2,3},{3,2},{4,5},{5,4},{6,7},{7,6},{8,9},{9,8},{10,11... | collective-permute-start | bytes 1130504 | tf_op jit(solution)/shard_map/ppermute | solution.py:666
  26.2 2.1 %collective-permute-start.5 = (bf16[1056,256]{1,0:T(8,128)(2,1)S(1)}, bf16[1056,256]{1,0:T(8,128)(2,1)S(1)}, u32[]{:S(2)}, u32[]{:S(2)}) collective-permute-start(bf16[1056,256]{1,0:T(8,128)(2,1)S(1)} %collective-permute-done.4.refs_4_.refs_5_), channel_id=1, source_target_pairs={{0,1},{1,0},{2,3},{3,2},{4,5},{5,4},{6,7},{7,6},{8,9},{9,8},{10,11... | collective-permute-start | bytes 1622024 | tf_op jit(solution)/shard_map/ppermute | solution.py:666
  26.3 9.2 %collective-permute-start.7 = (bf16[336,256]{1,0:T(8,128)(2,1)S(1)}, bf16[336,256]{1,0:T(8,128)(2,1)S(1)}, u32[]{:S(2)}, u32[]{:S(2)}) collective-permute-start(bf16[336,256]{1,0:T(8,128)(2,1)S(1)} %get-tuple-element.111.refs_5_), channel_id=1, source_target_pairs={{0,2},{1,3},{2,0},{3,1},{4,6},{5,7},{6,4},{7,5},{8,10},{9,11},{10,... | collective-permute-start | bytes 516104 | tf_op jit(solution)/shard_map/ppermute | solution.py:666
  28.1 7.8 %collective-permute-start.6 = (bf16[336,256]{1,0:T(8,128)(2,1)S(1)}, bf16[336,256]{1,0:T(8,128)(2,1)S(1)}, u32[]{:S(2)}, u32[]{:S(2)}) collective-permute-start(bf16[336,256]{1,0:T(8,128)(2,1)S(1)} %get-tuple-element.111.refs_5_), channel_id=1, source_target_pairs={{0,1},{1,0},{2,3},{3,2},{4,5},{5,4},{6,7},{7,6},{8,9},{9,8},{10,11... | collective-permute-start | bytes 516104 | tf_op jit(solution)/shard_map/ppermute | solution.py:666
  46.7 4.2 %collective-permute-start.9 = (bf16[2,336,256]{2,1,0:T(8,128)(2,1)S(1)}, bf16[2,336,256]{2,1,0:T(8,128)(2,1)S(1)}, u32[]{:S(2)}, u32[]{:S(2)}) collective-permute-start(bf16[2,336,256]{2,1,0:T(8,128)(2,1)S(1)} %get-tuple-element.126), channel_id=1, source_target_pairs={{0,1},{1,0},{2,3},{3,2},{4,5},{5,4},{6,7},{7,6},{8,9},{9,8},{10,11... | collective-permute-start | bytes 1032200 | tf_op jit(solution)/shard_map/ppermute | solution.py:666
  50.9 6.6 %collective-permute-start.10 = (bf16[336,256]{1,0:T(8,128)(2,1)S(1)}, bf16[336,256]{1,0:T(8,128)(2,1)S(1)}, u32[]{:S(2)}, u32[]{:S(2)}) collective-permute-start(bf16[336,256]{1,0:T(8,128)(2,1)S(1)} %fusion.5), channel_id=1, source_target_pairs={{0,2},{1,3},{2,0},{3,1},{4,6},{5,7},{6,4},{7,5},{8,10},{9,11},{10,... | collective-permute-start | bytes 516104 | tf_op jit(solution)/shard_map/ppermute | solution.py:666
  57.5 1.6 %collective-permute-start.12 = (bf16[512,256]{1,0:T(8,128)(2,1)S(1)}, bf16[512,256]{1,0:T(8,128)(2,1)S(1)}, u32[]{:S(2)}, u32[]{:S(2)}) collective-permute-start(bf16[512,256]{1,0:T(8,128)(2,1)S(1)} %get-tuple-element.136), channel_id=1, source_target_pairs={{0,1},{1,0},{2,3},{3,2},{4,5},{5,4},{6,7},{7,6},{8,9},{9,8},{10,11... | collective-permute-start | bytes 786440 | tf_op jit(solution)/shard_map/ppermute | solution.py:666
  59.2 12.4 %collective-permute-start.13 = (bf16[512,256]{1,0:T(8,128)(2,1)S(1)}, bf16[512,256]{1,0:T(8,128)(2,1)S(1)}, u32[]{:S(2)}, u32[]{:S(2)}) collective-permute-start(bf16[512,256]{1,0:T(8,128)(2,1)S(1)} %add_convert_fusion.2), channel_id=1, source_target_pairs={{0,2},{1,3},{2,0},{3,1},{4,6},{5,7},{6,4},{7,5},{8,10},{9,11},{10,... | collective-permute-start | bytes 786440 | tf_op jit(solution)/shard_map/ppermute | solution.py:666
  60.9 10.7 %collective-permute-start.11 = (bf16[336,256]{1,0:T(8,128)(2,1)S(1)}, bf16[336,256]{1,0:T(8,128)(2,1)S(1)}, u32[]{:S(2)}, u32[]{:S(2)}) collective-permute-start(bf16[336,256]{1,0:T(8,128)(2,1)S(1)} %fusion), channel_id=1, source_target_pairs={{0,16},{1,17},{2,18},{3,19},{4,20},{5,21},{6,22},{7,23},{8,24},{9,... | collective-permute-start | bytes 516104 | tf_op jit(solution)/shard_map/ppermute | solution.py:733
  74.1 8.4 %collective-permute-start.15 = (bf16[512,256]{1,0:T(8,128)(2,1)S(1)}, bf16[512,256]{1,0:T(8,128)(2,1)S(1)}, u32[]{:S(2)}, u32[]{:S(2)}) collective-permute-start(bf16[512,256]{1,0:T(8,128)(2,1)S(1)} %add_convert_fusion.1), channel_id=1, source_target_pairs={{0,2},{1,3},{2,0},{3,1},{4,6},{5,7},{6,4},{7,5},{8,10},{9,11},{10,... | collective-permute-start | bytes 786440 | tf_op jit(solution)/shard_map/ppermute | solution.py:666
  84.6 5.1 %collective-permute-start.20 = (bf16[208,256]{1,0:T(8,128)(2,1)S(1)}, bf16[208,256]{1,0:T(8,128)(2,1)S(1)}, u32[]{:S(2)}, u32[]{:S(2)}) collective-permute-start(bf16[208,256]{1,0:T(8,128)(2,1)S(1)} %fusion.7), channel_id=1, source_target_pairs={{0,2},{1,3},{2,0},{3,1},{4,6},{5,7},{6,4},{7,5},{8,10},{9,11},{10,... | collective-permute-start | bytes 319496 | tf_op jit(solution)/shard_map/ppermute | solution.py:666
  86.3 6.2 %collective-permute-start.25 = (bf16[336,256]{1,0:T(8,128)(2,1)S(1)}, bf16[336,256]{1,0:T(8,128)(2,1)S(1)}, u32[]{:S(2)}, u32[]{:S(2)}) collective-permute-start(bf16[336,256]{1,0:T(8,128)(2,1)S(1)} %add_convert_fusion.4), channel_id=1, source_target_pairs={{0,8},{1,9},{2,10},{3,11},{4,12},{5,13},{6,14},{7,15},{8,0},{9,1},... | collective-permute-start | bytes 516104 | tf_op jit(solution)/shard_map/ppermute | solution.py:733
  87.7 15.1 %collective-permute-start.17 = (bf16[512,256]{1,0:T(8,128)(2,1)S(1)}, bf16[512,256]{1,0:T(8,128)(2,1)S(1)}, u32[]{:S(2)}, u32[]{:S(2)}) collective-permute-start(bf16[512,256]{1,0:T(8,128)(2,1)S(1)} %get-tuple-element.161), channel_id=1, source_target_pairs={{0,1},{1,0},{2,3},{3,2},{4,5},{5,4},{6,7},{7,6},{8,9},{9,8},{10,11... | collective-permute-start | bytes 786440 | tf_op jit(solution)/shard_map/ppermute | solution.py:666
  88.6 7.8 %collective-permute-start.19 = (bf16[2,512,256]{2,1,0:T(8,128)(2,1)S(1)}, bf16[2,512,256]{2,1,0:T(8,128)(2,1)S(1)}, u32[]{:S(2)}, u32[]{:S(2)}) collective-permute-start(bf16[2,512,256]{2,1,0:T(8,128)(2,1)S(1)} %get-tuple-element.165), channel_id=1, source_target_pairs={{0,1},{1,0},{2,3},{3,2},{4,5},{5,4},{6,7},{7,6},{8,9},{9,8},{10,11... | collective-permute-start | bytes 1572872 | tf_op jit(solution)/shard_map/ppermute | solution.py:666
  89.8 5.1 %collective-permute-start.22 = (bf16[208,256]{1,0:T(8,128)(2,1)S(1)}, bf16[208,256]{1,0:T(8,128)(2,1)S(1)}, u32[]{:S(2)}, u32[]{:S(2)}) collective-permute-start(bf16[208,256]{1,0:T(8,128)(2,1)S(1)} %fusion.3), channel_id=1, source_target_pairs={{0,4},{1,5},{2,6},{3,7},{4,0},{5,1},{6,2},{7,3},{8,12},{9,13},{10,... | collective-permute-start | bytes 319496 | tf_op jit(solution)/shard_map/ppermute | solution.py:733
  92.6 9.5 %collective-permute-start.26 = (bf16[336,256]{1,0:T(8,128)(2,1)S(1)}, bf16[336,256]{1,0:T(8,128)(2,1)S(1)}, u32[]{:S(2)}, u32[]{:S(2)}) collective-permute-start(bf16[336,256]{1,0:T(8,128)(2,1)S(1)} %add_convert_fusion.3.a), channel_id=1, source_target_pairs={{0,4},{1,5},{2,6},{3,7},{4,0},{5,1},{6,2},{7,3},{8,12},{9,13},{10,... | collective-permute-start | bytes 516104 | tf_op jit(solution)/shard_map/ppermute | solution.py:733
  94.1 8.7 %collective-permute-start.18 = (bf16[512,256]{1,0:T(8,128)(2,1)S(1)}, bf16[512,256]{1,0:T(8,128)(2,1)S(1)}, u32[]{:S(2)}, u32[]{:S(2)}) collective-permute-start(bf16[512,256]{1,0:T(8,128)(2,1)S(1)} %get-tuple-element.163), channel_id=1, source_target_pairs={{0,1},{1,0},{2,3},{3,2},{4,5},{5,4},{6,7},{7,6},{8,9},{9,8},{10,11... | collective-permute-start | bytes 786440 | tf_op jit(solution)/shard_map/ppermute | solution.py:666
  94.9 4.8 %collective-permute-start.23 = (bf16[208,256]{1,0:T(8,128)(2,1)S(1)}, bf16[208,256]{1,0:T(8,128)(2,1)S(1)}, u32[]{:S(2)}, u32[]{:S(2)}) collective-permute-start(bf16[208,256]{1,0:T(8,128)(2,1)S(1)} %add_convert_fusion.8), channel_id=1, source_target_pairs={{0,8},{1,9},{2,10},{3,11},{4,12},{5,13},{6,14},{7,15},{8,0},{9,1},... | collective-permute-start | bytes 319496 | tf_op jit(solution)/shard_map/ppermute | solution.py:733
  96.5 7.7 %collective-permute-start.21 = (bf16[512,256]{1,0:T(8,128)(2,1)S(1)}, bf16[512,256]{1,0:T(8,128)(2,1)S(1)}, u32[]{:S(2)}, u32[]{:S(2)}) collective-permute-start(bf16[512,256]{1,0:T(8,128)(2,1)S(1)} %add_convert_fusion), channel_id=1, source_target_pairs={{0,2},{1,3},{2,0},{3,1},{4,6},{5,7},{6,4},{7,5},{8,10},{9,11},{10,... | collective-permute-start | bytes 786440 | tf_op jit(solution)/shard_map/ppermute | solution.py:666
  99.7 6.8 %collective-permute-start.24 = (bf16[208,256]{1,0:T(8,128)(2,1)S(1)}, bf16[208,256]{1,0:T(8,128)(2,1)S(1)}, u32[]{:S(2)}, u32[]{:S(2)}) collective-permute-start(bf16[208,256]{1,0:T(8,128)(2,1)S(1)} %add_convert_fusion.7.a), channel_id=1, source_target_pairs={{0,16},{1,17},{2,18},{3,19},{4,20},{5,21},{6,22},{7,23},{8,24},{9,... | collective-permute-start | bytes 319496 | tf_op jit(solution)/shard_map/ppermute | solution.py:733
  (14 other events, 182.9 us)

commit v5 on v4

--- a/solution.py
+++ b/solution.py
@@ -153,8 +153,9 @@
         top = jnp.broadcast_to(top, (scores.shape[0], 2 * hd))
         if before is None:
             return scores, top, None
-        steps = jnp.maximum(jnp.ceil((top - before[i]) * LOG2_E), 0.0)
-        return scores, before[i] + steps * LN_2, jnp.exp2(-steps)
+        old = before(i)
+        steps = jnp.maximum(jnp.ceil((top - old) * LOG2_E), 0.0)
+        return scores, old + steps * LN_2, jnp.exp2(-steps)
 
     later = score(0)
     for i in range(len(queries)):
@@ -269,10 +270,10 @@
 
         queries = [qs[h // 2][r, h % 2] for h in range(heads)]
         at = 3 * hd // 2
-        before = [
-            jnp.broadcast_to(os[h // 2][r, h % 2, :, at : at + 1], (here, 2 * hd))
-            for h in range(heads)
-        ]
+
+        def before(h):
+            return jnp.broadcast_to(os[h // 2][r, h % 2, :, at : at + 1], (here, 2 * hd))
+
         attend(queries, [kv_out[n, h] for h in range(heads)], [feats[n]] * heads, before, put)
         return 0
 

time: 108 us -> 108 us (level)
  no operation moved by 1% of the time
where the time goes in v5:
time: 108 us; the launch traced here: 107 us
  Pallas kernels  63.1 us (58%)
  starting transfers between devices  27.6 us (26%)
  waiting for transfers between devices  15 us (14%)
    pallas_call x19, Pallas kernels, call(): pl.pallas_call(kernel, out_shape=[jax.ShapeDtypeStruct(shape, kind) for s...  63.1 us
    ppermute x21, starting transfers between devices, swap(): return lax.ppermute(value, axis, [(i, i ^ bit) for i in range(size)])  16.6 us
    ppermute x21, waiting for transfers between devices, swap(): return lax.ppermute(value, axis, [(i, i ^ bit) for i in range(size)])  11.1 us
    ppermute x6, starting transfers between devices, over_dp(): got = lax.ppermute(sent, ('dp', 'mp'), pairs)  11 us
    ppermute x6, waiting for transfers between devices, over_dp(): got = lax.ppermute(sent, ('dp', 'mp'), pairs)  3.9 us
  transfers between devices with their start and end apart: 27, of which 15 were waited for; matrix products, arithmetic and copies ran while one was open for 0% of the time, Pallas kernels for 46%

profile of v5, /device:TPU:0, one launch (start us, length us, event | category | flops | bytes accessed | tf_op | source)
XLA Modules:
  0.0 107.2 jit_solution(15527725638520986210)
XLA Ops:
  0.6 1.5 %pack.1 = (bf16[736,256]{1,0:T(8,128)(2,1)S(1)}, bf16[1056,256]{1,0:T(8,128)(2,1)S(1)}, bf16[336,256]{1,0:T(8,128)(2,1)S(1)}, f32[8,256]{1,0:T(8,128)S(1)}) custom-call(bf16[3,64,256]{2,1,0:T(8,128)(2,1)} %bitcast.37, bf16[2,64]{1,0:T(2,128)(2,1)} %refs_1_.1, bf16[64,256]{1,0:T(8,128)(2,1)} %refs_2_.1, bf16[256]{0:T(256)(128)(2,1)} %refs_3_.1, ...), custom_call_target="tpu_custom_call" | custom-call | tf_op jit(solution)/shard_map/pack/pallas_call | solution.py:35
  2.7 2.9 %collective-permute-start.2 = (bf16[736,256]{1,0:T(8,128)(2,1)S(1)}, bf16[736,256]{1,0:T(8,128)(2,1)S(1)}, u32[]{:S(2)}, u32[]{:S(2)}) collective-permute-start(bf16[736,256]{1,0:T(8,128)(2,1)S(1)} %get-tuple-element.138.refs_0_.refs_4_.refs_6_.refs_2_.refs_9_.refs_3_), channel_id=1, source_target_pairs={{0,2},{1,3},{2,0},{3,1},{4,6},{5,7},{6,4},{7,5},{8,10},{9,11},{10,... | collective-permute-start | bytes 1130504 | tf_op jit(solution)/shard_map/ppermute | solution.py:667
  5.6 2.0 %collective-permute-start.4 = (bf16[1056,256]{1,0:T(8,128)(2,1)S(1)}, bf16[1056,256]{1,0:T(8,128)(2,1)S(1)}, u32[]{:S(2)}, u32[]{:S(2)}) collective-permute-start(bf16[1056,256]{1,0:T(8,128)(2,1)S(1)} %get-tuple-element.157.refs_1_.refs_3_), channel_id=1, source_target_pairs={{0,2},{1,3},{2,0},{3,1},{4,6},{5,7},{6,4},{7,5},{8,10},{9,11},{10,... | collective-permute-start | bytes 1622024 | tf_op jit(solution)/shard_map/ppermute | solution.py:667
  7.6 4.8 %attend_local.2 = (bf16[3,2,512,1024]{3,2,1,0:T(8,128)(2,1)S(1)}, bf16[3,2,128,1024]{3,2,1,0:T(8,128)(2,1)S(1)}, bf16[3,2,64,512]{3,2,1,0:T(8,128)(2,1)S(1)}, bf...) custom-call(bf16[736,256]{1,0:T(8,128)(2,1)S(1)} %get-tuple-element.138.refs_0_.refs_4_.refs_6_.refs_2_.refs_9_.refs_3_, ...), custom_call_target="tpu_custom_call" | custom-call | tf_op jit(solution)/shard_map/attend_local/pallas_call | solution.py:35
  12.4 2.8 %collective-permute-done.2.refs_4_.refs_8_.refs_11_.refs_6_.refs_5_ = bf16[736,256]{1,0:T(8,128)(2,1)S(1)} collective-permute-done((bf16[736,256]{1,0:T(8,128)(2,1)S(1)}, bf16[736,256]{1,0:T(8,128)(2,1)S(1)}, u32[]{:S(2)}, u32[]{:S(2)}) %collective-permute-start.2) | collective-permute-done | bytes 376864 | tf_op jit(solution)/shard_map/ppermute | solution.py:667
  15.2 1.7 %collective-permute-done.3.refs_5_.refs_9_.refs_12_.refs_7_.refs_6_ = bf16[736,256]{1,0:T(8,128)(2,1)S(1)} collective-permute-done((bf16[736,256]{1,0:T(8,128)(2,1)S(1)}, bf16[736,256]{1,0:T(8,128)(2,1)S(1)}, u32[]{:S(2)}, u32[]{:S(2)}) %collective-permute-start.3) | collective-permute-done | bytes 376864 | tf_op jit(solution)/shard_map/ppermute | solution.py:667
  16.9 4.8 %attend_local.3 = (bf16[3,2,512,1024]{3,2,1,0:T(8,128)(2,1)S(1)}, bf16[3,2,128,1024]{3,2,1,0:T(8,128)(2,1)S(1)}, bf16[3,2,64,512]{3,2,1,0:T(8,128)(2,1)S(1)}, bf...) custom-call(bf16[736,256]{1,0:T(8,128)(2,1)S(1)} %get-tuple-element.138.refs_0_.refs_4_.refs_6_.refs_2_.refs_9_.refs_3_, ...), custom_call_target="tpu_custom_call" | custom-call | tf_op jit(solution)/shard_map/attend_local/pallas_call | solution.py:35
  21.6 3.6 %attend_remote.2 = (bf16[1,4,512,1024]{3,2,1,0:T(8,128)(2,1)S(1)}, bf16[1,4,128,1024]{3,2,1,0:T(8,128)(2,1)S(1)}, f32[1,4,512,128]{3,2,1,0:T(8,128)S(1)}, bf16[1,4,512,128]{3,2,1,0:T(8,128)(2,1)S(1)}) custom-call(bf16[3,2,512,128]{3,2,1,0:T(8,128)(2,1)S(1)} %get-tuple-element.100.refs_0_, bf16[3,2,512,128]{3,2,1,0:T(8,128)(2,1)S(1)} %get-tuple-element.103.refs_1_, ...), custom_call_target="tpu_custom_call" | custom-call | tf_op jit(solution)/shard_map/attend_remote/pallas_call | solution.py:35
  26.3 1.8 %collective-permute-start.7 = (bf16[336,256]{1,0:T(8,128)(2,1)S(1)}, bf16[336,256]{1,0:T(8,128)(2,1)S(1)}, u32[]{:S(2)}, u32[]{:S(2)}) collective-permute-start(bf16[336,256]{1,0:T(8,128)(2,1)S(1)} %get-tuple-element.111.refs_5_), channel_id=1, source_target_pairs={{0,2},{1,3},{2,0},{3,1},{4,6},{5,7},{6,4},{7,5},{8,10},{9,11},{10,... | collective-permute-start | bytes 516104 | tf_op jit(solution)/shard_map/ppermute | solution.py:667
  28.3 7.2 %attend_remote.3 = (bf16[2,4,512,1024]{3,2,1,0:T(8,128)(2,1)S(1)}, bf16[2,4,128,1024]{3,2,1,0:T(8,128)(2,1)S(1)}, f32[2,4,512,128]{3,2,1,0:T(8,128)S(1)}, bf16[2,4,512,128]{3,2,1,0:T(8,128)(2,1)S(1)}) custom-call(bf16[3,2,512,128]{3,2,1,0:T(8,128)(2,1)S(1)} %get-tuple-element.100.refs_0_, bf16[3,2,512,128]{3,2,1,0:T(8,128)(2,1)S(1)} %get-tuple-element.103.refs_1_, ...), custom_call_target="tpu_custom_call" | custom-call | tf_op jit(solution)/shard_map/attend_remote/pallas_call | solution.py:35
  37.0 9.7 %middle.1 = (bf16[3,512,256]{2,1,0:T(8,128)(2,1)}, f32[2,336,256]{2,1,0:T(8,128)S(1)}, bf16[2,336,256]{2,1,0:T(8,128)(2,1)S(1)}, f32[3,512,256]{2,1,0:T(8,128)S(1)}, bf16[3,4,512,128]{3,2,1,0:T(8,128)(2,1)S(1)}) custom-call(f32[1,4,512,128]{3,2,1,0:T(8,128)S(1)} %get-tuple-element.106.refs_0_, f32[2,4,512,128]{3,2,1,0:T(8,128)S(1)} %get-tuple-element.109.refs_1_, ...), custom_call_target="tpu_custom_call" | custom-call | flops 181193936 | tf_op jit(solution)/shard_map/middle/pallas_call | solution.py:35
  47.0 3.9 %backward.10 = (bf16[2,128,2048]{2,1,0:T(8,128)(2,1)S(1)}, bf16[2,64,512]{2,1,0:T(8,128)(2,1)S(1)}) custom-call(bf16[3,4,512,128]{3,2,1,0:T(8,128)(2,1)S(1)} %get-tuple-element.116.refs_0_.refs_2_, bf16[3,2,512,1024]{3,2,1,0:T(8,128)(2,1)S(1)} %get-tuple-element.117.refs_1_, bf16[1,4,512,1024]{3,2,1,0:T(8,128)(2,1)S(1)} %get-tuple-element.128.refs_2_.refs_5_, ...), custom_call_target="tpu_custom_call" | custom-call | tf_op jit(solution)/shard_map/backward/pallas_call | solution.py:35
  50.9 1.5 %collective-permute-start.10 = (bf16[336,256]{1,0:T(8,128)(2,1)S(1)}, bf16[336,256]{1,0:T(8,128)(2,1)S(1)}, u32[]{:S(2)}, u32[]{:S(2)}) collective-permute-start(bf16[336,256]{1,0:T(8,128)(2,1)S(1)} %fusion.5), channel_id=1, source_target_pairs={{0,2},{1,3},{2,0},{3,1},{4,6},{5,7},{6,4},{7,5},{8,10},{9,11},{10,... | collective-permute-start | bytes 516104 | tf_op jit(solution)/shard_map/ppermute | solution.py:667
  52.4 4.7 %backward.11 = (bf16[2,128,2048]{2,1,0:T(8,128)(2,1)S(1)}, bf16[2,64,512]{2,1,0:T(8,128)(2,1)S(1)}, f32[512,256]{1,0:T(8,128)S(1)}, f32[512,256]{1,0:T(8,128)S(1...) custom-call(f32[3,512,256]{2,1,0:T(8,128)S(1)} %get-tuple-element.158.refs_0_, ...), custom_call_target="tpu_custom_call" | custom-call | tf_op jit(solution)/shard_map/backward/pallas_call | solution.py:35
  59.2 1.7 %collective-permute-start.13 = (bf16[512,256]{1,0:T(8,128)(2,1)S(1)}, bf16[512,256]{1,0:T(8,128)(2,1)S(1)}, u32[]{:S(2)}, u32[]{:S(2)}) collective-permute-start(bf16[512,256]{1,0:T(8,128)(2,1)S(1)} %add_convert_fusion.2), channel_id=1, source_target_pairs={{0,2},{1,3},{2,0},{3,1},{4,6},{5,7},{6,4},{7,5},{8,10},{9,11},{10,... | collective-permute-start | bytes 786440 | tf_op jit(solution)/shard_map/ppermute | solution.py:667
  60.9 2.6 %collective-permute-start.11 = (bf16[336,256]{1,0:T(8,128)(2,1)S(1)}, bf16[336,256]{1,0:T(8,128)(2,1)S(1)}, u32[]{:S(2)}, u32[]{:S(2)}) collective-permute-start(bf16[336,256]{1,0:T(8,128)(2,1)S(1)} %fusion), channel_id=1, source_target_pairs={{0,16},{1,17},{2,18},{3,19},{4,20},{5,21},{6,22},{7,23},{8,24},{9,... | collective-permute-start | bytes 516104 | tf_op jit(solution)/shard_map/ppermute | solution.py:734
  63.5 7.9 %backward.13 = (bf16[4,128,2048]{2,1,0:T(8,128)(2,1)S(1)}, bf16[4,64,512]{2,1,0:T(8,128)(2,1)S(1)}) custom-call(bf16[3,4,512,128]{3,2,1,0:T(8,128)(2,1)S(1)} %get-tuple-element.116.refs_0_.refs_2_, bf16[3,2,512,1024]{3,2,1,0:T(8,128)(2,1)S(1)} %get-tuple-element.117.refs_1_, bf16[3,2,512,1024]{3,2,1,0:T(8,128)(2,1)S(1)} %get-tuple-element.124.refs_4_.refs_2_, ...), custom_call_target="tpu_custom_call" | custom-call | tf_op jit(solution)/shard_map/backward/pallas_call | solution.py:35
  74.7 7.9 %backward.16 = (bf16[4,128,2048]{2,1,0:T(8,128)(2,1)S(1)}, bf16[4,64,512]{2,1,0:T(8,128)(2,1)S(1)}) custom-call(bf16[3,4,512,128]{3,2,1,0:T(8,128)(2,1)S(1)} %get-tuple-element.116.refs_0_.refs_2_, bf16[3,2,512,1024]{3,2,1,0:T(8,128)(2,1)S(1)} %get-tuple-element.117.refs_1_, bf16[3,2,512,1024]{3,2,1,0:T(8,128)(2,1)S(1)} %get-tuple-element.124.refs_4_.refs_2_, ...), custom_call_target="tpu_custom_call" | custom-call | tf_op jit(solution)/shard_map/backward/pallas_call | solution.py:35
  84.6 1.6 %collective-permute-start.20 = (bf16[208,256]{1,0:T(8,128)(2,1)S(1)}, bf16[208,256]{1,0:T(8,128)(2,1)S(1)}, u32[]{:S(2)}, u32[]{:S(2)}) collective-permute-start(bf16[208,256]{1,0:T(8,128)(2,1)S(1)} %fusion.7), channel_id=1, source_target_pairs={{0,2},{1,3},{2,0},{3,1},{4,6},{5,7},{6,4},{7,5},{8,10},{9,11},{10,... | collective-permute-start | bytes 319496 | tf_op jit(solution)/shard_map/ppermute | solution.py:667
  89.8 1.6 %collective-permute-start.22 = (bf16[208,256]{1,0:T(8,128)(2,1)S(1)}, bf16[208,256]{1,0:T(8,128)(2,1)S(1)}, u32[]{:S(2)}, u32[]{:S(2)}) collective-permute-start(bf16[208,256]{1,0:T(8,128)(2,1)S(1)} %fusion.3), channel_id=1, source_target_pairs={{0,4},{1,5},{2,6},{3,7},{4,0},{5,1},{6,2},{7,3},{8,12},{9,13},{10,... | collective-permute-start | bytes 319496 | tf_op jit(solution)/shard_map/ppermute | solution.py:734
  92.6 1.6 %collective-permute-start.26 = (bf16[336,256]{1,0:T(8,128)(2,1)S(1)}, bf16[336,256]{1,0:T(8,128)(2,1)S(1)}, u32[]{:S(2)}, u32[]{:S(2)}) collective-permute-start(bf16[336,256]{1,0:T(8,128)(2,1)S(1)} %add_convert_fusion.3.a), channel_id=1, source_target_pairs={{0,4},{1,5},{2,6},{3,7},{4,0},{5,1},{6,2},{7,3},{8,12},{9,13},{10,... | collective-permute-start | bytes 516104 | tf_op jit(solution)/shard_map/ppermute | solution.py:734
  94.9 1.5 %collective-permute-start.23 = (bf16[208,256]{1,0:T(8,128)(2,1)S(1)}, bf16[208,256]{1,0:T(8,128)(2,1)S(1)}, u32[]{:S(2)}, u32[]{:S(2)}) collective-permute-start(bf16[208,256]{1,0:T(8,128)(2,1)S(1)} %add_convert_fusion.8), channel_id=1, source_target_pairs={{0,8},{1,9},{2,10},{3,11},{4,12},{5,13},{6,14},{7,15},{8,0},{9,1},... | collective-permute-start | bytes 319496 | tf_op jit(solution)/shard_map/ppermute | solution.py:734
  96.5 2.3 %collective-permute-start.21 = (bf16[512,256]{1,0:T(8,128)(2,1)S(1)}, bf16[512,256]{1,0:T(8,128)(2,1)S(1)}, u32[]{:S(2)}, u32[]{:S(2)}) collective-permute-start(bf16[512,256]{1,0:T(8,128)(2,1)S(1)} %add_convert_fusion), channel_id=1, source_target_pairs={{0,2},{1,3},{2,0},{3,1},{4,6},{5,7},{6,4},{7,5},{8,10},{9,11},{10,... | collective-permute-start | bytes 786440 | tf_op jit(solution)/shard_map/ppermute | solution.py:667
  99.7 2.3 %collective-permute-start.24 = (bf16[208,256]{1,0:T(8,128)(2,1)S(1)}, bf16[208,256]{1,0:T(8,128)(2,1)S(1)}, u32[]{:S(2)}, u32[]{:S(2)}) collective-permute-start(bf16[208,256]{1,0:T(8,128)(2,1)S(1)} %add_convert_fusion.7.a), channel_id=1, source_target_pairs={{0,16},{1,17},{2,18},{3,19},{4,20},{5,21},{6,22},{7,23},{8,24},{9,... | collective-permute-start | bytes 319496 | tf_op jit(solution)/shard_map/ppermute | solution.py:734
  (83 shorter events, 22.6 us)
Async XLA Ops:
  2.1 5.5 %collective-permute-start.1 = (bf16[1056,256]{1,0:T(8,128)(2,1)S(1)}, bf16[1056,256]{1,0:T(8,128)(2,1)S(1)}, u32[]{:S(2)}, u32[]{:S(2)}) collective-permute-start(bf16[1056,256]{1,0:T(8,128)(2,1)S(1)} %get-tuple-element.157.refs_1_.refs_3_), channel_id=1, source_target_pairs={{0,1},{1,0},{2,3},{3,2},{4,5},{5,4},{6,7},{7,6},{8,9},{9,8},{10,11... | collective-permute-start | bytes 1622024 | tf_op jit(solution)/shard_map/ppermute | solution.py:667
  2.6 3.0 %collective-permute-start = (bf16[736,256]{1,0:T(8,128)(2,1)S(1)}, bf16[736,256]{1,0:T(8,128)(2,1)S(1)}, u32[]{:S(2)}, u32[]{:S(2)}) collective-permute-start(bf16[736,256]{1,0:T(8,128)(2,1)S(1)} %get-tuple-element.138.refs_0_.refs_4_.refs_6_.refs_2_.refs_9_.refs_3_), channel_id=1, source_target_pairs={{0,1},{1,0},{2,3},{3,2},{4,5},{5,4},{6,7},{7,6},{8,9},{9,8},{10,11... | collective-permute-start | bytes 1130504 | tf_op jit(solution)/shard_map/ppermute | solution.py:667
  2.7 12.5 %collective-permute-start.2 = (bf16[736,256]{1,0:T(8,128)(2,1)S(1)}, bf16[736,256]{1,0:T(8,128)(2,1)S(1)}, u32[]{:S(2)}, u32[]{:S(2)}) collective-permute-start(bf16[736,256]{1,0:T(8,128)(2,1)S(1)} %get-tuple-element.138.refs_0_.refs_4_.refs_6_.refs_2_.refs_9_.refs_3_), channel_id=1, source_target_pairs={{0,2},{1,3},{2,0},{3,1},{4,6},{5,7},{6,4},{7,5},{8,10},{9,11},{10,... | collective-permute-start | bytes 1130504 | tf_op jit(solution)/shard_map/ppermute | solution.py:667
  5.6 20.6 %collective-permute-start.4 = (bf16[1056,256]{1,0:T(8,128)(2,1)S(1)}, bf16[1056,256]{1,0:T(8,128)(2,1)S(1)}, u32[]{:S(2)}, u32[]{:S(2)}) collective-permute-start(bf16[1056,256]{1,0:T(8,128)(2,1)S(1)} %get-tuple-element.157.refs_1_.refs_3_), channel_id=1, source_target_pairs={{0,2},{1,3},{2,0},{3,1},{4,6},{5,7},{6,4},{7,5},{8,10},{9,11},{10,... | collective-permute-start | bytes 1622024 | tf_op jit(solution)/shard_map/ppermute | solution.py:667
  15.2 1.7 %collective-permute-start.3 = (bf16[736,256]{1,0:T(8,128)(2,1)S(1)}, bf16[736,256]{1,0:T(8,128)(2,1)S(1)}, u32[]{:S(2)}, u32[]{:S(2)}) collective-permute-start(bf16[736,256]{1,0:T(8,128)(2,1)S(1)} %collective-permute-done.2.refs_4_.refs_8_.refs_11_.refs_6_.refs_5_), channel_id=1, source_target_pairs={{0,1},{1,0},{2,3},{3,2},{4,5},{5,4},{6,7},{7,6},{8,9},{9,8},{10,11... | collective-permute-start | bytes 1130504 | tf_op jit(solution)/shard_map/ppermute | solution.py:667
  26.2 2.1 %collective-permute-start.5 = (bf16[1056,256]{1,0:T(8,128)(2,1)S(1)}, bf16[1056,256]{1,0:T(8,128)(2,1)S(1)}, u32[]{:S(2)}, u32[]{:S(2)}) collective-permute-start(bf16[1056,256]{1,0:T(8,128)(2,1)S(1)} %collective-permute-done.4.refs_4_.refs_5_), channel_id=1, source_target_pairs={{0,1},{1,0},{2,3},{3,2},{4,5},{5,4},{6,7},{7,6},{8,9},{9,8},{10,11... | collective-permute-start | bytes 1622024 | tf_op jit(solution)/shard_map/ppermute | solution.py:667
  26.3 9.2 %collective-permute-start.7 = (bf16[336,256]{1,0:T(8,128)(2,1)S(1)}, bf16[336,256]{1,0:T(8,128)(2,1)S(1)}, u32[]{:S(2)}, u32[]{:S(2)}) collective-permute-start(bf16[336,256]{1,0:T(8,128)(2,1)S(1)} %get-tuple-element.111.refs_5_), channel_id=1, source_target_pairs={{0,2},{1,3},{2,0},{3,1},{4,6},{5,7},{6,4},{7,5},{8,10},{9,11},{10,... | collective-permute-start | bytes 516104 | tf_op jit(solution)/shard_map/ppermute | solution.py:667
  28.1 7.8 %collective-permute-start.6 = (bf16[336,256]{1,0:T(8,128)(2,1)S(1)}, bf16[336,256]{1,0:T(8,128)(2,1)S(1)}, u32[]{:S(2)}, u32[]{:S(2)}) collective-permute-start(bf16[336,256]{1,0:T(8,128)(2,1)S(1)} %get-tuple-element.111.refs_5_), channel_id=1, source_target_pairs={{0,1},{1,0},{2,3},{3,2},{4,5},{5,4},{6,7},{7,6},{8,9},{9,8},{10,11... | collective-permute-start | bytes 516104 | tf_op jit(solution)/shard_map/ppermute | solution.py:667
  46.7 4.2 %collective-permute-start.9 = (bf16[2,336,256]{2,1,0:T(8,128)(2,1)S(1)}, bf16[2,336,256]{2,1,0:T(8,128)(2,1)S(1)}, u32[]{:S(2)}, u32[]{:S(2)}) collective-permute-start(bf16[2,336,256]{2,1,0:T(8,128)(2,1)S(1)} %get-tuple-element.126), channel_id=1, source_target_pairs={{0,1},{1,0},{2,3},{3,2},{4,5},{5,4},{6,7},{7,6},{8,9},{9,8},{10,11... | collective-permute-start | bytes 1032200 | tf_op jit(solution)/shard_map/ppermute | solution.py:667
  50.9 6.6 %collective-permute-start.10 = (bf16[336,256]{1,0:T(8,128)(2,1)S(1)}, bf16[336,256]{1,0:T(8,128)(2,1)S(1)}, u32[]{:S(2)}, u32[]{:S(2)}) collective-permute-start(bf16[336,256]{1,0:T(8,128)(2,1)S(1)} %fusion.5), channel_id=1, source_target_pairs={{0,2},{1,3},{2,0},{3,1},{4,6},{5,7},{6,4},{7,5},{8,10},{9,11},{10,... | collective-permute-start | bytes 516104 | tf_op jit(solution)/shard_map/ppermute | solution.py:667
  57.5 1.6 %collective-permute-start.12 = (bf16[512,256]{1,0:T(8,128)(2,1)S(1)}, bf16[512,256]{1,0:T(8,128)(2,1)S(1)}, u32[]{:S(2)}, u32[]{:S(2)}) collective-permute-start(bf16[512,256]{1,0:T(8,128)(2,1)S(1)} %get-tuple-element.136), channel_id=1, source_target_pairs={{0,1},{1,0},{2,3},{3,2},{4,5},{5,4},{6,7},{7,6},{8,9},{9,8},{10,11... | collective-permute-start | bytes 786440 | tf_op jit(solution)/shard_map/ppermute | solution.py:667
  59.2 12.4 %collective-permute-start.13 = (bf16[512,256]{1,0:T(8,128)(2,1)S(1)}, bf16[512,256]{1,0:T(8,128)(2,1)S(1)}, u32[]{:S(2)}, u32[]{:S(2)}) collective-permute-start(bf16[512,256]{1,0:T(8,128)(2,1)S(1)} %add_convert_fusion.2), channel_id=1, source_target_pairs={{0,2},{1,3},{2,0},{3,1},{4,6},{5,7},{6,4},{7,5},{8,10},{9,11},{10,... | collective-permute-start | bytes 786440 | tf_op jit(solution)/shard_map/ppermute | solution.py:667
  60.9 10.7 %collective-permute-start.11 = (bf16[336,256]{1,0:T(8,128)(2,1)S(1)}, bf16[336,256]{1,0:T(8,128)(2,1)S(1)}, u32[]{:S(2)}, u32[]{:S(2)}) collective-permute-start(bf16[336,256]{1,0:T(8,128)(2,1)S(1)} %fusion), channel_id=1, source_target_pairs={{0,16},{1,17},{2,18},{3,19},{4,20},{5,21},{6,22},{7,23},{8,24},{9,... | collective-permute-start | bytes 516104 | tf_op jit(solution)/shard_map/ppermute | solution.py:734
  74.1 8.4 %collective-permute-start.15 = (bf16[512,256]{1,0:T(8,128)(2,1)S(1)}, bf16[512,256]{1,0:T(8,128)(2,1)S(1)}, u32[]{:S(2)}, u32[]{:S(2)}) collective-permute-start(bf16[512,256]{1,0:T(8,128)(2,1)S(1)} %add_convert_fusion.1), channel_id=1, source_target_pairs={{0,2},{1,3},{2,0},{3,1},{4,6},{5,7},{6,4},{7,5},{8,10},{9,11},{10,... | collective-permute-start | bytes 786440 | tf_op jit(solution)/shard_map/ppermute | solution.py:667
  84.6 5.1 %collective-permute-start.20 = (bf16[208,256]{1,0:T(8,128)(2,1)S(1)}, bf16[208,256]{1,0:T(8,128)(2,1)S(1)}, u32[]{:S(2)}, u32[]{:S(2)}) collective-permute-start(bf16[208,256]{1,0:T(8,128)(2,1)S(1)} %fusion.7), channel_id=1, source_target_pairs={{0,2},{1,3},{2,0},{3,1},{4,6},{5,7},{6,4},{7,5},{8,10},{9,11},{10,... | collective-permute-start | bytes 319496 | tf_op jit(solution)/shard_map/ppermute | solution.py:667
  86.3 6.2 %collective-permute-start.25 = (bf16[336,256]{1,0:T(8,128)(2,1)S(1)}, bf16[336,256]{1,0:T(8,128)(2,1)S(1)}, u32[]{:S(2)}, u32[]{:S(2)}) collective-permute-start(bf16[336,256]{1,0:T(8,128)(2,1)S(1)} %add_convert_fusion.4), channel_id=1, source_target_pairs={{0,8},{1,9},{2,10},{3,11},{4,12},{5,13},{6,14},{7,15},{8,0},{9,1},... | collective-permute-start | bytes 516104 | tf_op jit(solution)/shard_map/ppermute | solution.py:734
  87.7 15.1 %collective-permute-start.17 = (bf16[512,256]{1,0:T(8,128)(2,1)S(1)}, bf16[512,256]{1,0:T(8,128)(2,1)S(1)}, u32[]{:S(2)}, u32[]{:S(2)}) collective-permute-start(bf16[512,256]{1,0:T(8,128)(2,1)S(1)} %get-tuple-element.161), channel_id=1, source_target_pairs={{0,1},{1,0},{2,3},{3,2},{4,5},{5,4},{6,7},{7,6},{8,9},{9,8},{10,11... | collective-permute-start | bytes 786440 | tf_op jit(solution)/shard_map/ppermute | solution.py:667
  88.6 7.8 %collective-permute-start.19 = (bf16[2,512,256]{2,1,0:T(8,128)(2,1)S(1)}, bf16[2,512,256]{2,1,0:T(8,128)(2,1)S(1)}, u32[]{:S(2)}, u32[]{:S(2)}) collective-permute-start(bf16[2,512,256]{2,1,0:T(8,128)(2,1)S(1)} %get-tuple-element.165), channel_id=1, source_target_pairs={{0,1},{1,0},{2,3},{3,2},{4,5},{5,4},{6,7},{7,6},{8,9},{9,8},{10,11... | collective-permute-start | bytes 1572872 | tf_op jit(solution)/shard_map/ppermute | solution.py:667
  89.8 5.1 %collective-permute-start.22 = (bf16[208,256]{1,0:T(8,128)(2,1)S(1)}, bf16[208,256]{1,0:T(8,128)(2,1)S(1)}, u32[]{:S(2)}, u32[]{:S(2)}) collective-permute-start(bf16[208,256]{1,0:T(8,128)(2,1)S(1)} %fusion.3), channel_id=1, source_target_pairs={{0,4},{1,5},{2,6},{3,7},{4,0},{5,1},{6,2},{7,3},{8,12},{9,13},{10,... | collective-permute-start | bytes 319496 | tf_op jit(solution)/shard_map/ppermute | solution.py:734
  92.6 9.5 %collective-permute-start.26 = (bf16[336,256]{1,0:T(8,128)(2,1)S(1)}, bf16[336,256]{1,0:T(8,128)(2,1)S(1)}, u32[]{:S(2)}, u32[]{:S(2)}) collective-permute-start(bf16[336,256]{1,0:T(8,128)(2,1)S(1)} %add_convert_fusion.3.a), channel_id=1, source_target_pairs={{0,4},{1,5},{2,6},{3,7},{4,0},{5,1},{6,2},{7,3},{8,12},{9,13},{10,... | collective-permute-start | bytes 516104 | tf_op jit(solution)/shard_map/ppermute | solution.py:734
  94.1 8.7 %collective-permute-start.18 = (bf16[512,256]{1,0:T(8,128)(2,1)S(1)}, bf16[512,256]{1,0:T(8,128)(2,1)S(1)}, u32[]{:S(2)}, u32[]{:S(2)}) collective-permute-start(bf16[512,256]{1,0:T(8,128)(2,1)S(1)} %get-tuple-element.163), channel_id=1, source_target_pairs={{0,1},{1,0},{2,3},{3,2},{4,5},{5,4},{6,7},{7,6},{8,9},{9,8},{10,11... | collective-permute-start | bytes 786440 | tf_op jit(solution)/shard_map/ppermute | solution.py:667
  94.9 4.8 %collective-permute-start.23 = (bf16[208,256]{1,0:T(8,128)(2,1)S(1)}, bf16[208,256]{1,0:T(8,128)(2,1)S(1)}, u32[]{:S(2)}, u32[]{:S(2)}) collective-permute-start(bf16[208,256]{1,0:T(8,128)(2,1)S(1)} %add_convert_fusion.8), channel_id=1, source_target_pairs={{0,8},{1,9},{2,10},{3,11},{4,12},{5,13},{6,14},{7,15},{8,0},{9,1},... | collective-permute-start | bytes 319496 | tf_op jit(solution)/shard_map/ppermute | solution.py:734
  96.5 7.7 %collective-permute-start.21 = (bf16[512,256]{1,0:T(8,128)(2,1)S(1)}, bf16[512,256]{1,0:T(8,128)(2,1)S(1)}, u32[]{:S(2)}, u32[]{:S(2)}) collective-permute-start(bf16[512,256]{1,0:T(8,128)(2,1)S(1)} %add_convert_fusion), channel_id=1, source_target_pairs={{0,2},{1,3},{2,0},{3,1},{4,6},{5,7},{6,4},{7,5},{8,10},{9,11},{10,... | collective-permute-start | bytes 786440 | tf_op jit(solution)/shard_map/ppermute | solution.py:667
  99.7 6.8 %collective-permute-start.24 = (bf16[208,256]{1,0:T(8,128)(2,1)S(1)}, bf16[208,256]{1,0:T(8,128)(2,1)S(1)}, u32[]{:S(2)}, u32[]{:S(2)}) collective-permute-start(bf16[208,256]{1,0:T(8,128)(2,1)S(1)} %add_convert_fusion.7.a), channel_id=1, source_target_pairs={{0,16},{1,17},{2,18},{3,19},{4,20},{5,21},{6,22},{7,23},{8,24},{9,... | collective-permute-start | bytes 319496 | tf_op jit(solution)/shard_map/ppermute | solution.py:734
  (14 other events, 182.9 us)
